TPU v7x, 256 devices: a whole 4x4x8 slice. The times are simulated.
256 devices in a mesh: seq: 32 (over z, x), head: 8 (over y, core).
Axes of the slice: x: 4, y: 4, z: 8, core: 2. Of those that a mesh axis runs over, the one named last changes fastest.
Arguments:
- queries: bfloat16 [32768, 2048], P('seq', 'head'), may hold values from -108 to 108
- pool: bfloat16 [1024, 128, 896], P('seq', 'head'), may hold values from -6 to 6
- w_key: bfloat16 [896, 2048], P(None, 'head'), may hold values from -0.1875 to 0.1875
- w_value: bfloat16 [896, 2048], P(None, 'head'), may hold values from -0.1875 to 0.1875
- out_grad: bfloat16 [32768, 2048], P('seq', 'head'), may hold values from -1.5 to 1.5
- nb_source: int32 [512, 2], replicated, may hold values from 0 to 31, all different within a row; in each aligned block of 16 rows (0 to 15, 16 to 31, ...) at most 2 rows name the same one
- nb_slot: int32 [512, 2], replicated, may hold values from 0 to 31
- nb_count: int32 [512], replicated, may hold values from 1 to 2
Outputs:
- attended: bfloat16 [32768, 2048], P('seq', 'head')
- grad_queries: bfloat16 [32768, 2048], P('seq', 'head')
- grad_pool: float32 [1024, 128, 896], P('seq', 'head')
- grad_w_key: float32 [896, 2048], P(None, 'head')
- grad_w_value: float32 [896, 2048], P(None, 'head')
Inputs may be any that keep to these rules, and one draw needn't show every extreme that they name: `nb_source`: for the 16 stretches of one device (aligned blocks of stretches), no encoder device is named by more than 2 entries, and in some block one is named exactly 2 times; the 2 neighbours of a stretch come from different encoder devices.
All inputs are finite; a program needn't handle non-finite values.
Results may differ from a plain program's by a relative error of at most 0.018.
The roundings to bfloat16 on the way count: a program that leaves them out, or rounds other values in their place, can miss the bound.
Values may be sent and summed in bfloat16 or wider, within the bound.
No kernel may reach another device: no remote copies, remote signals or barrier semaphores. Data moves between devices by JAX's collectives and lax.ppermute only.
A program may use at most 128 MiB of HBM per device.

v0:
```python
import math

import jax
import jax.numpy as jnp
from jax import lax
from jax.sharding import PartitionSpec as P

DH = 128
STRETCH = 64
KNB = 2
CH_DEV = 16


def local(queries, pool, w_key, w_value, out_grad, nb_source, nb_slot, nb_count):
    f32 = jnp.float32
    seq_count = lax.axis_size("seq")
    seq_index = lax.axis_index("seq")
    requests = CH_DEV * KNB
    capacity = max(2, 2 * requests // seq_count)
    slot_span = seq_count * capacity
    source_table = nb_source.reshape(seq_count, requests)
    slot_table = nb_slot.reshape(seq_count, requests)
    order_ids = jnp.arange(requests)
    matches = source_table[:, :, None] == source_table[:, None, :]
    before = order_ids[None, :] < order_ids[:, None]
    ranks = jnp.sum(jnp.logical_and(matches, before[None, :, :]), axis=2)
    places = jnp.arange(capacity)
    chosen = jnp.logical_and(
        (source_table == seq_index)[:, :, None], ranks[:, :, None] == places[None, None, :]
    )
    picked_slot = jnp.sum(jnp.where(chosen, slot_table[:, :, None], 0), axis=1).reshape(slot_span)
    filled = jnp.any(chosen, axis=1).reshape(slot_span)
    outgoing = jnp.take(pool, picked_slot, axis=0)
    outgoing = jnp.where(filled[:, None, None], outgoing, jnp.zeros_like(outgoing))
    incoming = lax.all_to_all(outgoing, "seq", split_axis=0, concat_axis=0, tiled=True)
    own_sources = lax.dynamic_index_in_dim(source_table, seq_index, 0, keepdims=False)
    own_ranks = lax.dynamic_index_in_dim(ranks, seq_index, 0, keepdims=False)
    positions = own_sources * capacity + own_ranks
    enc_width = pool.shape[2]
    local_width = w_key.shape[1]
    head_count = local_width // DH
    both_weights = jnp.concatenate([w_key, w_value], axis=1)
    wanted = jnp.take(incoming, positions, axis=0)
    panel_piece = lax.all_gather(wanted, "head", axis=1, tiled=True)
    projected = jnp.einsum(
        "jre,ec->jrc", panel_piece, both_weights, preferred_element_type=f32
    ).astype(jnp.bfloat16)
    joined = jnp.concatenate([panel_piece, projected], axis=2)
    panels = joined[:, :, :enc_width]
    rows_full = joined.shape[1]
    keys = joined[:, :, enc_width : enc_width + local_width].reshape(
        CH_DEV, KNB, rows_full, head_count, DH
    )
    values = joined[:, :, enc_width + local_width :].reshape(CH_DEV, KNB, rows_full, head_count, DH)
    query_blocks = queries.reshape(CH_DEV, STRETCH, head_count, DH)
    grad_blocks = out_grad.reshape(CH_DEV, STRETCH, head_count, DH)
    used_counts = lax.dynamic_slice_in_dim(nb_count, seq_index * CH_DEV, CH_DEV)
    used_mask = (jnp.arange(KNB)[None, :] < used_counts[:, None])[:, None, None, :, None]
    factor = 1.0 / math.sqrt(DH)
    scores = (
        jnp.einsum("cqhd,ckrhd->chqkr", query_blocks, keys, preferred_element_type=f32) * factor
    )
    masked_scores = jnp.where(used_mask, scores, -jnp.inf)
    row_max = jnp.max(masked_scores, axis=(3, 4), keepdims=True)
    exp_scores = jnp.where(used_mask, jnp.exp(masked_scores - row_max), 0.0)
    soft_probs = exp_scores / jnp.sum(exp_scores, axis=(3, 4), keepdims=True)
    soft_weights = soft_probs.astype(jnp.bfloat16)
    attended = jnp.einsum(
        "chqkr,ckrhd->cqhd", soft_weights, values, preferred_element_type=f32
    ).astype(jnp.bfloat16)
    grad_probs = jnp.einsum("cqhd,ckrhd->chqkr", grad_blocks, values, preferred_element_type=f32)
    row_dot = jnp.sum(soft_probs * grad_probs, axis=(3, 4), keepdims=True)
    grad_scores = (soft_probs * (grad_probs - row_dot)).astype(jnp.bfloat16)
    grad_queries = (
        jnp.einsum("chqkr,ckrhd->cqhd", grad_scores, keys, preferred_element_type=f32) * factor
    ).astype(jnp.bfloat16)
    grad_keys = (
        jnp.einsum("chqkr,cqhd->ckrhd", grad_scores, query_blocks, preferred_element_type=f32)
        * factor
    ).astype(jnp.bfloat16)
    grad_values = jnp.einsum(
        "chqkr,cqhd->ckrhd", soft_weights, grad_blocks, preferred_element_type=f32
    ).astype(jnp.bfloat16)
    grad_keys = grad_keys.reshape(requests, rows_full, local_width)
    grad_values = grad_values.reshape(requests, rows_full, local_width)
    summed = lax.psum_scatter(
        (
            jnp.einsum("jrc,ec->rje", grad_keys, w_key, preferred_element_type=f32)
            + jnp.einsum("jrc,ec->rje", grad_values, w_value, preferred_element_type=f32)
        ).astype(jnp.bfloat16),
        "head",
        scatter_dimension=0,
        tiled=True,
    )
    spread = (positions[None, :] == jnp.arange(slot_span)[:, None]).astype(jnp.bfloat16)
    returning = jnp.einsum("qj,rje->rqe", spread, summed, preferred_element_type=f32).astype(
        jnp.bfloat16
    )
    arrived = lax.all_to_all(returning, "seq", split_axis=1, concat_axis=1, tiled=True)
    pool_count = pool.shape[0]
    collect = jnp.logical_and(
        picked_slot[None, :] == jnp.arange(pool_count)[:, None], filled[None, :]
    ).astype(jnp.bfloat16)
    grad_pool = jnp.einsum("pq,rqe->pre", collect, arrived, preferred_element_type=f32)
    key_partial = jnp.einsum("jre,jrc->ec", panels, grad_keys, preferred_element_type=f32)
    value_partial = jnp.einsum("jre,jrc->ec", panels, grad_values, preferred_element_type=f32)
    grad_w_key, grad_w_value = lax.psum((key_partial, value_partial), "seq")
    token_rows = queries.shape[0]
    return (
        attended.reshape(token_rows, local_width),
        grad_queries.reshape(token_rows, local_width),
        grad_pool,
        grad_w_key,
        grad_w_value,
    )


def solution(mesh):
    return jax.shard_map(
        local,
        mesh=mesh,
        in_specs=(
            P("seq", "head"),
            P("seq", "head", None),
            P(None, "head"),
            P(None, "head"),
            P("seq", "head"),
            P(),
            P(),
            P(),
        ),
        out_specs=(
            P("seq", "head"),
            P("seq", "head"),
            P("seq", "head", None),
            P(None, "head"),
            P(None, "head"),
        ),
        check_vma=False,
    )
```

profile of v0, /device:TPU:8, one launch (start us, length us, event | category | flops | bytes accessed | tf_op | source)
XLA Modules:
  0.0 401.9 jit_solution(6219765014610650186)
XLA Ops:
  7.2 0.9 copy.61
  8.1 0.1 reshape.166
  8.3 0.8 convert_reduce_fusion
  9.1 0.8 copy.63
  9.9 0.1 broadcast_in_dim.85
  10.9 0.1 copy-done.22
  11.0 0.8 gather_fusion
  11.9 1.6 select_select_fusion
  13.5 11.3 %all-to-all-start = ((bf16[64,16,896]{2,1,0:T(8,128)(2,1)}), bf16[64,16,896]{2,1,0:T(8,128)(2,1)S(1)}, u32[]{:S(2)}, u32[]{:S(2)}) async-start(bf16[64,16,896]{2,1,0:T(8,128)(2,1)} %select_select_fusion), calls=%async_computation | async-start | bytes 3670016 | tf_op jit(solution)/shard_map/all_to_all | solution.py:35
  24.9 0.5 copy-done.24
  25.4 44.0 %all-to-all-done = bf16[64,16,896]{2,1,0:T(8,128)(2,1)S(1)} async-done(((bf16[64,16,896]{2,1,0:T(8,128)(2,1)}), bf16[64,16,896]{2,1,0:T(8,128)(2,1)S(1)}, u32[]{:S(2)}, u32[]{:S(2)}) %all-to-all-start) | async-done | bytes 1835040 | tf_op jit(solution)/shard_map/all_to_all | solution.py:35
  69.4 0.7 gather_fusion.1
  70.2 1.1 broadcast_select_fusion
  71.6 0.8 dynamic_slice.12
  72.4 43.4 %all-gather.2.cloned.1.call-done = bf16[32,128,896]{2,1,0:T(8,128)(2,1)} async-done(((bf16[32,16,896]{2,1,0:T(8,128)(2,1)}), bf16[32,128,896]{2,1,0:T(8,128)(2,1)}) %all-gather.2.cloned.1.call-update) | async-done | bytes 7340048 | tf_op jit(solution)/shard_map/all_gather | solution.py:44
  115.9 7.9 %convolution_convert_fusion = bf16[32,128,512]{2,1,0:T(8,128)(2,1)S(1)} fusion(bf16[32,128,896]{2,1,0:T(8,128)(2,1)} %all-gather.2.cloned.1.call-done, bf16[896,256]{1,0:T(8,128)(2,1)S(1)} %copy-done.14, bf16[896,256]{1,0:T(8,128)(2,1)S(1)} %copy-done.12), kind=kOutput, calls=%fused_computation.5 | convolution fusion | flops 3762028544 | bytes 12451840 | tf_op jit(solution)/shard_map/jre,ec->jrc/dot_general | solution.py:45
  123.8 1.9 fusion.67
  125.7 4.0 reshape.170
  129.7 2.0 reshape.169
  131.7 2.5 bitcast_reduce_fusion
  134.3 1.0 fusion.18
  135.4 1.6 convert_bitcast_fusion
  137.0 1.7 fusion.1
  138.7 1.6 copy.78
  140.3 1.3 fusion.3
  141.7 0.8 fusion.16
  142.5 0.1 copy.75
  142.7 0.7 copy-done.13
  143.5 2.4 fusion.50
  145.9 7.1 %fusion = bf16[128,32,896]{2,0,1:T(8,128)(2,1)} fusion(f32[32,128,896]{2,1,0:T(8,128)S(1)} %fusion.50, bf16[32,128,256]{1,2,0:T(8,128)(2,1)} %bitcast.108, bf16[896,256]{1,0:T(8,128)(2,1)S(1)} %copy-done.15), kind=kOutput, calls=%fused_computation.3 | convolution fusion | flops 1886388224 | bytes 24576000 | tf_op jit(solution)/shard_map/jrc,ec->rje/dot_general | solution.py:89
  153.0 48.8 %reduce-scatter.2.cloned.1.call-done = bf16[16,32,896]{2,0,1:T(8,128)(2,1)} async-done(((bf16[128,32,896]{2,0,1:T(8,128)(2,1)}), bf16[16,32,896]{2,0,1:T(8,128)(2,1)}) %reduce-scatter.2.cloned.1.call-update) | async-done | bytes 917520 | tf_op jit(solution)/shard_map/reduce_scatter | solution.py:86
  201.8 1.9 convert_bitcast_fusion.1
  203.7 2.3 copy.81
  206.0 10.1 %all-to-all-start.1 = ((bf16[16,64,896]{2,0,1:T(8,128)(2,1)}), bf16[16,64,896]{2,0,1:T(8,128)(2,1)}, u32[]{:S(2)}, u32[]{:S(2)}) async-start(bf16[16,64,896]{2,0,1:T(8,128)(2,1)} %copy.81), calls=%async_computation.2 | async-start | bytes 3670016 | tf_op jit(solution)/shard_map/all_to_all | solution.py:99
  216.1 0.3 all-reduce.3.cloned.1.call-start
  216.4 6.8 %convolution_bitcast_fusion.1 = f32[896,256]{1,0:T(8,128)} fusion(bf16[32,128,896]{2,1,0:T(8,128)(2,1)} %all-gather.2.cloned.1.call-done, bf16[32,128,256]{1,2,0:T(8,128)(2,1)} %bitcast.111), kind=kOutput, calls=%fused_computation.36 | convolution fusion | flops 1879048192 | bytes 10354688 | tf_op jit(solution)/shard_map/jre,jrc->ec/dot_general | solution.py:105
  223.3 6.1 %convolution_bitcast_fusion = f32[896,256]{1,0:T(8,128)} fusion(bf16[32,128,896]{2,1,0:T(8,128)(2,1)} %all-gather.2.cloned.1.call-done, bf16[32,128,256]{1,2,0:T(8,128)(2,1)S(1)} %bitcast.109), kind=kOutput, calls=%fused_computation.35 | convolution fusion | flops 1879048192 | bytes 10354688 | tf_op jit(solution)/shard_map/jre,jrc->ec/dot_general | solution.py:106
  229.5 3.5 fusion.37
  232.9 0.5 copy.69
  233.5 0.5 fusion.34
  234.0 0.5 copy.73
  234.5 1.1 copy_bitcast_fusion
  235.7 33.4 %all-to-all-done.1 = bf16[16,64,896]{2,0,1:T(8,128)(2,1)} async-done(((bf16[16,64,896]{2,0,1:T(8,128)(2,1)}), bf16[16,64,896]{2,0,1:T(8,128)(2,1)}, u32[]{:S(2)}, u32[]{:S(2)}) %all-to-all-start.1) | async-done | bytes 1835040 | tf_op jit(solution)/shard_map/all_to_all | solution.py:99
  269.1 2.0 fusion.14
  271.1 2.3 copy.85
  273.4 118.8 %all-reduce.3.cloned.1.call-done = (f32[896,256]{1,0:T(8,128)}, f32[896,256]{1,0:T(8,128)}) async-done(((f32[896,256]{1,0:T(8,128)}, f32[896,256]{1,0:T(8,128)}), (f32[896,256]{1,0:T(8,128)}, f32[896,256]{1,0:T(8,128)})) %all-reduce.3.cloned.1.call-update) | async-done | bytes 1835024 | tf_op jit(solution)/shard_map/psum | solution.py:107
  392.2 2.2 copy.152
  394.4 0.9 copy.153
  (72 shorter events, 1.5 us)
Async XLA Ops:
  7.2 3.9 copy-start
  10.5 0.5 copy-start.22
  10.8 2.6 copy-start.20
  13.5 56.0 %all-to-all-start = ((bf16[64,16,896]{2,1,0:T(8,128)(2,1)}), bf16[64,16,896]{2,1,0:T(8,128)(2,1)S(1)}, u32[]{:S(2)}, u32[]{:S(2)}) async-start(bf16[64,16,896]{2,1,0:T(8,128)(2,1)} %select_select_fusion), calls=%async_computation | async-start | bytes 3670016 | tf_op jit(solution)/shard_map/all_to_all | solution.py:35
  24.8 91.1 %all-gather.2.cloned.1.call-start = ((), (), s32[]{:S(2)}) async-start(), calls=%async_computation.3 | async-start | bytes 8257536 | tf_op jit(solution)/shard_map/all_gather | solution.py:44
  24.9 0.5 copy-start.24
  25.4 45.9 %copy-start.10 = (bf16[1024,256]{1,0:T(8,128)(2,1)S(1)}, bf16[1024,256]{1,0:T(8,128)(2,1)}, u32[]{:S(2)}) copy-start(bf16[1024,256]{1,0:T(8,128)(2,1)} %param.8) | copy-start | bytes 1572868
  70.1 1.3 copy-start.11
  70.1 45.7 %copy-start.12 = (bf16[896,256]{1,0:T(8,128)(2,1)S(1)}, bf16[896,256]{1,0:T(8,128)(2,1)}, u32[]{:S(2)}) copy-start(bf16[896,256]{1,0:T(8,128)(2,1)} %param.10) | copy-start | bytes 1376260
  70.1 45.7 %copy-start.14 = (bf16[896,256]{1,0:T(8,128)(2,1)S(1)}, bf16[896,256]{1,0:T(8,128)(2,1)}, u32[]{:S(2)}) copy-start(bf16[896,256]{1,0:T(8,128)(2,1)} %param.11) | copy-start | bytes 1376260
  71.3 130.5 %reduce-scatter.2.cloned.1.call-start = ((), (), s32[]{:S(2)}) async-start(), calls=%async_computation.4 | async-start | bytes 8257536 | tf_op jit(solution)/shard_map/reduce_scatter | solution.py:86
  72.4 67.9 %copy-start.18 = (pred[16,2]{1,0:T(8,128)(4,1)}, pred[16,2]{1,0:T(8,128)(4,1)S(1)}, u32[]{:S(2)}) copy-start(pred[16,2]{1,0:T(8,128)(4,1)S(1)} %iota_compare_fusion.4) | copy-start | bytes 100
  134.3 6.0 %copy-start.4 = (f32[16,2,2,128,64]{3,4,2,1,0:T(8,128)}, f32[16,2,2,128,64]{3,4,2,1,0:T(8,128)S(1)}, u32[]{:S(2)}) copy-start(f32[16,2,2,128,64]{3,4,2,1,0:T(8,128)S(1)} %get-tuple-element.32) | copy-start | bytes 6291460
  135.3 5.0 %copy-start.16 = (f32[16,2,64]{2,1,0:T(2,128)}, f32[16,2,64]{2,1,0:T(2,128)S(1)}, u32[]{:S(2)}) copy-start(f32[16,2,64]{2,1,0:T(2,128)S(1)} %fusion.18) | copy-start | bytes 24580
  135.4 1.7 copy-start.8
  141.7 1.1 copy-start.5
  142.4 1.0 copy-start.13
  142.7 3.1 copy-start.3
  143.5 2.4 copy-start.15
  153.0 48.8 %copy-start.25 = (s32[1,32]{1,0:T(1,128)S(1)}, s32[1,32]{1,0:T(1,128)}, u32[]{:S(2)}) copy-start(s32[1,32]{1,0:T(1,128)} %copy-done.24) | copy-start | bytes 388
  206.0 63.1 %all-to-all-start.1 = ((bf16[16,64,896]{2,0,1:T(8,128)(2,1)}), bf16[16,64,896]{2,0,1:T(8,128)(2,1)}, u32[]{:S(2)}, u32[]{:S(2)}) async-start(bf16[16,64,896]{2,0,1:T(8,128)(2,1)} %copy.81), calls=%async_computation.2 | async-start | bytes 3670016 | tf_op jit(solution)/shard_map/all_to_all | solution.py:99
  216.1 7.1 %copy-start.2 = (bf16[16,2,128,2,128]{2,4,3,1,0:T(8,128)(2,1)S(1)}, bf16[16,2,128,2,128]{2,4,3,1,0:T(8,128)(2,1)}, u32[]{:S(2)}) copy-start(bf16[16,2,128,2,128]{2,4,3,1,0:T(8,128)(2,1)} %copy.78) | copy-start | bytes 6291460
  216.1 176.0 %all-reduce.3.cloned.1.call-start = ((), (), s32[]{:S(2)}) async-start(), calls=%async_computation.5 | async-start | bytes 3670016 | tf_op jit(solution)/shard_map/psum | solution.py:107
  223.2 6.2 %copy-start.17 = (f32[16,2,64]{2,1,0:T(2,128)S(1)}, f32[16,2,64]{2,1,0:T(2,128)}, u32[]{:S(2)}) copy-start(f32[16,2,64]{2,1,0:T(2,128)} %copy-done.16) | copy-start | bytes 24580
  223.2 6.2 %copy-start.19 = (pred[16,2]{1,0:T(8,128)(4,1)S(1)}, pred[16,2]{1,0:T(8,128)(4,1)}, u32[]{:S(2)}) copy-start(pred[16,2]{1,0:T(8,128)(4,1)} %copy-done.18) | copy-start | bytes 100
  229.4 4.1 %copy-start.6 = (bf16[16,2,64,2,128]{4,2,3,1,0:T(8,128)(2,1)S(1)}, bf16[16,2,64,2,128]{4,2,3,1,0:T(8,128)(2,1)}, u32[]{:S(2)}) copy-start(bf16[16,2,64,2,128]{4,2,3,1,0:T(8,128)(2,1)} %copy-done.5) | copy-start | bytes 3145732
  229.4 4.1 %copy-start.7 = (bf16[16,2,128,2,128]{4,3,2,1,0:T(2,128)(2,1)S(1)}, bf16[16,2,128,2,128]{4,3,2,1,0:T(2,128)(2,1)}, u32[]{:S(2)}) copy-start(bf16[16,2,128,2,128]{4,3,2,1,0:T(2,128)(2,1)} %reshape.170) | copy-start | bytes 6291460
  234.0 35.1 %copy-start.21 = (pred[64]{0:T(512)(128)(4,1)S(1)}, pred[64]{0:T(512)(128)(4,1)}, u32[]{:S(2)}) copy-start(pred[64]{0:T(512)(128)(4,1)} %copy-done.20) | copy-start | bytes 196
  234.0 35.1 %copy-start.23 = (s32[64]{0:T(128)S(1)}, s32[64]{0:T(128)}, u32[]{:S(2)}) copy-start(s32[64]{0:T(128)} %copy-done.22) | copy-start | bytes 772
  271.1 124.3 %copy-start.1 = (bf16[32,16,896]{2,1,0:T(8,128)(2,1)S(1)}, bf16[32,16,896]{2,1,0:T(8,128)(2,1)}, u32[]{:S(2)}) copy-start(bf16[32,16,896]{2,1,0:T(8,128)(2,1)} %param.9) | copy-start | bytes 2752516
  392.2 2.2 copy-start.9
Sparse Core Ops, SparseCore 0:
  71.4 44.4 all-gather.1
  153.1 48.5 reduce-scatter.1
  229.5 162.5 all-reduce.2
where the time goes:
time: 402 us
  waiting for transfers between devices  288 us (72%)
  matrix products  44.9 us (11%)
  local copies, waits for them, and re-layouts  26.3 us (7%)
  starting transfers between devices  21.8 us (5%)
  between operations  14.2 us (4%)
  other arithmetic  6.16 us (2%)
    psum x1, waiting for transfers between devices, local(): grad_w_key, grad_w_value = lax.psum((key_partial, value_partial), 'seq')  119 us
    reduce_scatter x1, waiting for transfers between devices, local(): lax.psum_scatter((jnp.einsum('jrc,ec->rje', grad_keys, w_key, preferred_e...  48.8 us
    all_to_all x1, waiting for transfers between devices, local(): lax.all_to_all(outgoing, 'seq', split_axis=0, concat_axis=0, tiled=True)  44 us
    all_gather x1, waiting for transfers between devices, local(): panel_piece = lax.all_gather(wanted, 'head', axis=1, tiled=True)  43.4 us
    all_to_all x1, waiting for transfers between devices, local(): lax.all_to_all(returning, 'seq', split_axis=1, concat_axis=1, tiled=True)  33.4 us
    all_to_all x1, starting transfers between devices, local(): lax.all_to_all(outgoing, 'seq', split_axis=0, concat_axis=0, tiled=True)  11.3 us
    all_to_all x1, starting transfers between devices, local(): lax.all_to_all(returning, 'seq', split_axis=1, concat_axis=1, tiled=True)  10.1 us
    unnamed x57, local copies, waits for them, and re-layouts  8.79 us
  transfers between devices with their start and end apart: 5, of which 5 were waited for; matrix products, arithmetic and copies ran while one was open for 6% of the time, Pallas kernels for 0%

commit v1 on v0

v1 whole, which is shorter than its diff:
```python
import functools
import math

import jax
import jax.numpy as jnp
from jax import lax
from jax.experimental import pallas as pl
from jax.experimental.pallas import tpu as pltpu
from jax.sharding import Mesh
from jax.sharding import PartitionSpec as P

DH = 128
STRETCH = 64
KNB = 2
CH_DEV = 16
ROWS = 16
PIECES = 8
SPAN = KNB * ROWS * PIECES
HALF = 8
GROUP = 4
F32 = jnp.float32
BF16 = jnp.bfloat16

UP = [(i, (i + 1) % 4) for i in range(4)]
DOWN = [((i + 1) % 4, i) for i in range(4)]
SWAP = [(0, 1), (1, 0)]


def dot(a, b, ca, cb):
    return lax.dot_general(a, b, (((ca,), (cb,)), ((), ())), preferred_element_type=F32)


def shift(size, k):
    return [(i, (i + k) % size) for i in range(size)]


def gather_pieces(own):
    half = own.shape[0] // 2
    below = lax.ppermute(own, "y", UP)
    above = lax.ppermute(own, "y", DOWN)
    far_low = lax.ppermute(below[:half], "y", UP)
    far_high = lax.ppermute(above[half:], "y", DOWN)
    mine = [own, above, below, far_low, far_high]
    return mine + [lax.ppermute(piece, "core", SWAP) for piece in mine]


def plus(*terms):
    total = terms[0].astype(F32)
    for term in terms[1:]:
        total = total + term.astype(F32)
    return total


def scatter_pieces(mine, other):
    swapped = lax.ppermute(other, "core", SWAP)
    half = mine.shape[1] // 2
    far = plus(mine[3], swapped[3]).astype(BF16)
    got_low = lax.ppermute(far[:half], "y", UP)
    got_high = lax.ppermute(far[half:], "y", DOWN)
    up_low = plus(mine[1, :half], swapped[1, :half], got_low).astype(BF16)
    up_high = plus(mine[1, half:], swapped[1, half:]).astype(BF16)
    down_low = plus(mine[2, :half], swapped[2, :half]).astype(BF16)
    down_high = plus(mine[2, half:], swapped[2, half:], got_high).astype(BF16)
    from_below = lax.ppermute(jnp.concatenate([up_low, up_high]), "y", UP)
    from_above = lax.ppermute(jnp.concatenate([down_low, down_high]), "y", DOWN)
    return plus(mine[0], swapped[0], from_below, from_above).astype(BF16)


def fill_rows(step, refs, rows_ref):
    half_steps = HALF // GROUP // 2
    for core in range(2):
        own, above, below, far_low, far_high = refs[core * 5 : core * 5 + 5]

        def put(place, ref):
            for c in range(GROUP):
                at = c * SPAN + (core * 4 + place) * KNB * ROWS
                rows_ref[at : at + KNB * ROWS, :] = ref[c * KNB : (c + 1) * KNB].reshape(
                    KNB * ROWS, ref.shape[2]
                )

        put(0, own)
        put(1, above)
        put(2, below)

        @pl.when(step < half_steps)
        def _():
            put(3, far_low)

        @pl.when(step >= half_steps)
        def _():
            put(3, far_high)


def attention_kernel(first, count_ref, *refs):
    pieces = refs[:10]
    key_weight_ref, value_weight_ref, query_ref, grad_ref = refs[10:14]
    if first:
        begun_ref, rest = None, refs[14:]
    else:
        begun_ref, rest = refs[14], refs[15:]
    attended_ref, grad_query_ref, mine_ref, other_ref, out_ref = rest[:5]
    rows_ref, kv_ref, both_ref = rest[5:8]
    total_ref = out_ref if first else rest[8]
    step = pl.program_id(0)
    local = key_weight_ref.shape[1]
    factor = 1.0 / math.sqrt(DH)
    key_cols, value_cols = slice(0, local), slice(local, 2 * local)
    fill_rows(step, pieces, rows_ref)
    head_of = lax.broadcasted_iota(jnp.int32, (STRETCH, local), 1) < DH
    neighbour = (lax.broadcasted_iota(jnp.int32, (SPAN, 1), 0) // ROWS) % KNB

    def spread_heads(x):
        zero = jnp.zeros_like(x)
        return jnp.concatenate([jnp.where(head_of, x, zero), jnp.where(head_of, zero, x)], axis=0)

    def join_heads(x):
        return jnp.where(head_of, x[:STRETCH], x[STRETCH:])

    stretches = [
        (slice(c * SPAN, (c + 1) * SPAN), slice(c * STRETCH, (c + 1) * STRETCH))
        for c in range(GROUP)
    ]
    for rows, _ in stretches:
        panel = rows_ref[rows, :]
        kv_ref[rows, key_cols] = dot(panel, key_weight_ref[...], 1, 0).astype(BF16)
        kv_ref[rows, value_cols] = dot(panel, value_weight_ref[...], 1, 0).astype(BF16)
    products = []
    for rows, tokens in stretches:
        query, grad = spread_heads(query_ref[tokens, :]), spread_heads(grad_ref[tokens, :])
        scores = dot(kv_ref[rows, key_cols], query, 1, 1) * factor
        dprobs = dot(kv_ref[rows, value_cols], grad, 1, 1)
        products.append((query, grad, scores, dprobs))
    softened = []
    for c in range(GROUP):
        _, _, scores, dprobs = products[c]
        scores = jnp.where(neighbour < count_ref[step * GROUP + c], scores, -jnp.inf)
        powers = jnp.exp(scores - jnp.max(scores, axis=0, keepdims=True))
        probs = powers * (1.0 / jnp.sum(powers, axis=0, keepdims=True))
        row_dot = jnp.sum(probs * dprobs, axis=0, keepdims=True)
        softened.append((probs.astype(BF16), (probs * (dprobs - row_dot)).astype(BF16)))
    for c, (rows, tokens) in enumerate(stretches):
        query, grad, _, _ = products[c]
        weights, dscores = softened[c]
        both_ref[rows, key_cols] = (dot(dscores, query, 1, 0) * factor).astype(BF16)
        both_ref[rows, value_cols] = dot(weights, grad, 1, 0).astype(BF16)
        attended_ref[tokens, :] = join_heads(dot(weights, kv_ref[rows, value_cols], 0, 0)).astype(
            BF16
        )
        grad_query_ref[tokens, :] = (
            join_heads(dot(dscores, kv_ref[rows, key_cols], 0, 0)) * factor
        ).astype(BF16)
    for c, (rows, _) in enumerate(stretches):
        share = dot(both_ref[rows, key_cols], key_weight_ref[...], 1, 1)
        share = share + dot(both_ref[rows, value_cols], value_weight_ref[...], 1, 1)
        share = share.astype(BF16)
        for piece in range(PIECES):
            ref = mine_ref if piece < 4 else other_ref
            at = piece * KNB * ROWS
            ref[piece % 4, c * KNB : (c + 1) * KNB] = share[at : at + KNB * ROWS].reshape(
                KNB, ROWS, share.shape[1]
            )
    part = dot(rows_ref[...], both_ref[...], 0, 0)

    @pl.when(step == 0)
    def _():
        total_ref[...] = part if first else begun_ref[...] + part

    @pl.when(step > 0)
    def _():
        total_ref[...] += part

    if not first:

        @pl.when(step == pl.num_programs(0) - 1)
        def _():
            for g in range(4):
                out_ref[g] = total_ref[:, g * DH : (g + 1) * DH].astype(BF16)


def attention(counts, pieces, w_key, w_value, queries, out_grad, half, begun):
    width, local = w_key.shape
    tokens = HALF * STRETCH
    panels = HALF * KNB
    steps = HALF // GROUP
    half_steps = steps // 2
    first = begun is None
    block = (GROUP * KNB, ROWS, width)
    plain = pl.BlockSpec(block, lambda i, *_: (i, 0, 0))
    low = pl.BlockSpec(block, lambda i, *_: (jnp.minimum(i, half_steps - 1), 0, 0))
    high = pl.BlockSpec(block, lambda i, *_: (jnp.maximum(i - half_steps, 0), 0, 0))
    token_in = pl.BlockSpec((GROUP * STRETCH, local), lambda i, *_: (i + half * steps, 0))
    token_out = pl.BlockSpec((GROUP * STRETCH, local), lambda i, *_: (i, 0))
    share = pl.BlockSpec((4, GROUP * KNB, ROWS, width), lambda i, *_: (0, i, 0, 0))
    whole = lambda shape: pl.BlockSpec(shape, lambda i, *_: (0,) * len(shape))
    total = (width, 2 * local)
    out = jax.ShapeDtypeStruct(total, F32) if first else jax.ShapeDtypeStruct((4, width, DH), BF16)
    token_shape = jax.ShapeDtypeStruct((tokens, local), BF16)
    share_shape = jax.ShapeDtypeStruct((4, panels, ROWS, width), BF16)
    scratch = [
        pltpu.VMEM((GROUP * SPAN, width), BF16),
        pltpu.VMEM((GROUP * SPAN, 2 * local), BF16),
        pltpu.VMEM((GROUP * SPAN, 2 * local), BF16),
    ]
    return pl.pallas_call(
        functools.partial(attention_kernel, first),
        grid_spec=pltpu.PrefetchScalarGridSpec(
            num_scalar_prefetch=1,
            grid=(steps,),
            in_specs=[plain, plain, plain, low, high] * 2
            + [whole(w_key.shape), whole(w_key.shape), token_in, token_in]
            + ([] if first else [whole(total)]),
            out_specs=[token_out, token_out, share, share, whole(out.shape)],
            scratch_shapes=scratch + ([] if first else [pltpu.VMEM(total, F32)]),
        ),
        out_shape=[token_shape, token_shape, share_shape, share_shape, out],
        compiler_params=pltpu.CompilerParams(vmem_limit_bytes=56 * 2**20),
        cost_estimate=pl.CostEstimate(
            flops=8 * 2**30, bytes_accessed=16 * 2**20, transcendentals=2**18
        ),
        name="attention",
    )(counts, *pieces, w_key, w_value, queries, out_grad, *([] if first else [begun]))


def collect_kernel(slot_ref, filled_ref, arrived_ref, out_ref):
    out_ref[...] = jnp.zeros_like(out_ref)

    def one(q, carry):
        @pl.when(filled_ref[q] != 0)
        def _():
            out_ref[slot_ref[q]] += arrived_ref[q].astype(F32)

        return carry

    lax.fori_loop(0, slot_ref.shape[0], one, 0)


def collect(slots, filled, arrived, pool_count):
    count, rows, width = arrived.shape
    return pl.pallas_call(
        collect_kernel,
        grid_spec=pltpu.PrefetchScalarGridSpec(
            num_scalar_prefetch=2,
            grid=(1,),
            in_specs=[pl.BlockSpec((count, rows, width), lambda i, *_: (0, 0, 0))],
            out_specs=pl.BlockSpec((pool_count, rows, width), lambda i, *_: (0, 0, 0)),
        ),
        out_shape=jax.ShapeDtypeStruct((pool_count, rows, width), F32),
        compiler_params=pltpu.CompilerParams(vmem_limit_bytes=16 * 2**20),
        name="collect",
    )(slots, filled, arrived)


def reduce_weight_grads(parts):
    width = parts.shape[1]
    by_x = lax.all_to_all(parts, "x", split_axis=0, concat_axis=0, tiled=True)
    part = plus(*[by_x[k] for k in range(4)]).astype(BF16).reshape(8, width // 8, DH)
    by_z = lax.all_to_all(part, "z", split_axis=0, concat_axis=0, tiled=True)
    total = plus(*[by_z[k] for k in range(8)])
    column = lax.all_gather(total, "z", axis=0, tiled=True)
    groups = lax.all_gather(column, "x", axis=0, tiled=False)
    return (
        jnp.concatenate([groups[0], groups[1]], axis=1),
        jnp.concatenate([groups[2], groups[3]], axis=1),
    )


def exchange(array):
    return lax.all_to_all(array, ("z", "x"), split_axis=0, concat_axis=0, tiled=True)


def local(queries, pool, w_key, w_value, out_grad, nb_source, nb_slot, nb_count):
    seq_count = lax.axis_size(("z", "x"))
    seq_index = lax.axis_index(("z", "x"))
    requests = CH_DEV * KNB
    capacity = max(2, 2 * requests // seq_count)
    slot_span = seq_count * capacity
    source_table = nb_source.reshape(seq_count, requests)
    slot_table = nb_slot.reshape(seq_count, requests)
    order_ids = jnp.arange(requests)
    matches = source_table[:, :, None] == source_table[:, None, :]
    before = order_ids[None, :] < order_ids[:, None]
    ranks = jnp.sum(jnp.logical_and(matches, before[None, :, :]), axis=2)
    places = jnp.arange(capacity)
    chosen = jnp.logical_and(
        (source_table == seq_index)[:, :, None], ranks[:, :, None] == places[None, None, :]
    )
    picked_slot = jnp.sum(jnp.where(chosen, slot_table[:, :, None], 0), axis=1).reshape(slot_span)
    filled = jnp.any(chosen, axis=1).reshape(slot_span).astype(jnp.int32)
    own_sources = lax.dynamic_index_in_dim(source_table, seq_index, 0, keepdims=False)
    own_ranks = lax.dynamic_index_in_dim(ranks, seq_index, 0, keepdims=False)
    positions = own_sources * capacity + own_ranks
    back = jnp.sum(
        jnp.where(positions[None, :] == jnp.arange(slot_span)[:, None], order_ids[None, :], 0), axis=1
    )
    counts = lax.dynamic_slice_in_dim(nb_count, seq_index * CH_DEV, CH_DEV)
    take = lambda array, index: jnp.take(array, index, axis=0, mode="clip")

    incoming = exchange(take(pool, picked_slot))
    begun, attended, grad_queries, summed = None, [], [], []
    panels = HALF * KNB
    pieces = [
        gather_pieces(take(incoming, positions[half * panels : (half + 1) * panels]))
        for half in range(2)
    ]
    for half in range(2):
        attended_half, grad_half, mine, other, begun = attention(
            counts[half * HALF : (half + 1) * HALF],
            pieces[half],
            w_key,
            w_value,
            queries,
            out_grad,
            half,
            begun,
        )
        attended.append(attended_half)
        grad_queries.append(grad_half)
        summed.append(scatter_pieces(mine, other))
    grad_w_key, grad_w_value = reduce_weight_grads(begun)
    arrived = exchange(take(jnp.concatenate(summed), back))
    grad_pool = collect(picked_slot, filled, arrived, pool.shape[0])
    return (
        jnp.concatenate(attended),
        jnp.concatenate(grad_queries),
        grad_pool,
        grad_w_key,
        grad_w_value,
    )


def solution(mesh):
    grid = Mesh(mesh.devices.reshape(8, 4, 4, 2), ("z", "x", "y", "core"))
    seq, head = ("z", "x"), ("y", "core")
    return jax.shard_map(
        local,
        mesh=grid,
        in_specs=(
            P(seq, head),
            P(seq, head, None),
            P(None, head),
            P(None, head),
            P(seq, head),
            P(),
            P(),
            P(),
        ),
        out_specs=(
            P(seq, head),
            P(seq, head),
            P(seq, head, None),
            P(None, head),
            P(None, head),
        ),
        check_vma=False,
    )
```

time: 402 us -> 293 us (0.73)
  waiting for transfers between devices: 288 us -> 104 us
  blocking collectives: 0 us -> 61.7 us
  matrix products: 44.9 us -> 0 us
  Pallas kernels: 0 us -> 31.1 us
  starting transfers between devices: 21.8 us -> 48.4 us
  local copies, waits for them, and re-layouts: 26.3 us -> 14.9 us
  other arithmetic: 6.16 us -> 17.2 us
    psum x1 -> x0, waiting for transfers between devices: 119 us -> none  [local(): grad_w_key, grad_w_value = lax.psum((key_partial, value_partial), 'seq')]
    all_gather x0 -> x1, blocking collectives: none -> 61.7 us  [reduce_weight_grads(): column = lax.all_gather(total, 'z', axis=0, tiled=True)]
    reduce_scatter x1 -> x0, waiting for transfers between devices: 48.8 us -> none  [local(): lax.psum_scatter((jnp.einsum('jrc,ec->rje', grad_keys, w_key, preferred_e...]
    dot_general x13 -> x0, matrix products: 44.9 us -> none  [the longest x1 7.93 us: local(): jnp.einsum('jre,ec->jrc', panel_piece, both_weights, preferred_element_ty...]
    all_to_all x2 -> x4, waiting for transfers between devices: 77.5 us -> 44.5 us  [the longest x2 44.5 us: exchange(): lax.all_to_all(array, ('z', 'x'), split_axis=0, concat_axis=0, tiled=True)]
    pallas_call x0 -> x3, Pallas kernels: none -> 31.1 us  [the longest x2 28.1 us: attention(): pl.pallas_call(functools.partial(attention_kernel, first), grid_spec=pltp...]
    ppermute x0 -> x28, waiting for transfers between devices: none -> 30.3 us  [the longest x2 14 us: gather_pieces(): below = lax.ppermute(own, 'y', UP)]
    ppermute x0 -> x28, starting transfers between devices: none -> 23.1 us  [the longest x2 4.28 us: scatter_pieces(): from_above = lax.ppermute(jnp.concatenate([down_low, down_high]), 'y', DOWN)]
  transfers between devices with their start and end apart: 5 -> 33, of which waited for: 5 -> 13; matrix products, arithmetic and copies ran while one was open for 6% -> 8% of each run, Pallas kernels for 0% -> 5%
where the time goes in v1:
time: 293 us; the launch traced here: 292 us
  waiting for transfers between devices  104 us (35%)
  blocking collectives  61.7 us (21%)
  starting transfers between devices  48.4 us (17%)
  Pallas kernels  31.1 us (11%)
  other arithmetic  17.2 us (6%)
  local copies, waits for them, and re-layouts  14.9 us (5%)
  between operations  14.5 us (5%)
    all_gather x1, blocking collectives, reduce_weight_grads(): column = lax.all_gather(total, 'z', axis=0, tiled=True)  61.7 us
    all_to_all x2, waiting for transfers between devices, exchange(): lax.all_to_all(array, ('z', 'x'), split_axis=0, concat_axis=0, tiled=True)  44.5 us
    all_gather x1, waiting for transfers between devices, reduce_weight_grads(): groups = lax.all_gather(column, 'x', axis=0, tiled=False)  29.1 us
    pallas_call x2, Pallas kernels, attention(): pl.pallas_call(functools.partial(attention_kernel, first), grid_spec=pltp...  28.1 us
    all_to_all x2, starting transfers between devices, exchange(): lax.all_to_all(array, ('z', 'x'), split_axis=0, concat_axis=0, tiled=True)  16.4 us
    ppermute x2, waiting for transfers between devices, gather_pieces(): below = lax.ppermute(own, 'y', UP)  14 us
    gather x4, local copies, waits for them, and re-layouts, local(): take = lambda array, index: jnp.take(array, index, axis=0, mode='clip')  5.94 us
  transfers between devices with their start and end apart: 33, of which 13 were waited for; matrix products, arithmetic and copies ran while one was open for 8% of the time, Pallas kernels for 5%

profile of v1, /device:TPU:8, one launch (start us, length us, event | category | flops | bytes accessed | tf_op | source)
XLA Modules:
  0.0 291.6 jit_solution(11845950244835346429)
XLA Ops:
  7.2 0.9 copy.15
  9.1 0.8 copy.16
  10.4 2.0 gather_fusion
  12.4 11.3 %all-to-all-start = ((bf16[64,16,896]{2,1,0:T(8,128)(2,1)}), bf16[64,16,896]{2,1,0:T(8,128)(2,1)S(1)}, u32[]{:S(2)}, u32[]{:S(2)}) async-start(bf16[64,16,896]{2,1,0:T(8,128)(2,1)} %gather_fusion), calls=%async_computation | async-start | bytes 3670016 | tf_op jit(solution)/shard_map/all_to_all | solution.py:268
  23.8 44.5 %all-to-all-done = bf16[64,16,896]{2,1,0:T(8,128)(2,1)S(1)} async-done(((bf16[64,16,896]{2,1,0:T(8,128)(2,1)}), bf16[64,16,896]{2,1,0:T(8,128)(2,1)S(1)}, u32[]{:S(2)}, u32[]{:S(2)}) %all-to-all-start) | async-done | bytes 1835040 | tf_op jit(solution)/shard_map/all_to_all | solution.py:268
  68.3 1.4 gather_fusion.1
  69.7 1.6 collective-permute-start.1
  72.4 1.7 collective-permute-start.10
  74.5 9.0 %collective-permute-done.1.refs_2_ = bf16[16,16,896]{2,1,0:T(8,128)(2,1)} collective-permute-done((bf16[16,16,896]{2,1,0:T(8,128)(2,1)}, bf16[16,16,896]{2,1,0:T(8,128)(2,1)}, u32[]{:S(2)}, u32[]{:S(2)}) %collective-permute-start.1) | collective-permute-done | bytes 458784 | tf_op jit(solution)/shard_map/ppermute | solution.py:39
  83.5 1.0 slice.242
  84.4 1.7 collective-permute-start.2
  86.1 1.0 slice.243
  87.6 5.0 %collective-permute-done.10.refs_2_ = bf16[16,16,896]{2,1,0:T(8,128)(2,1)S(1)} collective-permute-done((bf16[16,16,896]{2,1,0:T(8,128)(2,1)S(1)}, bf16[16,16,896]{2,1,0:T(8,128)(2,1)S(1)}, u32[]{:S(2)}, u32[]{:S(2)}) %collective-permute-start.10) | collective-permute-done | bytes 458784 | tf_op jit(solution)/shard_map/ppermute | solution.py:39
  92.7 1.7 collective-permute-start.11
  95.2 1.7 collective-permute-start.12
  96.9 3.9 %collective-permute-done.11.refs_3_ = bf16[8,16,896]{2,1,0:T(8,128)(2,1)S(1)} collective-permute-done((bf16[8,16,896]{2,1,0:T(8,128)(2,1)S(1)}, bf16[8,16,896]{2,1,0:T(8,128)(2,1)S(1)}, u32[]{:S(2)}, u32[]{:S(2)}) %collective-permute-start.11) | collective-permute-done | bytes 229408 | tf_op jit(solution)/shard_map/ppermute | solution.py:41
  104.0 13.8 %attention.2 = (bf16[512,256]{1,0:T(8,128)(2,1)}, bf16[512,256]{1,0:T(8,128)(2,1)}, bf16[4,16,16,896]{3,2,1,0:T(8,128)(2,1)}, bf16[4,16,16,896]{3,2,1,0:T(8,128)(2,1)}, f32[896,512]{1,0:T(8,128)}) custom-call(s32[8]{0:T(128)} %get-tuple-element.43.count_ref, bf16[16,16,896]{2,1,0:T(8,128)(2,1)} %gather_fusion.1, ...), custom_call_target="tpu_custom_call" | custom-call | flops 8589934592 | bytes 16777216 | tf_op jit(solution)/shard_map/attention/pallas_call | solution.py:204
  119.1 14.4 %attention.3 = (bf16[512,256]{1,0:T(8,128)(2,1)}, bf16[512,256]{1,0:T(8,128)(2,1)}, bf16[4,16,16,896]{3,2,1,0:T(8,128)(2,1)}, bf16[4,16,16,896]{3,2,1,0:T(8,128)(2,1)}, bf16[4,896,128]{2,1,0:T(8,128)(2,1)}) custom-call(s32[8]{0:T(128)} %get-tuple-element.44.count_ref, bf16[16,16,896]{2,1,0:T(8,128)(2,1)} %copy-done.3, bf16[16,16,896]{2,1,0:T(8,128)(2,1)} %copy-done.7, ...), custom_call_target="tpu_custom_call" | custom-call | flops 8589934592 | bytes 16777216 | tf_op jit(solution)/shard_map/attention/pallas_call | solution.py:204
  134.2 5.4 %all-to-all-start.2 = ((bf16[4,896,128]{2,1,0:T(8,128)(2,1)}), bf16[4,896,128]{2,1,0:T(8,128)(2,1)S(1)}, u32[]{:S(2)}, u32[]{:S(2)}) async-start(bf16[4,896,128]{2,1,0:T(8,128)(2,1)} %get-tuple-element.24), calls=%async_computation.2 | async-start | bytes 1835008 | tf_op jit(solution)/shard_map/all_to_all | solution.py:255
  139.6 1.4 add_convert_fusion
  141.1 1.8 collective-permute-start.24
  142.9 1.4 collective-permute-start.26
  144.3 1.2 add_convert_fusion.1
  145.5 1.2 collective-permute-start.19
  146.6 2.2 collective-permute-start.21
  148.8 1.2 fusion.10
  150.0 1.2 fusion.8
  151.8 1.2 fusion.5
  153.1 2.6 collective-permute-start.27
  155.8 0.8 collective-permute-done.21
  156.7 1.2 fusion.7
  158.0 1.7 collective-permute-start.22
  159.6 0.8 pad_maximum_fusion.5
  161.7 3.4 %all-to-all-start.3 = ((bf16[8,112,128]{2,1,0:T(8,128)(2,1)}), bf16[8,112,128]{2,1,0:T(8,128)(2,1)S(1)}, u32[]{:S(2)}, u32[]{:S(2)}) async-start(bf16[8,112,128]{2,1,0:T(8,128)(2,1)} %bitcast.17), calls=%async_computation.3 | async-start | bytes 458752 | tf_op jit(solution)/shard_map/all_to_all | solution.py:257
  165.1 1.6 collective-permute-done.27
  166.7 3.1 %collective-permute-done.25 = bf16[16,16,896]{2,1,0:T(8,128)(2,1)} collective-permute-done((bf16[16,16,896]{2,1,0:T(8,128)(2,1)S(1)}, bf16[16,16,896]{2,1,0:T(8,128)(2,1)}, u32[]{:S(2)}, u32[]{:S(2)}) %collective-permute-start.25) | collective-permute-done | bytes 458784 | tf_op jit(solution)/shard_map/ppermute | solution.py:64
  169.8 1.7 fusion.1
  171.4 4.0 %collective-permute-done.22 = bf16[16,16,896]{2,1,0:T(8,128)(2,1)} collective-permute-done((bf16[16,16,896]{2,1,0:T(8,128)(2,1)S(1)}, bf16[16,16,896]{2,1,0:T(8,128)(2,1)}, u32[]{:S(2)}, u32[]{:S(2)}) %collective-permute-start.22) | collective-permute-done | bytes 458784 | tf_op jit(solution)/shard_map/ppermute | solution.py:65
  175.4 1.4 collective-permute-done.20
  176.8 1.7 fusion.3
  178.6 2.0 gather_fusion.3
  180.5 5.1 %all-to-all-start.1 = ((bf16[64,16,896]{2,1,0:T(8,128)(2,1)}), bf16[64,16,896]{2,1,0:T(8,128)(2,1)S(1)}, u32[]{:S(2)}, u32[]{:S(2)}) async-start(bf16[64,16,896]{2,1,0:T(8,128)(2,1)} %gather_fusion.3), calls=%async_computation.1 | async-start | bytes 3670016 | tf_op jit(solution)/shard_map/all_to_all | solution.py:268
  185.7 61.7 %all-gather.1 = f32[1,896,128]{2,1,0:T(8,128)} all-gather(f32[1,112,128]{2,1,0:T(8,128)S(1)} %add_add_fusion), channel_id=3, replica_groups=mesh['z'=8,'x'=4,'y'=4,'core'=2] {'z'}, dimensions={1}, use_global_device_ids=true | all-gather | bytes 516096 | tf_op jit(solution)/shard_map/all_gather | solution.py:259
  247.8 2.1 pad_maximum_fusion.3
  249.9 29.1 %all-gather.5.cloned.1.call-done = f32[1,3584,128]{2,1,0:T(8,128)} async-done(((f32[1,896,128]{2,1,0:T(8,128)}), f32[1,3584,128]{2,1,0:T(8,128)}) %all-gather.5.cloned.1.call-update) | async-done | bytes 1835024 | tf_op jit(solution)/shard_map/all_gather | solution.py:260
  278.9 1.6 slice_bitcast_fusion.1
  280.5 1.3 pad_maximum_fusion.1
  281.8 2.9 %collect.1 = f32[32,16,896]{2,1,0:T(8,128)} custom-call(s32[64]{0:T(128)S(1)} %reshape.134.slot_ref, s32[64]{0:T(128)S(1)} %reshape.124.filled_ref, bf16[64,16,896]{2,1,0:T(8,128)(2,1)S(1)} %all-to-all-done.1.arrived_ref), custom_call_target="tpu_custom_call" | custom-call | tf_op jit(solution)/shard_map/collect/pallas_call | solution.py:239
  (110 shorter events, 12.3 us)
Async XLA Ops:
  7.2 3.2 %copy-start = (bf16[32,16,896]{2,1,0:T(8,128)(2,1)S(1)}, bf16[32,16,896]{2,1,0:T(8,128)(2,1)}, u32[]{:S(2)}) copy-start(bf16[32,16,896]{2,1,0:T(8,128)(2,1)} %param.9) | copy-start | bytes 2752516
  12.4 56.0 %all-to-all-start = ((bf16[64,16,896]{2,1,0:T(8,128)(2,1)}), bf16[64,16,896]{2,1,0:T(8,128)(2,1)S(1)}, u32[]{:S(2)}, u32[]{:S(2)}) async-start(bf16[64,16,896]{2,1,0:T(8,128)(2,1)} %gather_fusion), calls=%async_computation | async-start | bytes 3670016 | tf_op jit(solution)/shard_map/all_to_all | solution.py:268
  69.7 13.8 %collective-permute-start.1 = (bf16[16,16,896]{2,1,0:T(8,128)(2,1)}, bf16[16,16,896]{2,1,0:T(8,128)(2,1)}, u32[]{:S(2)}, u32[]{:S(2)}) collective-permute-start(bf16[16,16,896]{2,1,0:T(8,128)(2,1)} %gather_fusion.1), channel_id=1, source_target_pairs={{0,2},{2,4},{4,6},{6,0},{1,3},{3,5},{5,7},{7,1},{8,10},{10,12},{12... | collective-permute-start | bytes 1376264 | tf_op jit(solution)/shard_map/ppermute | solution.py:39
  71.3 14.8 %collective-permute-start = (bf16[16,16,896]{2,1,0:T(8,128)(2,1)}, bf16[16,16,896]{2,1,0:T(8,128)(2,1)}, u32[]{:S(2)}, u32[]{:S(2)}) collective-permute-start(bf16[16,16,896]{2,1,0:T(8,128)(2,1)} %gather_fusion.1), channel_id=1, source_target_pairs={{2,0},{4,2},{6,4},{0,6},{3,1},{5,3},{7,5},{1,7},{10,8},{12,10},{14... | collective-permute-start | bytes 1376264 | tf_op jit(solution)/shard_map/ppermute | solution.py:40
  72.4 45.4 %copy-start.3 = (bf16[16,16,896]{2,1,0:T(8,128)(2,1)}, bf16[16,16,896]{2,1,0:T(8,128)(2,1)S(1)}, u32[]{:S(2)}) copy-start(bf16[16,16,896]{2,1,0:T(8,128)(2,1)S(1)} %gather_fusion.2) | copy-start | bytes 1376260
  72.4 20.3 %collective-permute-start.10 = (bf16[16,16,896]{2,1,0:T(8,128)(2,1)S(1)}, bf16[16,16,896]{2,1,0:T(8,128)(2,1)S(1)}, u32[]{:S(2)}, u32[]{:S(2)}) collective-permute-start(bf16[16,16,896]{2,1,0:T(8,128)(2,1)S(1)} %gather_fusion.2), channel_id=1, source_target_pairs={{0,2},{2,4},{4,6},{6,0},{1,3},{3,5},{5,7},{7,1},{8,10},{10,12},{12... | collective-permute-start | bytes 1376264 | tf_op jit(solution)/shard_map/ppermute | solution.py:39
  74.0 18.6 %collective-permute-start.4 = (bf16[16,16,896]{2,1,0:T(8,128)(2,1)}, bf16[16,16,896]{2,1,0:T(8,128)(2,1)S(1)}, u32[]{:S(2)}, u32[]{:S(2)}) collective-permute-start(bf16[16,16,896]{2,1,0:T(8,128)(2,1)} %gather_fusion.1), channel_id=1, source_target_pairs={{0,1},{1,0},{2,3},{3,2},{4,5},{5,4},{6,7},{7,6},{8,9},{9,8},{10,11... | collective-permute-start | bytes 1376264 | tf_op jit(solution)/shard_map/ppermute | solution.py:44
  74.0 20.3 %collective-permute-start.9 = (bf16[16,16,896]{2,1,0:T(8,128)(2,1)S(1)}, bf16[16,16,896]{2,1,0:T(8,128)(2,1)S(1)}, u32[]{:S(2)}, u32[]{:S(2)}) collective-permute-start(bf16[16,16,896]{2,1,0:T(8,128)(2,1)S(1)} %gather_fusion.2), channel_id=1, source_target_pairs={{2,0},{4,2},{6,4},{0,6},{3,1},{5,3},{7,5},{1,7},{10,8},{12,10},{14... | collective-permute-start | bytes 1376264 | tf_op jit(solution)/shard_map/ppermute | solution.py:40
  84.4 10.8 %collective-permute-start.2 = (bf16[8,16,896]{2,1,0:T(8,128)(2,1)S(1)}, bf16[8,16,896]{2,1,0:T(8,128)(2,1)}, u32[]{:S(2)}, u32[]{:S(2)}) collective-permute-start(bf16[8,16,896]{2,1,0:T(8,128)(2,1)S(1)} %slice.242), channel_id=1, source_target_pairs={{0,2},{2,4},{4,6},{6,0},{1,3},{3,5},{5,7},{7,1},{8,10},{10,12},{12... | collective-permute-start | bytes 688136 | tf_op jit(solution)/shard_map/ppermute | solution.py:41
  87.1 9.9 %collective-permute-start.3 = (bf16[8,16,896]{2,1,0:T(8,128)(2,1)S(1)}, bf16[8,16,896]{2,1,0:T(8,128)(2,1)}, u32[]{:S(2)}, u32[]{:S(2)}) collective-permute-start(bf16[8,16,896]{2,1,0:T(8,128)(2,1)S(1)} %slice.243), channel_id=1, source_target_pairs={{2,0},{4,2},{6,4},{0,6},{3,1},{5,3},{7,5},{1,7},{10,8},{12,10},{14... | collective-permute-start | bytes 688136 | tf_op jit(solution)/shard_map/ppermute | solution.py:42
  92.6 25.1 %copy-start.6 = (bf16[16,16,896]{2,1,0:T(8,128)(2,1)}, bf16[16,16,896]{2,1,0:T(8,128)(2,1)S(1)}, u32[]{:S(2)}) copy-start(bf16[16,16,896]{2,1,0:T(8,128)(2,1)S(1)} %collective-permute-done.10.refs_2_) | copy-start | bytes 1376260
  92.6 10.4 %collective-permute-start.6 = (bf16[16,16,896]{2,1,0:T(8,128)(2,1)}, bf16[16,16,896]{2,1,0:T(8,128)(2,1)}, u32[]{:S(2)}, u32[]{:S(2)}) collective-permute-start(bf16[16,16,896]{2,1,0:T(8,128)(2,1)} %collective-permute-done.1.refs_2_), channel_id=1, source_target_pairs={{0,1},{1,0},{2,3},{3,2},{4,5},{5,4},{6,7},{7,6},{8,9},{9,8},{10,11... | collective-permute-start | bytes 1376264 | tf_op jit(solution)/shard_map/ppermute | solution.py:44
  92.7 8.1 %copy-start.8 = (bf16[16,16,896]{2,1,0:T(8,128)(2,1)}, bf16[16,16,896]{2,1,0:T(8,128)(2,1)S(1)}, u32[]{:S(2)}) copy-start(bf16[16,16,896]{2,1,0:T(8,128)(2,1)S(1)} %collective-permute-done.4.refs_5_) | copy-start | bytes 1376260
  92.7 8.1 %collective-permute-start.11 = (bf16[8,16,896]{2,1,0:T(8,128)(2,1)S(1)}, bf16[8,16,896]{2,1,0:T(8,128)(2,1)S(1)}, u32[]{:S(2)}, u32[]{:S(2)}) collective-permute-start(bf16[8,16,896]{2,1,0:T(8,128)(2,1)S(1)} %slice.244), channel_id=1, source_target_pairs={{0,2},{2,4},{4,6},{6,0},{1,3},{3,5},{5,7},{7,1},{8,10},{10,12},{12... | collective-permute-start | bytes 688136 | tf_op jit(solution)/shard_map/ppermute | solution.py:41
  94.3 23.4 %copy-start.7 = (bf16[16,16,896]{2,1,0:T(8,128)(2,1)}, bf16[16,16,896]{2,1,0:T(8,128)(2,1)S(1)}, u32[]{:S(2)}) copy-start(bf16[16,16,896]{2,1,0:T(8,128)(2,1)S(1)} %collective-permute-done.9.refs_1_) | copy-start | bytes 1376260
  94.3 9.2 %collective-permute-start.5 = (bf16[16,16,896]{2,1,0:T(8,128)(2,1)}, bf16[16,16,896]{2,1,0:T(8,128)(2,1)}, u32[]{:S(2)}, u32[]{:S(2)}) collective-permute-start(bf16[16,16,896]{2,1,0:T(8,128)(2,1)} %collective-permute-done.refs_1_), channel_id=1, source_target_pairs={{0,1},{1,0},{2,3},{3,2},{4,5},{5,4},{6,7},{7,6},{8,9},{9,8},{10,11... | collective-permute-start | bytes 1376264 | tf_op jit(solution)/shard_map/ppermute | solution.py:44
  95.2 7.3 %collective-permute-start.12 = (bf16[8,16,896]{2,1,0:T(8,128)(2,1)S(1)}, bf16[8,16,896]{2,1,0:T(8,128)(2,1)S(1)}, u32[]{:S(2)}, u32[]{:S(2)}) collective-permute-start(bf16[8,16,896]{2,1,0:T(8,128)(2,1)S(1)} %slice.245), channel_id=1, source_target_pairs={{2,0},{4,2},{6,4},{0,6},{3,1},{5,3},{7,5},{1,7},{10,8},{12,10},{14... | collective-permute-start | bytes 688136 | tf_op jit(solution)/shard_map/ppermute | solution.py:42
  96.9 5.7 %collective-permute-start.7 = (bf16[8,16,896]{2,1,0:T(8,128)(2,1)}, bf16[8,16,896]{2,1,0:T(8,128)(2,1)S(1)}, u32[]{:S(2)}, u32[]{:S(2)}) collective-permute-start(bf16[8,16,896]{2,1,0:T(8,128)(2,1)} %collective-permute-done.2.refs_3_), channel_id=1, source_target_pairs={{0,1},{1,0},{2,3},{3,2},{4,5},{5,4},{6,7},{7,6},{8,9},{9,8},{10,11... | collective-permute-start | bytes 688136 | tf_op jit(solution)/shard_map/ppermute | solution.py:44
  100.8 17.0 %copy-start.12 = (bf16[8,16,896]{2,1,0:T(8,128)(2,1)}, bf16[8,16,896]{2,1,0:T(8,128)(2,1)S(1)}, u32[]{:S(2)}) copy-start(bf16[8,16,896]{2,1,0:T(8,128)(2,1)S(1)} %collective-permute-done.11.refs_3_) | copy-start | bytes 688132
  100.8 2.5 collective-permute-start.8
  102.5 15.3 %copy-start.13 = (bf16[8,16,896]{2,1,0:T(8,128)(2,1)}, bf16[8,16,896]{2,1,0:T(8,128)(2,1)S(1)}, u32[]{:S(2)}) copy-start(bf16[8,16,896]{2,1,0:T(8,128)(2,1)S(1)} %collective-permute-done.12.refs_4_) | copy-start | bytes 688132
  102.5 15.3 %collective-permute-start.13 = (bf16[16,16,896]{2,1,0:T(8,128)(2,1)S(1)}, bf16[16,16,896]{2,1,0:T(8,128)(2,1)S(1)}, u32[]{:S(2)}, u32[]{:S(2)}) collective-permute-start(bf16[16,16,896]{2,1,0:T(8,128)(2,1)S(1)} %gather_fusion.2), channel_id=1, source_target_pairs={{0,1},{1,0},{2,3},{3,2},{4,5},{5,4},{6,7},{7,6},{8,9},{9,8},{10,11... | collective-permute-start | bytes 1376264 | tf_op jit(solution)/shard_map/ppermute | solution.py:44
  102.7 1.1 copy-start.14
  102.7 15.2 %collective-permute-start.15 = (bf16[16,16,896]{2,1,0:T(8,128)(2,1)S(1)}, bf16[16,16,896]{2,1,0:T(8,128)(2,1)S(1)}, u32[]{:S(2)}, u32[]{:S(2)}) collective-permute-start(bf16[16,16,896]{2,1,0:T(8,128)(2,1)S(1)} %collective-permute-done.10.refs_2_), channel_id=1, source_target_pairs={{0,1},{1,0},{2,3},{3,2},{4,5},{5,4},{6,7},{7,6},{8,9},{9,8},{10,11... | collective-permute-start | bytes 1376264 | tf_op jit(solution)/shard_map/ppermute | solution.py:44
  103.0 14.9 %collective-permute-start.14 = (bf16[16,16,896]{2,1,0:T(8,128)(2,1)S(1)}, bf16[16,16,896]{2,1,0:T(8,128)(2,1)S(1)}, u32[]{:S(2)}, u32[]{:S(2)}) collective-permute-start(bf16[16,16,896]{2,1,0:T(8,128)(2,1)S(1)} %collective-permute-done.9.refs_1_), channel_id=1, source_target_pairs={{0,1},{1,0},{2,3},{3,2},{4,5},{5,4},{6,7},{7,6},{8,9},{9,8},{10,11... | collective-permute-start | bytes 1376264 | tf_op jit(solution)/shard_map/ppermute | solution.py:44
  103.3 14.5 %collective-permute-start.16 = (bf16[8,16,896]{2,1,0:T(8,128)(2,1)S(1)}, bf16[8,16,896]{2,1,0:T(8,128)(2,1)S(1)}, u32[]{:S(2)}, u32[]{:S(2)}) collective-permute-start(bf16[8,16,896]{2,1,0:T(8,128)(2,1)S(1)} %collective-permute-done.11.refs_3_), channel_id=1, source_target_pairs={{0,1},{1,0},{2,3},{3,2},{4,5},{5,4},{6,7},{7,6},{8,9},{9,8},{10,11... | collective-permute-start | bytes 688136 | tf_op jit(solution)/shard_map/ppermute | solution.py:44
  103.5 14.3 %collective-permute-start.17 = (bf16[8,16,896]{2,1,0:T(8,128)(2,1)S(1)}, bf16[8,16,896]{2,1,0:T(8,128)(2,1)S(1)}, u32[]{:S(2)}, u32[]{:S(2)}) collective-permute-start(bf16[8,16,896]{2,1,0:T(8,128)(2,1)S(1)} %collective-permute-done.12.refs_4_), channel_id=1, source_target_pairs={{0,1},{1,0},{2,3},{3,2},{4,5},{5,4},{6,7},{7,6},{8,9},{9,8},{10,11... | collective-permute-start | bytes 688136 | tf_op jit(solution)/shard_map/ppermute | solution.py:44
  117.8 1.0 copy-start.10
  117.8 1.1 copy-start.17
  117.9 1.2 copy-start.11
  133.5 6.1 %collective-permute-start.23 = (bf16[4,16,16,896]{3,2,1,0:T(8,128)(2,1)}, bf16[4,16,16,896]{3,2,1,0:T(8,128)(2,1)}, u32[]{:S(2)}, u32[]{:S(2)}) collective-permute-start(bf16[4,16,16,896]{3,2,1,0:T(8,128)(2,1)} %get-tuple-element.23), channel_id=1, source_target_pairs={{0,1},{1,0},{2,3},{3,2},{4,5},{5,4},{6,7},{7,6},{8,9},{9,8},{10,11... | collective-permute-start | bytes 5505032 | tf_op jit(solution)/shard_map/ppermute | solution.py:55
  133.8 10.4 %collective-permute-start.18 = (bf16[4,16,16,896]{3,2,1,0:T(8,128)(2,1)}, bf16[4,16,16,896]{3,2,1,0:T(8,128)(2,1)}, u32[]{:S(2)}, u32[]{:S(2)}) collective-permute-start(bf16[4,16,16,896]{3,2,1,0:T(8,128)(2,1)} %get-tuple-element.21), channel_id=1, source_target_pairs={{0,1},{1,0},{2,3},{3,2},{4,5},{5,4},{6,7},{7,6},{8,9},{9,8},{10,11... | collective-permute-start | bytes 5505032 | tf_op jit(solution)/shard_map/ppermute | solution.py:55
  134.2 26.7 %all-to-all-start.2 = ((bf16[4,896,128]{2,1,0:T(8,128)(2,1)}), bf16[4,896,128]{2,1,0:T(8,128)(2,1)S(1)}, u32[]{:S(2)}, u32[]{:S(2)}) async-start(bf16[4,896,128]{2,1,0:T(8,128)(2,1)} %get-tuple-element.24), calls=%async_computation.2 | async-start | bytes 1835008 | tf_op jit(solution)/shard_map/all_to_all | solution.py:255
  139.6 4.6 %copy-start.1 = (bf16[4,16,16,896]{3,2,1,0:T(8,128)(2,1)S(1)}, bf16[4,16,16,896]{3,2,1,0:T(8,128)(2,1)}, u32[]{:S(2)}) copy-start(bf16[4,16,16,896]{3,2,1,0:T(8,128)(2,1)} %get-tuple-element.20) | copy-start | bytes 5505028
  141.0 7.7 %copy-start.2 = (bf16[4,16,16,896]{3,2,1,0:T(8,128)(2,1)S(1)}, bf16[4,16,16,896]{3,2,1,0:T(8,128)(2,1)}, u32[]{:S(2)}) copy-start(bf16[4,16,16,896]{3,2,1,0:T(8,128)(2,1)} %get-tuple-element.22) | copy-start | bytes 5505028
  141.1 10.1 %collective-permute-start.24 = (bf16[8,16,896]{2,1,0:T(8,128)(2,1)S(1)}, bf16[8,16,896]{2,1,0:T(8,128)(2,1)S(1)}, u32[]{:S(2)}, u32[]{:S(2)}) collective-permute-start(bf16[8,16,896]{2,1,0:T(8,128)(2,1)S(1)} %get-tuple-element.39), channel_id=1, source_target_pairs={{0,2},{2,4},{4,6},{6,0},{1,3},{3,5},{5,7},{7,1},{8,10},{10,12},{12... | collective-permute-start | bytes 688136 | tf_op jit(solution)/shard_map/ppermute | solution.py:58
  142.9 8.9 %collective-permute-start.26 = (bf16[8,16,896]{2,1,0:T(8,128)(2,1)S(1)}, bf16[8,16,896]{2,1,0:T(8,128)(2,1)S(1)}, u32[]{:S(2)}, u32[]{:S(2)}) collective-permute-start(bf16[8,16,896]{2,1,0:T(8,128)(2,1)S(1)} %get-tuple-element.40), channel_id=1, source_target_pairs={{2,0},{4,2},{6,4},{0,6},{3,1},{5,3},{7,5},{1,7},{10,8},{12,10},{14... | collective-permute-start | bytes 688136 | tf_op jit(solution)/shard_map/ppermute | solution.py:59
  145.5 10.4 %collective-permute-start.19 = (bf16[8,16,896]{2,1,0:T(8,128)(2,1)S(1)}, bf16[8,16,896]{2,1,0:T(8,128)(2,1)S(1)}, u32[]{:S(2)}, u32[]{:S(2)}) collective-permute-start(bf16[8,16,896]{2,1,0:T(8,128)(2,1)S(1)} %get-tuple-element.37), channel_id=1, source_target_pairs={{0,2},{2,4},{4,6},{6,0},{1,3},{3,5},{5,7},{7,1},{8,10},{10,12},{12... | collective-permute-start | bytes 688136 | tf_op jit(solution)/shard_map/ppermute | solution.py:58
  146.6 10.1 %collective-permute-start.21 = (bf16[8,16,896]{2,1,0:T(8,128)(2,1)S(1)}, bf16[8,16,896]{2,1,0:T(8,128)(2,1)S(1)}, u32[]{:S(2)}, u32[]{:S(2)}) collective-permute-start(bf16[8,16,896]{2,1,0:T(8,128)(2,1)S(1)} %get-tuple-element.38), channel_id=1, source_target_pairs={{2,0},{4,2},{6,4},{0,6},{3,1},{5,3},{7,5},{1,7},{10,8},{12,10},{14... | collective-permute-start | bytes 688136 | tf_op jit(solution)/shard_map/ppermute | solution.py:59
  153.1 13.6 %collective-permute-start.27 = (bf16[16,16,896]{2,1,0:T(8,128)(2,1)S(1)}, bf16[16,16,896]{2,1,0:T(8,128)(2,1)}, u32[]{:S(2)}, u32[]{:S(2)}) collective-permute-start(bf16[16,16,896]{2,1,0:T(8,128)(2,1)S(1)} %pad_maximum_fusion.8), channel_id=1, source_target_pairs={{2,0},{4,2},{6,4},{0,6},{3,1},{5,3},{7,5},{1,7},{10,8},{12,10},{14... | collective-permute-start | bytes 1376264 | tf_op jit(solution)/shard_map/ppermute | solution.py:65
  155.7 14.0 %collective-permute-start.25 = (bf16[16,16,896]{2,1,0:T(8,128)(2,1)S(1)}, bf16[16,16,896]{2,1,0:T(8,128)(2,1)}, u32[]{:S(2)}, u32[]{:S(2)}) collective-permute-start(bf16[16,16,896]{2,1,0:T(8,128)(2,1)S(1)} %pad_maximum_fusion.7), channel_id=1, source_target_pairs={{0,2},{2,4},{4,6},{6,0},{1,3},{3,5},{5,7},{7,1},{8,10},{10,12},{12... | collective-permute-start | bytes 1376264 | tf_op jit(solution)/shard_map/ppermute | solution.py:64
  158.0 17.5 %collective-permute-start.22 = (bf16[16,16,896]{2,1,0:T(8,128)(2,1)S(1)}, bf16[16,16,896]{2,1,0:T(8,128)(2,1)}, u32[]{:S(2)}, u32[]{:S(2)}) collective-permute-start(bf16[16,16,896]{2,1,0:T(8,128)(2,1)S(1)} %pad_maximum_fusion.6), channel_id=1, source_target_pairs={{2,0},{4,2},{6,4},{0,6},{3,1},{5,3},{7,5},{1,7},{10,8},{12,10},{14... | collective-permute-start | bytes 1376264 | tf_op jit(solution)/shard_map/ppermute | solution.py:65
  160.4 16.3 %collective-permute-start.20 = (bf16[16,16,896]{2,1,0:T(8,128)(2,1)}, bf16[16,16,896]{2,1,0:T(8,128)(2,1)}, u32[]{:S(2)}, u32[]{:S(2)}) collective-permute-start(bf16[16,16,896]{2,1,0:T(8,128)(2,1)} %pad_maximum_fusion.5), channel_id=1, source_target_pairs={{0,2},{2,4},{4,6},{6,0},{1,3},{3,5},{5,7},{7,1},{8,10},{10,12},{12... | collective-permute-start | bytes 1376264 | tf_op jit(solution)/shard_map/ppermute | solution.py:64
  161.7 18.8 %all-to-all-start.3 = ((bf16[8,112,128]{2,1,0:T(8,128)(2,1)}), bf16[8,112,128]{2,1,0:T(8,128)(2,1)S(1)}, u32[]{:S(2)}, u32[]{:S(2)}) async-start(bf16[8,112,128]{2,1,0:T(8,128)(2,1)} %bitcast.17), calls=%async_computation.3 | async-start | bytes 458752 | tf_op jit(solution)/shard_map/all_to_all | solution.py:257
  180.5 67.2 %copy-start.4 = (bf16[512,256]{1,0:T(8,128)(2,1)S(1)}, bf16[512,256]{1,0:T(8,128)(2,1)}, u32[]{:S(2)}) copy-start(bf16[512,256]{1,0:T(8,128)(2,1)} %get-tuple-element.15) | copy-start | bytes 786436
  180.5 67.3 %copy-start.5 = (bf16[512,256]{1,0:T(8,128)(2,1)S(1)}, bf16[512,256]{1,0:T(8,128)(2,1)}, u32[]{:S(2)}) copy-start(bf16[512,256]{1,0:T(8,128)(2,1)} %get-tuple-element.18) | copy-start | bytes 786436
  180.5 101.3 %all-to-all-start.1 = ((bf16[64,16,896]{2,1,0:T(8,128)(2,1)}), bf16[64,16,896]{2,1,0:T(8,128)(2,1)S(1)}, u32[]{:S(2)}, u32[]{:S(2)}) async-start(bf16[64,16,896]{2,1,0:T(8,128)(2,1)} %gather_fusion.3), calls=%async_computation.1 | async-start | bytes 3670016 | tf_op jit(solution)/shard_map/all_to_all | solution.py:268
  185.6 93.3 %all-gather.5.cloned.1.call-start = ((), (), s32[]{:S(2)}) async-start(), calls=%async_computation.4 | async-start | bytes 2293760 | tf_op jit(solution)/shard_map/all_gather | solution.py:260
  (3 other events, 2.3 us)
Sparse Core Ops, SparseCore 0:
  247.6 31.3 all-gather.4

commit v2 on v1

--- a/solution.py
+++ b/solution.py
@@ -51,10 +51,10 @@
     return total
 
 
-def scatter_pieces(mine, other):
+def scatter_pieces(mine, other, parts):
     swapped = lax.ppermute(other, "core", SWAP)
     half = mine.shape[1] // 2
-    far = plus(mine[3], swapped[3]).astype(BF16)
+    far, parts = lax.optimization_barrier((plus(mine[3], swapped[3]).astype(BF16), parts))
     got_low = lax.ppermute(far[:half], "y", UP)
     got_high = lax.ppermute(far[half:], "y", DOWN)
     up_low = plus(mine[1, :half], swapped[1, :half], got_low).astype(BF16)
@@ -63,10 +63,15 @@
     down_high = plus(mine[2, half:], swapped[2, half:], got_high).astype(BF16)
     from_below = lax.ppermute(jnp.concatenate([up_low, up_high]), "y", UP)
     from_above = lax.ppermute(jnp.concatenate([down_low, down_high]), "y", DOWN)
-    return plus(mine[0], swapped[0], from_below, from_above).astype(BF16)
-
-
-def fill_rows(step, refs, rows_ref):
+    total = plus(mine[0], swapped[0], from_below, from_above).astype(BF16)
+    return total, parts, (from_below, total)
+
+
+def after(value, *others):
+    return lax.optimization_barrier((value,) + others)[0]
+
+
+def fill_from_pieces(step, refs, rows_ref):
     half_steps = HALF // GROUP // 2
     for core in range(2):
         own, above, below, far_low, far_high = refs[core * 5 : core * 5 + 5]
@@ -91,21 +96,34 @@
             put(3, far_high)
 
 
-def attention_kernel(first, count_ref, *refs):
-    pieces = refs[:10]
-    key_weight_ref, value_weight_ref, query_ref, grad_ref = refs[10:14]
+def fill_from_gathered(order_ref, gathered_ref, rows_ref):
+    for piece in range(PIECES):
+        source = order_ref[piece]
+        for c in range(GROUP):
+            at = c * SPAN + piece * KNB * ROWS
+            rows_ref[at : at + KNB * ROWS, :] = gathered_ref[
+                source, c * KNB : (c + 1) * KNB
+            ].reshape(KNB * ROWS, gathered_ref.shape[3])
+
+
+def attention_kernel(first, count_ref, order_ref, *refs):
+    step = pl.program_id(0)
     if first:
-        begun_ref, rest = None, refs[14:]
+        pieces, refs = refs[:10], refs[10:]
     else:
-        begun_ref, rest = refs[14], refs[15:]
-    attended_ref, grad_query_ref, mine_ref, other_ref, out_ref = rest[:5]
-    rows_ref, kv_ref, both_ref = rest[5:8]
-    total_ref = out_ref if first else rest[8]
-    step = pl.program_id(0)
+        gathered_ref, begun_ref, refs = refs[0], refs[1], refs[2:]
+    key_weight_ref, value_weight_ref, query_ref, grad_ref, attended_ref, grad_query_ref = refs[:6]
+    refs = refs[6:]
+    if first:
+        share_ref, out_ref, rows_ref, kv_ref, both_ref = refs
+        total_ref = out_ref
+        fill_from_pieces(step, pieces, rows_ref)
+    else:
+        mine_ref, other_ref, out_ref, rows_ref, kv_ref, both_ref, total_ref = refs
+        fill_from_gathered(order_ref, gathered_ref, rows_ref)
     local = key_weight_ref.shape[1]
     factor = 1.0 / math.sqrt(DH)
     key_cols, value_cols = slice(0, local), slice(local, 2 * local)
-    fill_rows(step, pieces, rows_ref)
     head_of = lax.broadcasted_iota(jnp.int32, (STRETCH, local), 1) < DH
     neighbour = (lax.broadcasted_iota(jnp.int32, (SPAN, 1), 0) // ROWS) % KNB
 
@@ -154,11 +172,15 @@
         share = share + dot(both_ref[rows, value_cols], value_weight_ref[...], 1, 1)
         share = share.astype(BF16)
         for piece in range(PIECES):
-            ref = mine_ref if piece < 4 else other_ref
             at = piece * KNB * ROWS
-            ref[piece % 4, c * KNB : (c + 1) * KNB] = share[at : at + KNB * ROWS].reshape(
-                KNB, ROWS, share.shape[1]
-            )
+            part = share[at : at + KNB * ROWS].reshape(KNB, ROWS, share.shape[1])
+            panels = slice(c * KNB, (c + 1) * KNB)
+            if first:
+                share_ref[order_ref[piece], panels] = part
+            elif piece < 4:
+                mine_ref[piece, panels] = part
+            else:
+                other_ref[piece - 4, panels] = part
     part = dot(rows_ref[...], both_ref[...], 0, 0)
 
     @pl.when(step == 0)
@@ -177,10 +199,9 @@
                 out_ref[g] = total_ref[:, g * DH : (g + 1) * DH].astype(BF16)
 
 
-def attention(counts, pieces, w_key, w_value, queries, out_grad, half, begun):
+def attention(counts, order, panels, w_key, w_value, queries, out_grad, half, begun):
     width, local = w_key.shape
     tokens = HALF * STRETCH
-    panels = HALF * KNB
     steps = HALF // GROUP
     half_steps = steps // 2
     first = begun is None
@@ -188,37 +209,44 @@
     plain = pl.BlockSpec(block, lambda i, *_: (i, 0, 0))
     low = pl.BlockSpec(block, lambda i, *_: (jnp.minimum(i, half_steps - 1), 0, 0))
     high = pl.BlockSpec(block, lambda i, *_: (jnp.maximum(i - half_steps, 0), 0, 0))
+    stacked = lambda n: pl.BlockSpec((n,) + block, lambda i, *_: (0, i, 0, 0))
+    stacked_shape = lambda n: jax.ShapeDtypeStruct((n, HALF * KNB, ROWS, width), BF16)
     token_in = pl.BlockSpec((GROUP * STRETCH, local), lambda i, *_: (i + half * steps, 0))
     token_out = pl.BlockSpec((GROUP * STRETCH, local), lambda i, *_: (i, 0))
-    share = pl.BlockSpec((4, GROUP * KNB, ROWS, width), lambda i, *_: (0, i, 0, 0))
+    token_shape = jax.ShapeDtypeStruct((tokens, local), BF16)
     whole = lambda shape: pl.BlockSpec(shape, lambda i, *_: (0,) * len(shape))
     total = (width, 2 * local)
-    out = jax.ShapeDtypeStruct(total, F32) if first else jax.ShapeDtypeStruct((4, width, DH), BF16)
-    token_shape = jax.ShapeDtypeStruct((tokens, local), BF16)
-    share_shape = jax.ShapeDtypeStruct((4, panels, ROWS, width), BF16)
     scratch = [
         pltpu.VMEM((GROUP * SPAN, width), BF16),
         pltpu.VMEM((GROUP * SPAN, 2 * local), BF16),
         pltpu.VMEM((GROUP * SPAN, 2 * local), BF16),
     ]
+    if first:
+        in_specs = [plain, plain, plain, low, high] * 2
+        share_specs, share_shapes = [stacked(PIECES)], [stacked_shape(PIECES)]
+        out = jax.ShapeDtypeStruct(total, F32)
+    else:
+        in_specs = [stacked(PIECES), whole(total)]
+        panels = [panels, begun]
+        share_specs, share_shapes = [stacked(4)] * 2, [stacked_shape(4)] * 2
+        out = jax.ShapeDtypeStruct((4, width, DH), BF16)
+        scratch = scratch + [pltpu.VMEM(total, F32)]
     return pl.pallas_call(
         functools.partial(attention_kernel, first),
         grid_spec=pltpu.PrefetchScalarGridSpec(
-            num_scalar_prefetch=1,
+            num_scalar_prefetch=2,
             grid=(steps,),
-            in_specs=[plain, plain, plain, low, high] * 2
-            + [whole(w_key.shape), whole(w_key.shape), token_in, token_in]
-            + ([] if first else [whole(total)]),
-            out_specs=[token_out, token_out, share, share, whole(out.shape)],
-            scratch_shapes=scratch + ([] if first else [pltpu.VMEM(total, F32)]),
-        ),
-        out_shape=[token_shape, token_shape, share_shape, share_shape, out],
+            in_specs=in_specs + [whole(w_key.shape), whole(w_key.shape), token_in, token_in],
+            out_specs=[token_out, token_out] + share_specs + [whole(out.shape)],
+            scratch_shapes=scratch,
+        ),
+        out_shape=[token_shape, token_shape] + share_shapes + [out],
         compiler_params=pltpu.CompilerParams(vmem_limit_bytes=56 * 2**20),
         cost_estimate=pl.CostEstimate(
             flops=8 * 2**30, bytes_accessed=16 * 2**20, transcendentals=2**18
         ),
         name="attention",
-    )(counts, *pieces, w_key, w_value, queries, out_grad, *([] if first else [begun]))
+    )(counts, order, *panels, w_key, w_value, queries, out_grad)
 
 
 def collect_kernel(slot_ref, filled_ref, arrived_ref, out_ref):
@@ -250,14 +278,18 @@
     )(slots, filled, arrived)
 
 
-def reduce_weight_grads(parts):
+def reduce_weight_grads(parts, stages):
     width = parts.shape[1]
     by_x = lax.all_to_all(parts, "x", split_axis=0, concat_axis=0, tiled=True)
     part = plus(*[by_x[k] for k in range(4)]).astype(BF16).reshape(8, width // 8, DH)
     by_z = lax.all_to_all(part, "z", split_axis=0, concat_axis=0, tiled=True)
-    total = plus(*[by_z[k] for k in range(8)])
-    column = lax.all_gather(total, "z", axis=0, tiled=True)
-    groups = lax.all_gather(column, "x", axis=0, tiled=False)
+    by_z = after(by_z, stages[0])
+    total = plus(*[by_z[k] for k in range(8)]).astype(BF16)
+    column = jnp.broadcast_to(total[None], part.shape)
+    column = lax.all_to_all(column, "z", split_axis=0, concat_axis=0, tiled=True)
+    column = after(column, stages[1])
+    groups = jnp.broadcast_to(column.reshape(width, DH)[None], parts.shape)
+    groups = lax.all_to_all(groups, "x", split_axis=0, concat_axis=0, tiled=True).astype(F32)
     return (
         jnp.concatenate([groups[0], groups[1]], axis=1),
         jnp.concatenate([groups[2], groups[3]], axis=1),
@@ -296,32 +328,29 @@
     take = lambda array, index: jnp.take(array, index, axis=0, mode="clip")
 
     incoming = exchange(take(pool, picked_slot))
-    begun, attended, grad_queries, summed = None, [], [], []
+    y, core = lax.axis_index("y"), lax.axis_index("core")
+    order = jnp.stack(
+        [(y + dy) % 4 * 2 + (core + other) % 2 for other in (0, 1) for dy in (0, 1, 3, 2)]
+    ).astype(jnp.int32)
     panels = HALF * KNB
-    pieces = [
-        gather_pieces(take(incoming, positions[half * panels : (half + 1) * panels]))
-        for half in range(2)
-    ]
-    for half in range(2):
-        attended_half, grad_half, mine, other, begun = attention(
-            counts[half * HALF : (half + 1) * HALF],
-            pieces[half],
-            w_key,
-            w_value,
-            queries,
-            out_grad,
-            half,
-            begun,
-        )
-        attended.append(attended_half)
-        grad_queries.append(grad_half)
-        summed.append(scatter_pieces(mine, other))
-    grad_w_key, grad_w_value = reduce_weight_grads(begun)
-    arrived = exchange(take(jnp.concatenate(summed), back))
+    wanted = take(incoming, positions)
+    pieces = gather_pieces(wanted[:panels])
+    gathered = lax.all_gather(wanted[panels:], ("y", "core"), axis=0)
+    weights = (w_key, w_value, queries, out_grad)
+    attended_0, grad_queries_0, share, begun = attention(
+        counts[:HALF], order, pieces, *weights, 0, None
+    )
+    summed_0 = lax.psum_scatter(share, ("y", "core"), scatter_dimension=0)
+    attended_1, grad_queries_1, mine, other, parts = attention(
+        counts[HALF:], order, gathered, *weights, 1, begun
+    )
+    summed_1, parts, stages = scatter_pieces(mine, other, parts)
+    grad_w_key, grad_w_value = reduce_weight_grads(parts, stages)
+    arrived = exchange(take(jnp.concatenate([summed_0, summed_1]), back))
     grad_pool = collect(picked_slot, filled, arrived, pool.shape[0])
     return (
-        jnp.concatenate(attended),
-        jnp.concatenate(grad_queries),
+        jnp.concatenate([attended_0, attended_1]),
+        jnp.concatenate([grad_queries_0, grad_queries_1]),
         grad_pool,
         grad_w_key,
         grad_w_value,

time: 293 us -> 260 us (0.89)
  blocking collectives: 61.7 us -> 0 us
  waiting for transfers between devices: 104 us -> 137 us
  other arithmetic: 17.2 us -> 13 us
  local copies, waits for them, and re-layouts: 14.9 us -> 18.2 us
    all_gather x1 -> x0, blocking collectives: 61.7 us -> none  [reduce_weight_grads(): column = lax.all_gather(total, 'z', axis=0, tiled=True)]
    all_to_all x2, waiting for transfers between devices: 44.5 us -> 79.1 us  [exchange(): lax.all_to_all(array, ('z', 'x'), split_axis=0, concat_axis=0, tiled=True)]
    all_gather x1, waiting for transfers between devices: 29.1 us -> 0.02 us  [local(): gathered = lax.all_gather(wanted[panels:], ('y', 'core'), axis=0)]
    all_to_all x0 -> x2, waiting for transfers between devices: none -> 15.5 us  [the longest x1 8.5 us: reduce_weight_grads(): lax.all_to_all(column, 'z', split_axis=0, concat_axis=0, tiled=True)]
    all_to_all x0 -> x2, starting transfers between devices: none -> 8.01 us  [the longest x1 4.61 us: reduce_weight_grads(): lax.all_to_all(groups, 'x', split_axis=0, concat_axis=0, tiled=True)]
    ppermute x2 -> x1, waiting for transfers between devices: 0.01 us -> 7.06 us  [scatter_pieces(): got_low = lax.ppermute(far[:half], 'y', UP)]
    ppermute x2 -> x1, waiting for transfers between devices: 5.58 us -> 0.01 us  [scatter_pieces(): from_above = lax.ppermute(jnp.concatenate([down_low, down_high]), 'y', DOWN)]
    ppermute x2 -> x1, waiting for transfers between devices: 14 us -> 8.5 us  [gather_pieces(): below = lax.ppermute(own, 'y', UP)]
  transfers between devices with their start and end apart: 33 -> 22, of which waited for: 13 -> 12; matrix products, arithmetic and copies ran while one was open for 8% -> 8% of each run, Pallas kernels for 5% -> 11%
where the time goes in v2:
time: 260 us; the launch traced here: 259 us
  waiting for transfers between devices  137 us (53%)
  starting transfers between devices  45.7 us (18%)
  Pallas kernels  30.4 us (12%)
  local copies, waits for them, and re-layouts  18.2 us (7%)
  between operations  14.4 us (6%)
  other arithmetic  13 us (5%)
    all_to_all x2, waiting for transfers between devices, exchange(): lax.all_to_all(array, ('z', 'x'), split_axis=0, concat_axis=0, tiled=True)  79.1 us
    pallas_call x2, Pallas kernels, attention(): pl.pallas_call(functools.partial(attention_kernel, first), grid_spec=pltp...  27.3 us
    all_to_all x2, starting transfers between devices, exchange(): lax.all_to_all(array, ('z', 'x'), split_axis=0, concat_axis=0, tiled=True)  15.3 us
    ppermute x1, waiting for transfers between devices, gather_pieces(): far_low = lax.ppermute(below[:half], 'y', UP)  8.89 us
    ppermute x1, waiting for transfers between devices, gather_pieces(): below = lax.ppermute(own, 'y', UP)  8.5 us
    all_to_all x1, waiting for transfers between devices, reduce_weight_grads(): lax.all_to_all(column, 'z', split_axis=0, concat_axis=0, tiled=True)  8.5 us
    all_to_all x1, starting transfers between devices, reduce_weight_grads(): by_x = lax.all_to_all(parts, 'x', split_axis=0, concat_axis=0, tiled=True)  8.23 us
    ppermute x1, waiting for transfers between devices, scatter_pieces(): got_low = lax.ppermute(far[:half], 'y', UP)  7.06 us
  transfers between devices with their start and end apart: 22, of which 12 were waited for; matrix products, arithmetic and copies ran while one was open for 8% of the time, Pallas kernels for 11%

profile of v2, /device:TPU:8, one launch (start us, length us, event | category | flops | bytes accessed | tf_op | source)
XLA Modules:
  0.0 258.6 jit_solution(14946607832513677708)
XLA Ops:
  7.2 0.9 copy.17
  8.3 0.8 convert_reduce_fusion
  9.1 0.8 copy.18
  10.4 2.0 gather_fusion
  12.4 11.3 %all-to-all-start = ((bf16[64,16,896]{2,1,0:T(8,128)(2,1)}), bf16[64,16,896]{2,1,0:T(8,128)(2,1)S(1)}, u32[]{:S(2)}, u32[]{:S(2)}) async-start(bf16[64,16,896]{2,1,0:T(8,128)(2,1)} %gather_fusion), calls=%async_computation | async-start | bytes 3670016 | tf_op jit(solution)/shard_map/all_to_all | solution.py:300
  23.8 44.5 %all-to-all-done = bf16[64,16,896]{2,1,0:T(8,128)(2,1)S(1)} async-done(((bf16[64,16,896]{2,1,0:T(8,128)(2,1)}), bf16[64,16,896]{2,1,0:T(8,128)(2,1)S(1)}, u32[]{:S(2)}, u32[]{:S(2)}) %all-to-all-start) | async-done | bytes 1835040 | tf_op jit(solution)/shard_map/all_to_all | solution.py:300
  68.4 1.6 gather_fusion.1
  69.9 2.0 fusion.10
  72.0 1.7 collective-permute-start.1
  74.1 8.5 %collective-permute-done.1.refs_2_ = bf16[16,16,896]{2,1,0:T(8,128)(2,1)S(1)} collective-permute-done((bf16[16,16,896]{2,1,0:T(8,128)(2,1)S(1)}, bf16[16,16,896]{2,1,0:T(8,128)(2,1)S(1)}, u32[]{:S(2)}, u32[]{:S(2)}) %collective-permute-start.1) | collective-permute-done | bytes 458784 | tf_op jit(solution)/shard_map/ppermute | solution.py:39
  82.6 1.7 collective-permute-start.2
  85.4 8.9 %collective-permute-done.2.refs_3_ = bf16[8,16,896]{2,1,0:T(8,128)(2,1)S(1)} collective-permute-done((bf16[8,16,896]{2,1,0:T(8,128)(2,1)S(1)}, bf16[8,16,896]{2,1,0:T(8,128)(2,1)S(1)}, u32[]{:S(2)}, u32[]{:S(2)}) %collective-permute-start.2) | collective-permute-done | bytes 229408 | tf_op jit(solution)/shard_map/ppermute | solution.py:41
  94.2 1.7 collective-permute-done.3.refs_4_
  96.0 0.8 dynamic_slice.10
  98.0 0.7 copy-done.11
  98.8 13.8 %attention.2 = (bf16[512,256]{1,0:T(8,128)(2,1)}, bf16[512,256]{1,0:T(8,128)(2,1)}, bf16[8,16,16,896]{3,2,1,0:T(8,128)(2,1)}, f32[896,512]{1,0:T(8,128)}) custom-call(s32[8]{0:T(128)} %get-tuple-element.43.count_ref, s32[8]{0:T(128)} %stack.35.order_ref, bf16[16,16,896]{2,1,0:T(8,128)(2,1)} %copy-done.4, bf16[16,16,896]{2,1,0:T(8,128)(2,1)} %copy-done.10, ...), custom_call_target="tpu_custom_call" | custom-call | flops 8589934592 | bytes 16777216 | tf_op jit(solution)/shard_map/attention/pallas_call | solution.py:234
  112.7 13.5 %attention.3 = (bf16[512,256]{1,0:T(8,128)(2,1)}, bf16[512,256]{1,0:T(8,128)(2,1)}, bf16[4,16,16,896]{3,2,1,0:T(8,128)(2,1)}, bf16[4,16,16,896]{3,2,1,0:T(8,128)(2,1)}, bf16[4,896,128]{2,1,0:T(8,128)(2,1)}) custom-call(s32[8]{0:T(128)} %get-tuple-element.44.count_ref, s32[8]{0:T(128)} %stack.35.order_ref, bf16[8,16,16,896]{3,2,1,0:T(8,128)(2,1)} %bitcast.46, ...), custom_call_target="tpu_custom_call" | custom-call | flops 8589934592 | bytes 16777216 | tf_op jit(solution)/shard_map/attention/pallas_call | solution.py:234
  126.8 3.6 %collective-permute-done.9 = bf16[4,16,16,896]{3,2,1,0:T(8,128)(2,1)S(1)} collective-permute-done((bf16[4,16,16,896]{3,2,1,0:T(8,128)(2,1)}, bf16[4,16,16,896]{3,2,1,0:T(8,128)(2,1)S(1)}, u32[]{:S(2)}, u32[]{:S(2)}) %collective-permute-start.9) | collective-permute-done | bytes 1835040 | tf_op jit(solution)/shard_map/ppermute | solution.py:55
  130.4 1.2 copy-done.3
  131.6 1.1 fusion.2
  132.8 8.2 %all-to-all-start.2 = ((bf16[4,896,128]{2,1,0:T(8,128)(2,1)}), bf16[4,896,128]{2,1,0:T(8,128)(2,1)S(1)}, u32[]{:S(2)}, u32[]{:S(2)}) async-start(bf16[4,896,128]{2,1,0:T(8,128)(2,1)} %get-tuple-element.28), calls=%async_computation.3 | async-start | bytes 1835008 | tf_op jit(solution)/shard_map/all_to_all | solution.py:283
  141.0 2.5 collective-permute-start.10
  143.9 1.4 fusion.5
  145.3 7.1 %collective-permute-done.10 = bf16[8,16,896]{2,1,0:T(8,128)(2,1)S(1)} collective-permute-done((bf16[8,16,896]{2,1,0:T(8,128)(2,1)S(1)}, bf16[8,16,896]{2,1,0:T(8,128)(2,1)S(1)}, u32[]{:S(2)}, u32[]{:S(2)}) %collective-permute-start.10) | collective-permute-done | bytes 229408 | tf_op jit(solution)/shard_map/ppermute | solution.py:58
  152.3 2.4 collective-permute-done.12
  154.8 1.5 fusion.4
  156.3 1.8 collective-permute-start.11
  158.1 0.8 add_convert_fusion.1
  158.9 3.6 %all-to-all-start.3 = ((bf16[8,112,128]{2,1,0:T(8,128)(2,1)}), bf16[8,112,128]{2,1,0:T(8,128)(2,1)S(1)}, u32[]{:S(2)}, u32[]{:S(2)}) async-start(bf16[8,112,128]{2,1,0:T(8,128)(2,1)} %bitcast.17), calls=%async_computation.4 | async-start | bytes 458752 | tf_op jit(solution)/shard_map/all_to_all | solution.py:285
  163.0 5.2 %collective-permute-done.11 = bf16[16,16,896]{2,1,0:T(8,128)(2,1)} collective-permute-done((bf16[16,16,896]{2,1,0:T(8,128)(2,1)S(1)}, bf16[16,16,896]{2,1,0:T(8,128)(2,1)}, u32[]{:S(2)}, u32[]{:S(2)}) %collective-permute-start.11) | collective-permute-done | bytes 458784 | tf_op jit(solution)/shard_map/ppermute | solution.py:64
  168.2 4.7 %all-to-all-done.3 = bf16[8,112,128]{2,1,0:T(8,128)(2,1)S(1)} async-done(((bf16[8,112,128]{2,1,0:T(8,128)(2,1)}), bf16[8,112,128]{2,1,0:T(8,128)(2,1)S(1)}, u32[]{:S(2)}, u32[]{:S(2)}) %all-to-all-start.3) | async-done | bytes 229408 | tf_op jit(solution)/shard_map/all_to_all | solution.py:285
  172.9 0.7 broadcast_in_dim.67
  173.6 3.4 %all-to-all-start.4 = ((bf16[8,112,128]{2,1,0:T(8,128)(2,1)}), bf16[8,112,128]{2,1,0:T(8,128)(2,1)S(1)}, u32[]{:S(2)}, u32[]{:S(2)}) async-start(bf16[8,112,128]{2,1,0:T(8,128)(2,1)} %broadcast_in_dim.67), calls=%async_computation.5 | async-start | bytes 458752 | tf_op jit(solution)/shard_map/all_to_all | solution.py:289
  177.1 1.5 fusion.1
  178.6 8.5 %all-to-all-done.4 = bf16[8,112,128]{2,1,0:T(8,128)(2,1)S(1)} async-done(((bf16[8,112,128]{2,1,0:T(8,128)(2,1)}), bf16[8,112,128]{2,1,0:T(8,128)(2,1)S(1)}, u32[]{:S(2)}, u32[]{:S(2)}) %all-to-all-start.4) | async-done | bytes 229408 | tf_op jit(solution)/shard_map/all_to_all | solution.py:289
  187.1 1.0 broadcast_in_dim.69
  188.1 4.6 %all-to-all-start.5 = ((bf16[4,896,128]{2,1,0:T(8,128)(2,1)}), bf16[4,896,128]{2,1,0:T(8,128)(2,1)S(1)}, u32[]{:S(2)}, u32[]{:S(2)}) async-start(bf16[4,896,128]{2,1,0:T(8,128)(2,1)} %broadcast_in_dim.69), calls=%async_computation.6 | async-start | bytes 1835008 | tf_op jit(solution)/shard_map/all_to_all | solution.py:292
  192.9 1.1 pad_maximum_fusion
  194.0 2.0 gather_fusion.2
  196.0 7.0 %all-to-all-done.5 = bf16[4,896,128]{2,1,0:T(8,128)(2,1)S(1)} async-done(((bf16[4,896,128]{2,1,0:T(8,128)(2,1)}), bf16[4,896,128]{2,1,0:T(8,128)(2,1)S(1)}, u32[]{:S(2)}, u32[]{:S(2)}) %all-to-all-start.5) | async-done | bytes 917536 | tf_op jit(solution)/shard_map/all_to_all | solution.py:292
  203.0 0.9 copy-done.1
  203.9 4.0 %all-to-all-start.1 = ((bf16[64,16,896]{2,1,0:T(8,128)(2,1)}), bf16[64,16,896]{2,1,0:T(8,128)(2,1)S(1)}, u32[]{:S(2)}, u32[]{:S(2)}) async-start(bf16[64,16,896]{2,1,0:T(8,128)(2,1)} %gather_fusion.2), calls=%async_computation.2 | async-start | bytes 3670016 | tf_op jit(solution)/shard_map/all_to_all | solution.py:300
  208.0 0.8 fusion.8
  209.5 0.8 reshape.101.filled_ref
  210.4 2.1 pad_maximum_fusion.3
  212.7 1.3 pad_maximum_fusion.1
  214.0 34.5 %all-to-all-done.1.arrived_ref = bf16[64,16,896]{2,1,0:T(8,128)(2,1)S(1)} async-done(((bf16[64,16,896]{2,1,0:T(8,128)(2,1)}), bf16[64,16,896]{2,1,0:T(8,128)(2,1)S(1)}, u32[]{:S(2)}, u32[]{:S(2)}) %all-to-all-start.1) | async-done | bytes 1835040 | tf_op jit(solution)/shard_map/all_to_all | solution.py:300
  248.6 3.2 %collect.1 = f32[32,16,896]{2,1,0:T(8,128)} custom-call(s32[64]{0:T(128)S(1)} %reshape.104.slot_ref, s32[64]{0:T(128)S(1)} %reshape.101.filled_ref, bf16[64,16,896]{2,1,0:T(8,128)(2,1)S(1)} %all-to-all-done.1.arrived_ref), custom_call_target="tpu_custom_call" | custom-call | tf_op jit(solution)/shard_map/collect/pallas_call | solution.py:267
  (75 shorter events, 6.1 us)
Async XLA Ops:
  7.2 3.2 %copy-start = (bf16[32,16,896]{2,1,0:T(8,128)(2,1)S(1)}, bf16[32,16,896]{2,1,0:T(8,128)(2,1)}, u32[]{:S(2)}) copy-start(bf16[32,16,896]{2,1,0:T(8,128)(2,1)} %param.9) | copy-start | bytes 2752516
  9.1 14.7 %copy-start.8 = (s32[32,32]{1,0:T(8,128)}, s32[32,32]{1,0:T(8,128)S(1)}, u32[]{:S(2)}) copy-start(s32[32,32]{1,0:T(8,128)S(1)} %convert_reduce_fusion) | copy-start | bytes 12292
  12.4 56.0 %all-to-all-start = ((bf16[64,16,896]{2,1,0:T(8,128)(2,1)}), bf16[64,16,896]{2,1,0:T(8,128)(2,1)S(1)}, u32[]{:S(2)}, u32[]{:S(2)}) async-start(bf16[64,16,896]{2,1,0:T(8,128)(2,1)} %gather_fusion), calls=%async_computation | async-start | bytes 3670016 | tf_op jit(solution)/shard_map/all_to_all | solution.py:300
  23.7 89.0 %all-gather.3.cloned.1.call-start = ((), (), s32[]{:S(2)}) async-start(), calls=%async_computation.8 | async-start | bytes 4128768 | tf_op jit(solution)/shard_map/all_gather | solution.py:338
  71.9 26.0 %copy-start.4 = (bf16[16,16,896]{2,1,0:T(8,128)(2,1)}, bf16[16,16,896]{2,1,0:T(8,128)(2,1)S(1)}, u32[]{:S(2)}) copy-start(bf16[16,16,896]{2,1,0:T(8,128)(2,1)S(1)} %get-tuple-element.39.refs_0_) | copy-start | bytes 1376260
  71.9 120.9 %reduce-scatter.2.cloned.1.call-start = ((), (), s32[]{:S(2)}) async-start(), calls=%async_computation.7 | async-start | bytes 4128768 | tf_op jit(solution)/shard_map/reduce_scatter | solution.py:343
  72.0 10.6 %collective-permute-start.1 = (bf16[16,16,896]{2,1,0:T(8,128)(2,1)S(1)}, bf16[16,16,896]{2,1,0:T(8,128)(2,1)S(1)}, u32[]{:S(2)}, u32[]{:S(2)}) collective-permute-start(bf16[16,16,896]{2,1,0:T(8,128)(2,1)S(1)} %get-tuple-element.39.refs_0_), channel_id=1, source_target_pairs={{0,2},{2,4},{4,6},{6,0},{1,3},{3,5},{5,7},{7,1},{8,10},{10,12},{12... | collective-permute-start | bytes 1376264 | tf_op jit(solution)/shard_map/ppermute | solution.py:39
  73.6 10.7 %collective-permute-start = (bf16[16,16,896]{2,1,0:T(8,128)(2,1)S(1)}, bf16[16,16,896]{2,1,0:T(8,128)(2,1)S(1)}, u32[]{:S(2)}, u32[]{:S(2)}) collective-permute-start(bf16[16,16,896]{2,1,0:T(8,128)(2,1)S(1)} %get-tuple-element.39.refs_0_), channel_id=1, source_target_pairs={{2,0},{4,2},{6,4},{0,6},{3,1},{5,3},{7,5},{1,7},{10,8},{12,10},{14... | collective-permute-start | bytes 1376264 | tf_op jit(solution)/shard_map/ppermute | solution.py:40
  74.1 23.8 %collective-permute-start.4 = (bf16[16,16,896]{2,1,0:T(8,128)(2,1)S(1)}, bf16[16,16,896]{2,1,0:T(8,128)(2,1)S(1)}, u32[]{:S(2)}, u32[]{:S(2)}) collective-permute-start(bf16[16,16,896]{2,1,0:T(8,128)(2,1)S(1)} %get-tuple-element.39.refs_0_), channel_id=1, source_target_pairs={{0,1},{1,0},{2,3},{3,2},{4,5},{5,4},{6,7},{7,6},{8,9},{9,8},{10,11... | collective-permute-start | bytes 1376264 | tf_op jit(solution)/shard_map/ppermute | solution.py:44
  82.6 15.4 %copy-start.9 = (bf16[16,16,896]{2,1,0:T(8,128)(2,1)}, bf16[16,16,896]{2,1,0:T(8,128)(2,1)S(1)}, u32[]{:S(2)}) copy-start(bf16[16,16,896]{2,1,0:T(8,128)(2,1)S(1)} %collective-permute-done.1.refs_2_) | copy-start | bytes 1376260
  82.6 11.6 %collective-permute-start.2 = (bf16[8,16,896]{2,1,0:T(8,128)(2,1)S(1)}, bf16[8,16,896]{2,1,0:T(8,128)(2,1)S(1)}, u32[]{:S(2)}, u32[]{:S(2)}) collective-permute-start(bf16[8,16,896]{2,1,0:T(8,128)(2,1)S(1)} %slice.151), channel_id=1, source_target_pairs={{0,2},{2,4},{4,6},{6,0},{1,3},{3,5},{5,7},{7,1},{8,10},{10,12},{12... | collective-permute-start | bytes 688136 | tf_op jit(solution)/shard_map/ppermute | solution.py:41
  84.3 13.6 %copy-start.10 = (bf16[16,16,896]{2,1,0:T(8,128)(2,1)}, bf16[16,16,896]{2,1,0:T(8,128)(2,1)S(1)}, u32[]{:S(2)}) copy-start(bf16[16,16,896]{2,1,0:T(8,128)(2,1)S(1)} %collective-permute-done.refs_1_) | copy-start | bytes 1376260
  84.4 11.6 %collective-permute-start.3 = (bf16[8,16,896]{2,1,0:T(8,128)(2,1)S(1)}, bf16[8,16,896]{2,1,0:T(8,128)(2,1)}, u32[]{:S(2)}, u32[]{:S(2)}) collective-permute-start(bf16[8,16,896]{2,1,0:T(8,128)(2,1)S(1)} %slice.152), channel_id=1, source_target_pairs={{2,0},{4,2},{6,4},{0,6},{3,1},{5,3},{7,5},{1,7},{10,8},{12,10},{14... | collective-permute-start | bytes 688136 | tf_op jit(solution)/shard_map/ppermute | solution.py:42
  84.8 13.1 %collective-permute-start.6 = (bf16[16,16,896]{2,1,0:T(8,128)(2,1)S(1)}, bf16[16,16,896]{2,1,0:T(8,128)(2,1)}, u32[]{:S(2)}, u32[]{:S(2)}) collective-permute-start(bf16[16,16,896]{2,1,0:T(8,128)(2,1)S(1)} %collective-permute-done.1.refs_2_), channel_id=1, source_target_pairs={{0,1},{1,0},{2,3},{3,2},{4,5},{5,4},{6,7},{7,6},{8,9},{9,8},{10,11... | collective-permute-start | bytes 1376264 | tf_op jit(solution)/shard_map/ppermute | solution.py:44
  84.8 13.1 %collective-permute-start.5 = (bf16[16,16,896]{2,1,0:T(8,128)(2,1)S(1)}, bf16[16,16,896]{2,1,0:T(8,128)(2,1)}, u32[]{:S(2)}, u32[]{:S(2)}) collective-permute-start(bf16[16,16,896]{2,1,0:T(8,128)(2,1)S(1)} %collective-permute-done.refs_1_), channel_id=1, source_target_pairs={{0,1},{1,0},{2,3},{3,2},{4,5},{5,4},{6,7},{7,6},{8,9},{9,8},{10,11... | collective-permute-start | bytes 1376264 | tf_op jit(solution)/shard_map/ppermute | solution.py:44
  94.2 3.7 %copy-start.12 = (bf16[8,16,896]{2,1,0:T(8,128)(2,1)}, bf16[8,16,896]{2,1,0:T(8,128)(2,1)S(1)}, u32[]{:S(2)}) copy-start(bf16[8,16,896]{2,1,0:T(8,128)(2,1)S(1)} %collective-permute-done.2.refs_3_) | copy-start | bytes 688132
  94.2 3.7 %collective-permute-start.7 = (bf16[8,16,896]{2,1,0:T(8,128)(2,1)S(1)}, bf16[8,16,896]{2,1,0:T(8,128)(2,1)S(1)}, u32[]{:S(2)}, u32[]{:S(2)}) collective-permute-start(bf16[8,16,896]{2,1,0:T(8,128)(2,1)S(1)} %collective-permute-done.2.refs_3_), channel_id=1, source_target_pairs={{0,1},{1,0},{2,3},{3,2},{4,5},{5,4},{6,7},{7,6},{8,9},{9,8},{10,11... | collective-permute-start | bytes 688136 | tf_op jit(solution)/shard_map/ppermute | solution.py:44
  96.0 2.0 collective-permute-start.8
  97.9 0.8 copy-start.11
  97.9 0.9 copy-start.13
  97.9 0.9 copy-start.14
  126.2 4.2 %collective-permute-start.9 = (bf16[4,16,16,896]{3,2,1,0:T(8,128)(2,1)}, bf16[4,16,16,896]{3,2,1,0:T(8,128)(2,1)S(1)}, u32[]{:S(2)}, u32[]{:S(2)}) collective-permute-start(bf16[4,16,16,896]{3,2,1,0:T(8,128)(2,1)} %get-tuple-element.25), channel_id=1, source_target_pairs={{0,1},{1,0},{2,3},{3,2},{4,5},{5,4},{6,7},{7,6},{8,9},{9,8},{10,11... | collective-permute-start | bytes 5505032 | tf_op jit(solution)/shard_map/ppermute | solution.py:55
  130.4 1.2 copy-start.3
  132.8 25.3 %all-to-all-start.2 = ((bf16[4,896,128]{2,1,0:T(8,128)(2,1)}), bf16[4,896,128]{2,1,0:T(8,128)(2,1)S(1)}, u32[]{:S(2)}, u32[]{:S(2)}) async-start(bf16[4,896,128]{2,1,0:T(8,128)(2,1)} %get-tuple-element.28), calls=%async_computation.3 | async-start | bytes 1835008 | tf_op jit(solution)/shard_map/all_to_all | solution.py:283
  141.0 11.3 %collective-permute-start.10 = (bf16[8,16,896]{2,1,0:T(8,128)(2,1)S(1)}, bf16[8,16,896]{2,1,0:T(8,128)(2,1)S(1)}, u32[]{:S(2)}, u32[]{:S(2)}) collective-permute-start(bf16[8,16,896]{2,1,0:T(8,128)(2,1)S(1)} %get-tuple-element.41), channel_id=1, source_target_pairs={{0,2},{2,4},{4,6},{6,0},{1,3},{3,5},{5,7},{7,1},{8,10},{10,12},{12... | collective-permute-start | bytes 688136 | tf_op jit(solution)/shard_map/ppermute | solution.py:58
  143.6 11.2 %collective-permute-start.12 = (bf16[8,16,896]{2,1,0:T(8,128)(2,1)S(1)}, bf16[8,16,896]{2,1,0:T(8,128)(2,1)S(1)}, u32[]{:S(2)}, u32[]{:S(2)}) collective-permute-start(bf16[8,16,896]{2,1,0:T(8,128)(2,1)S(1)} %get-tuple-element.42), channel_id=1, source_target_pairs={{2,0},{4,2},{6,4},{0,6},{3,1},{5,3},{7,5},{1,7},{10,8},{12,10},{14... | collective-permute-start | bytes 688136 | tf_op jit(solution)/shard_map/ppermute | solution.py:59
  156.3 11.9 %collective-permute-start.11 = (bf16[16,16,896]{2,1,0:T(8,128)(2,1)S(1)}, bf16[16,16,896]{2,1,0:T(8,128)(2,1)}, u32[]{:S(2)}, u32[]{:S(2)}) collective-permute-start(bf16[16,16,896]{2,1,0:T(8,128)(2,1)S(1)} %pad_maximum_fusion.5), channel_id=1, source_target_pairs={{0,2},{2,4},{4,6},{6,0},{1,3},{3,5},{5,7},{7,1},{8,10},{10,12},{12... | collective-permute-start | bytes 1376264 | tf_op jit(solution)/shard_map/ppermute | solution.py:64
  158.9 14.0 %all-to-all-start.3 = ((bf16[8,112,128]{2,1,0:T(8,128)(2,1)}), bf16[8,112,128]{2,1,0:T(8,128)(2,1)S(1)}, u32[]{:S(2)}, u32[]{:S(2)}) async-start(bf16[8,112,128]{2,1,0:T(8,128)(2,1)} %bitcast.17), calls=%async_computation.4 | async-start | bytes 458752 | tf_op jit(solution)/shard_map/all_to_all | solution.py:285
  162.6 14.4 %collective-permute-start.13 = (bf16[16,16,896]{2,1,0:T(8,128)(2,1)S(1)}, bf16[16,16,896]{2,1,0:T(8,128)(2,1)S(1)}, u32[]{:S(2)}, u32[]{:S(2)}) collective-permute-start(bf16[16,16,896]{2,1,0:T(8,128)(2,1)S(1)} %pad_maximum_fusion.6), channel_id=1, source_target_pairs={{2,0},{4,2},{6,4},{0,6},{3,1},{5,3},{7,5},{1,7},{10,8},{12,10},{14... | collective-permute-start | bytes 1376264 | tf_op jit(solution)/shard_map/ppermute | solution.py:65
  173.6 13.5 %all-to-all-start.4 = ((bf16[8,112,128]{2,1,0:T(8,128)(2,1)}), bf16[8,112,128]{2,1,0:T(8,128)(2,1)S(1)}, u32[]{:S(2)}, u32[]{:S(2)}) async-start(bf16[8,112,128]{2,1,0:T(8,128)(2,1)} %broadcast_in_dim.67), calls=%async_computation.5 | async-start | bytes 458752 | tf_op jit(solution)/shard_map/all_to_all | solution.py:289
  188.1 14.9 %all-to-all-start.5 = ((bf16[4,896,128]{2,1,0:T(8,128)(2,1)}), bf16[4,896,128]{2,1,0:T(8,128)(2,1)S(1)}, u32[]{:S(2)}, u32[]{:S(2)}) async-start(bf16[4,896,128]{2,1,0:T(8,128)(2,1)} %broadcast_in_dim.69), calls=%async_computation.6 | async-start | bytes 1835008 | tf_op jit(solution)/shard_map/all_to_all | solution.py:292
  196.0 14.4 %copy-start.5 = (bf16[512,256]{1,0:T(8,128)(2,1)S(1)}, bf16[512,256]{1,0:T(8,128)(2,1)}, u32[]{:S(2)}) copy-start(bf16[512,256]{1,0:T(8,128)(2,1)} %get-tuple-element.18) | copy-start | bytes 786436
  196.0 14.4 %copy-start.6 = (bf16[512,256]{1,0:T(8,128)(2,1)S(1)}, bf16[512,256]{1,0:T(8,128)(2,1)}, u32[]{:S(2)}) copy-start(bf16[512,256]{1,0:T(8,128)(2,1)} %get-tuple-element.21) | copy-start | bytes 786436
  196.0 14.4 %copy-start.7 = (bf16[512,256]{1,0:T(8,128)(2,1)S(1)}, bf16[512,256]{1,0:T(8,128)(2,1)}, u32[]{:S(2)}) copy-start(bf16[512,256]{1,0:T(8,128)(2,1)} %get-tuple-element.20) | copy-start | bytes 786436
  203.0 0.9 copy-start.1
  203.9 44.6 %all-to-all-start.1 = ((bf16[64,16,896]{2,1,0:T(8,128)(2,1)}), bf16[64,16,896]{2,1,0:T(8,128)(2,1)S(1)}, u32[]{:S(2)}, u32[]{:S(2)}) async-start(bf16[64,16,896]{2,1,0:T(8,128)(2,1)} %gather_fusion.2), calls=%async_computation.2 | async-start | bytes 3670016 | tf_op jit(solution)/shard_map/all_to_all | solution.py:300
  210.3 2.1 copy-start.2
Sparse Core Ops, SparseCore 0:
  72.1 32.9 all-gather.2
  112.8 41.7 reduce-scatter.1

commit v3 on v2

--- a/solution.py
+++ b/solution.py
@@ -51,24 +51,30 @@
     return total
 
 
-def scatter_pieces(mine, other, parts):
+def scatter_and_reduce(mine, other, parts):
+    half = mine.shape[1] // 2
     swapped = lax.ppermute(other, "core", SWAP)
-    half = mine.shape[1] // 2
-    far, parts = lax.optimization_barrier((plus(mine[3], swapped[3]).astype(BF16), parts))
+    by_x = lax.all_to_all(parts, "x", split_axis=0, concat_axis=0, tiled=True)
+    part = plus(*[by_x[k] for k in range(4)]).astype(BF16).reshape(8, -1, DH)
+    far = plus(mine[3], swapped[3]).astype(BF16)
+    far, part = lax.optimization_barrier((far, part))
     got_low = lax.ppermute(far[:half], "y", UP)
     got_high = lax.ppermute(far[half:], "y", DOWN)
+    by_z = lax.all_to_all(part, "z", split_axis=0, concat_axis=0, tiled=True)
     up_low = plus(mine[1, :half], swapped[1, :half], got_low).astype(BF16)
     up_high = plus(mine[1, half:], swapped[1, half:]).astype(BF16)
     down_low = plus(mine[2, :half], swapped[2, :half]).astype(BF16)
     down_high = plus(mine[2, half:], swapped[2, half:], got_high).astype(BF16)
-    from_below = lax.ppermute(jnp.concatenate([up_low, up_high]), "y", UP)
-    from_above = lax.ppermute(jnp.concatenate([down_low, down_high]), "y", DOWN)
-    total = plus(mine[0], swapped[0], from_below, from_above).astype(BF16)
-    return total, parts, (from_below, total)
-
-
-def after(value, *others):
-    return lax.optimization_barrier((value,) + others)[0]
+    up = jnp.concatenate([up_low, up_high])
+    down = jnp.concatenate([down_low, down_high])
+    total = plus(*[by_z[k] for k in range(8)]).astype(BF16)
+    up, down, total = lax.optimization_barrier((up, down, total))
+    from_below = lax.ppermute(up, "y", UP)
+    from_above = lax.ppermute(down, "y", DOWN)
+    column = jnp.broadcast_to(total[None], part.shape)
+    column = lax.all_to_all(column, "z", split_axis=0, concat_axis=0, tiled=True)
+    summed = plus(mine[0], swapped[0], from_below, from_above).astype(BF16)
+    return summed, column.reshape(-1, DH)
 
 
 def fill_from_pieces(step, refs, rows_ref):
@@ -278,22 +284,32 @@
     )(slots, filled, arrived)
 
 
-def reduce_weight_grads(parts, stages):
-    width = parts.shape[1]
-    by_x = lax.all_to_all(parts, "x", split_axis=0, concat_axis=0, tiled=True)
-    part = plus(*[by_x[k] for k in range(4)]).astype(BF16).reshape(8, width // 8, DH)
-    by_z = lax.all_to_all(part, "z", split_axis=0, concat_axis=0, tiled=True)
-    by_z = after(by_z, stages[0])
-    total = plus(*[by_z[k] for k in range(8)]).astype(BF16)
-    column = jnp.broadcast_to(total[None], part.shape)
-    column = lax.all_to_all(column, "z", split_axis=0, concat_axis=0, tiled=True)
-    column = after(column, stages[1])
-    groups = jnp.broadcast_to(column.reshape(width, DH)[None], parts.shape)
-    groups = lax.all_to_all(groups, "x", split_axis=0, concat_axis=0, tiled=True).astype(F32)
-    return (
-        jnp.concatenate([groups[0], groups[1]], axis=1),
-        jnp.concatenate([groups[2], groups[3]], axis=1),
-    )
+def spread_kernel(place_ref, *refs):
+    pieces, (key_ref, value_ref, held_ref) = refs[:4], refs[4:]
+    for k in range(4):
+        held_ref[lax.rem(place_ref[0] - k + 4, 4)] = pieces[k][...].astype(F32)
+    key_ref[:, :DH], key_ref[:, DH:] = held_ref[0], held_ref[1]
+    value_ref[:, :DH], value_ref[:, DH:] = held_ref[2], held_ref[3]
+
+
+def spread_columns(column, place):
+    width = column.shape[0]
+    pieces = [column] + [lax.ppermute(column, "x", shift(4, k)) for k in (1, 3, 2)]
+    pieces = [pieces[0], pieces[1], pieces[3], pieces[2]]
+    shape = jax.ShapeDtypeStruct((width, 2 * DH), F32)
+    return pl.pallas_call(
+        spread_kernel,
+        grid_spec=pltpu.PrefetchScalarGridSpec(
+            num_scalar_prefetch=1,
+            grid=(1,),
+            in_specs=[pl.BlockSpec(column.shape, lambda i, *_: (0, 0))] * 4,
+            out_specs=[pl.BlockSpec(shape.shape, lambda i, *_: (0, 0))] * 2,
+            scratch_shapes=[pltpu.VMEM((4, width, DH), F32)],
+        ),
+        out_shape=[shape, shape],
+        compiler_params=pltpu.CompilerParams(vmem_limit_bytes=16 * 2**20),
+        name="spread",
+    )(place, *pieces)
 
 
 def exchange(array):
@@ -332,10 +348,13 @@
     order = jnp.stack(
         [(y + dy) % 4 * 2 + (core + other) % 2 for other in (0, 1) for dy in (0, 1, 3, 2)]
     ).astype(jnp.int32)
+    place = lax.axis_index("x").astype(jnp.int32).reshape(1)
+    positions, back, counts, order, filled, place = lax.optimization_barrier(
+        (positions, back, counts, order, filled, place)
+    )
     panels = HALF * KNB
-    wanted = take(incoming, positions)
-    pieces = gather_pieces(wanted[:panels])
-    gathered = lax.all_gather(wanted[panels:], ("y", "core"), axis=0)
+    pieces = gather_pieces(take(incoming, positions[:panels]))
+    gathered = lax.all_gather(take(incoming, positions[panels:]), ("y", "core"), axis=0)
     weights = (w_key, w_value, queries, out_grad)
     attended_0, grad_queries_0, share, begun = attention(
         counts[:HALF], order, pieces, *weights, 0, None
@@ -344,9 +363,11 @@
     attended_1, grad_queries_1, mine, other, parts = attention(
         counts[HALF:], order, gathered, *weights, 1, begun
     )
-    summed_1, parts, stages = scatter_pieces(mine, other, parts)
-    grad_w_key, grad_w_value = reduce_weight_grads(parts, stages)
-    arrived = exchange(take(jnp.concatenate([summed_0, summed_1]), back))
+    summed_1, column = scatter_and_reduce(mine, other, parts)
+    returning = take(jnp.concatenate([summed_0, summed_1]), back)
+    returning, column = lax.optimization_barrier((returning, column))
+    arrived = exchange(returning)
+    grad_w_key, grad_w_value = spread_columns(column, place)
     grad_pool = collect(picked_slot, filled, arrived, pool.shape[0])
     return (
         jnp.concatenate([attended_0, attended_1]),

time: 260 us -> 246 us (0.946)
  waiting for transfers between devices: 137 us -> 109 us
  blocking collectives: 0 us -> 23.9 us
  local copies, waits for them, and re-layouts: 18.2 us -> 13.4 us
  starting transfers between devices: 45.7 us -> 41.2 us
  other arithmetic: 13 us -> 10.1 us
    all_to_all x0 -> x1, blocking collectives: none -> 23.9 us  [scatter_and_reduce(): by_x = lax.all_to_all(parts, 'x', split_axis=0, concat_axis=0, tiled=True)]
    all_to_all x2, waiting for transfers between devices: 79.1 us -> 58.8 us  [exchange(): lax.all_to_all(array, ('z', 'x'), split_axis=0, concat_axis=0, tiled=True)]
    all_to_all x4 -> x2, waiting for transfers between devices: 20.2 us -> 4.09 us  [the longest x1 4.09 us: scatter_and_reduce(): lax.all_to_all(column, 'z', split_axis=0, concat_axis=0, tiled=True)]
    all_to_all x4 -> x2, starting transfers between devices: 19.9 us -> 10.3 us  [the longest x1 6.84 us: scatter_and_reduce(): lax.all_to_all(column, 'z', split_axis=0, concat_axis=0, tiled=True)]
    ppermute x5 -> x8, waiting for transfers between devices: 18.3 us -> 24.3 us  [the longest x3 17 us: spread_columns(): lax.ppermute(column, 'x', shift(4, k))]
    ppermute x5 -> x8, starting transfers between devices: 5.6 us -> 10.4 us  [the longest x3 4.69 us: spread_columns(): lax.ppermute(column, 'x', shift(4, k))]
    gather x3 -> x4, local copies, waits for them, and re-layouts: 5.52 us -> 5.94 us  [local(): take = lambda array, index: jnp.take(array, index, axis=0, mode='clip')]
  transfers between devices with their start and end apart: 22 -> 23, of which waited for: 12 -> 12; matrix products, arithmetic and copies ran while one was open for 8% -> 6% of each run, Pallas kernels for 11% -> 12%
where the time goes in v3:
time: 246 us; the launch traced here: 243 us
  waiting for transfers between devices  109 us (44%)
  starting transfers between devices  41.2 us (17%)
  Pallas kernels  31.7 us (13%)
  blocking collectives  23.9 us (10%)
  between operations  14.4 us (6%)
  local copies, waits for them, and re-layouts  13.4 us (5%)
  other arithmetic  10.1 us (4%)
    all_to_all x2, waiting for transfers between devices, exchange(): lax.all_to_all(array, ('z', 'x'), split_axis=0, concat_axis=0, tiled=True)  58.8 us
    pallas_call x2, Pallas kernels, attention(): pl.pallas_call(functools.partial(attention_kernel, first), grid_spec=pltp...  27.3 us
    all_to_all x1, blocking collectives, scatter_and_reduce(): by_x = lax.all_to_all(parts, 'x', split_axis=0, concat_axis=0, tiled=True)  23.9 us
    ppermute x3, waiting for transfers between devices, spread_columns(): lax.ppermute(column, 'x', shift(4, k))  17 us
    all_to_all x2, starting transfers between devices, exchange(): lax.all_to_all(array, ('z', 'x'), split_axis=0, concat_axis=0, tiled=True)  15.4 us
    ppermute x1, waiting for transfers between devices, gather_pieces(): far_low = lax.ppermute(below[:half], 'y', UP)  8.96 us
    ppermute x1, waiting for transfers between devices, gather_pieces(): below = lax.ppermute(own, 'y', UP)  8.53 us
    all_to_all x1, starting transfers between devices, scatter_and_reduce(): lax.all_to_all(column, 'z', split_axis=0, concat_axis=0, tiled=True)  6.84 us
  transfers between devices with their start and end apart: 23, of which 12 were waited for; matrix products, arithmetic and copies ran while one was open for 6% of the time, Pallas kernels for 12%

profile of v3, /device:TPU:8, one launch (start us, length us, event | category | flops | bytes accessed | tf_op | source)
XLA Modules:
  0.0 243.2 jit_solution(2694974262084254127)
XLA Ops:
  7.2 0.9 copy.17
  8.3 0.8 convert_reduce_fusion
  9.1 0.8 copy.19
  10.4 2.0 gather_fusion
  12.4 11.3 %all-to-all-start = ((bf16[64,16,896]{2,1,0:T(8,128)(2,1)}), bf16[64,16,896]{2,1,0:T(8,128)(2,1)S(1)}, u32[]{:S(2)}, u32[]{:S(2)}) async-start(bf16[64,16,896]{2,1,0:T(8,128)(2,1)} %gather_fusion), calls=%async_computation | async-start | bytes 3670016 | tf_op jit(solution)/shard_map/all_to_all | solution.py:316
  24.1 0.8 dynamic_slice.12
  25.7 42.6 %all-to-all-done = bf16[64,16,896]{2,1,0:T(8,128)(2,1)S(1)} async-done(((bf16[64,16,896]{2,1,0:T(8,128)(2,1)}), bf16[64,16,896]{2,1,0:T(8,128)(2,1)S(1)}, u32[]{:S(2)}, u32[]{:S(2)}) %all-to-all-start) | async-done | bytes 1835040 | tf_op jit(solution)/shard_map/all_to_all | solution.py:316
  68.3 1.4 gather_fusion.2
  70.4 1.7 collective-permute-start.1
  72.5 8.5 %collective-permute-done.1.refs_2_ = bf16[16,16,896]{2,1,0:T(8,128)(2,1)S(1)} collective-permute-done((bf16[16,16,896]{2,1,0:T(8,128)(2,1)S(1)}, bf16[16,16,896]{2,1,0:T(8,128)(2,1)S(1)}, u32[]{:S(2)}, u32[]{:S(2)}) %collective-permute-start.1) | collective-permute-done | bytes 458784 | tf_op jit(solution)/shard_map/ppermute | solution.py:39
  81.1 1.7 collective-permute-start.2
  82.8 1.3 collective-permute-start.3
  84.1 9.0 %collective-permute-done.2.refs_3_ = bf16[8,16,896]{2,1,0:T(8,128)(2,1)S(1)} collective-permute-done((bf16[8,16,896]{2,1,0:T(8,128)(2,1)S(1)}, bf16[8,16,896]{2,1,0:T(8,128)(2,1)S(1)}, u32[]{:S(2)}, u32[]{:S(2)}) %collective-permute-start.2) | collective-permute-done | bytes 229408 | tf_op jit(solution)/shard_map/ppermute | solution.py:41
  93.1 3.0 %collective-permute-done.3.refs_4_ = bf16[8,16,896]{2,1,0:T(8,128)(2,1)S(1)} collective-permute-done((bf16[8,16,896]{2,1,0:T(8,128)(2,1)S(1)}, bf16[8,16,896]{2,1,0:T(8,128)(2,1)S(1)}, u32[]{:S(2)}, u32[]{:S(2)}) %collective-permute-start.3) | collective-permute-done | bytes 229408 | tf_op jit(solution)/shard_map/ppermute | solution.py:42
  96.1 0.6 fusion.12
  96.8 0.8 collective-permute-done.8.refs_9_
  98.5 13.8 %attention.2 = (bf16[512,256]{1,0:T(8,128)(2,1)}, bf16[512,256]{1,0:T(8,128)(2,1)}, bf16[8,16,16,896]{3,2,1,0:T(8,128)(2,1)}, f32[896,512]{1,0:T(8,128)}) custom-call(s32[8]{0:T(128)} %get-tuple-element.61.count_ref, s32[8]{0:T(128)} %stack.35.order_ref, bf16[16,16,896]{2,1,0:T(8,128)(2,1)} %copy-done.3, bf16[16,16,896]{2,1,0:T(8,128)(2,1)} %copy-done.7, ...), custom_call_target="tpu_custom_call" | custom-call | flops 8589934592 | bytes 16777216 | tf_op jit(solution)/shard_map/attention/pallas_call | solution.py:240
  112.3 13.5 %attention.3 = (bf16[512,256]{1,0:T(8,128)(2,1)}, bf16[512,256]{1,0:T(8,128)(2,1)}, bf16[4,16,16,896]{3,2,1,0:T(8,128)(2,1)}, bf16[4,16,16,896]{3,2,1,0:T(8,128)(2,1)}, bf16[4,896,128]{2,1,0:T(8,128)(2,1)}) custom-call(s32[8]{0:T(128)} %get-tuple-element.62.count_ref, s32[8]{0:T(128)} %stack.35.order_ref, bf16[8,16,16,896]{3,2,1,0:T(8,128)(2,1)} %bitcast.43, ...), custom_call_target="tpu_custom_call" | custom-call | flops 8589934592 | bytes 16777216 | tf_op jit(solution)/shard_map/attention/pallas_call | solution.py:240
  126.1 23.9 %all_to_all.25 = bf16[4,896,128]{2,1,0:T(8,128)(2,1)S(1)} all-to-all(bf16[4,896,128]{2,1,0:T(8,128)(2,1)} %get-tuple-element.41), channel_id=1, replica_groups=mesh['z'=8,'x'=4,'y'=4,'core'=2] {'x'}, dimensions={0} | all-to-all | bytes 1835008 | tf_op jit(solution)/shard_map/all_to_all | solution.py:57
  149.9 0.8 add_convert_fusion.3
  150.7 1.2 copy-done.2
  152.1 3.4 %all-to-all-start.2 = ((bf16[8,112,128]{2,1,0:T(8,128)(2,1)}), bf16[8,112,128]{2,1,0:T(8,128)(2,1)S(1)}, u32[]{:S(2)}, u32[]{:S(2)}) async-start(bf16[8,112,128]{2,1,0:T(8,128)(2,1)} %bitcast.41), calls=%async_computation.3 | async-start | bytes 458752 | tf_op jit(solution)/shard_map/all_to_all | solution.py:63
  155.6 0.7 collective-permute-start.11
  156.3 1.4 collective-permute-start.10
  157.7 1.2 fusion.6
  158.9 3.5 %collective-permute-done.11 = bf16[8,16,896]{2,1,0:T(8,128)(2,1)S(1)} collective-permute-done((bf16[8,16,896]{2,1,0:T(8,128)(2,1)S(1)}, bf16[8,16,896]{2,1,0:T(8,128)(2,1)S(1)}, u32[]{:S(2)}, u32[]{:S(2)}) %collective-permute-start.11) | collective-permute-done | bytes 229408 | tf_op jit(solution)/shard_map/ppermute | solution.py:62
  162.4 2.3 collective-permute-done.10
  164.7 1.2 fusion.3
  166.0 0.9 pad_maximum_fusion.3
  166.9 0.9 collective-permute-start.12
  167.8 2.4 collective-permute-start.13
  170.2 0.7 broadcast_in_dim.64
  171.0 6.8 %all-to-all-start.3 = ((bf16[8,112,128]{2,1,0:T(8,128)(2,1)}), bf16[8,112,128]{2,1,0:T(8,128)(2,1)S(1)}, u32[]{:S(2)}, u32[]{:S(2)}) async-start(bf16[8,112,128]{2,1,0:T(8,128)(2,1)} %broadcast_in_dim.64), calls=%async_computation.4 | async-start | bytes 458752 | tf_op jit(solution)/shard_map/all_to_all | solution.py:75
  177.8 1.4 collective-permute-done.12
  179.2 1.5 fusion.1
  180.7 1.1 pad_maximum_fusion
  181.9 2.0 gather_fusion.3
  183.8 4.1 %all-to-all-done.3 = bf16[8,112,128]{2,1,0:T(8,128)(2,1)S(1)} async-done(((bf16[8,112,128]{2,1,0:T(8,128)(2,1)}), bf16[8,112,128]{2,1,0:T(8,128)(2,1)S(1)}, u32[]{:S(2)}, u32[]{:S(2)}) %all-to-all-start.3) | async-done | bytes 229408 | tf_op jit(solution)/shard_map/all_to_all | solution.py:75
  187.9 4.1 %all-to-all-start.4 = ((bf16[64,16,896]{2,1,0:T(8,128)(2,1)}), bf16[64,16,896]{2,1,0:T(8,128)(2,1)S(1)}, u32[]{:S(2)}, u32[]{:S(2)}) async-start(bf16[64,16,896]{2,1,0:T(8,128)(2,1)} %gather_fusion.3), calls=%async_computation.5 | async-start | bytes 3670016 | tf_op jit(solution)/shard_map/all_to_all | solution.py:316
  192.1 3.0 %collective-permute-start.16 = (bf16[896,128]{1,0:T(8,128)(2,1)S(1)}, bf16[896,128]{1,0:T(8,128)(2,1)S(1)}, u32[]{:S(2)}, u32[]{:S(2)}) collective-permute-start(bf16[896,128]{1,0:T(8,128)(2,1)S(1)} %bitcast.37), channel_id=1, source_target_pairs={{0,24},{8,0},{16,8},{24,16},{1,25},{9,1},{17,9},{25,17},{2,26},{10... | collective-permute-start | bytes 688136 | tf_op jit(solution)/shard_map/ppermute | solution.py:297
  195.0 0.8 collective-permute-start.15
  195.9 0.9 collective-permute-start.14
  196.8 2.1 pad_maximum_fusion.1
  198.8 11.4 %collective-permute-done.16.refs_3_ = bf16[896,128]{1,0:T(8,128)(2,1)S(1)} collective-permute-done((bf16[896,128]{1,0:T(8,128)(2,1)S(1)}, bf16[896,128]{1,0:T(8,128)(2,1)S(1)}, u32[]{:S(2)}, u32[]{:S(2)}) %collective-permute-start.16) | collective-permute-done | bytes 229408 | tf_op jit(solution)/shard_map/ppermute | solution.py:297
  210.2 5.7 %collective-permute-done.14.refs_1_ = bf16[896,128]{1,0:T(8,128)(2,1)S(1)} collective-permute-done((bf16[896,128]{1,0:T(8,128)(2,1)S(1)}, bf16[896,128]{1,0:T(8,128)(2,1)S(1)}, u32[]{:S(2)}, u32[]{:S(2)}) %collective-permute-start.14) | collective-permute-done | bytes 229408 | tf_op jit(solution)/shard_map/ppermute | solution.py:297
  215.9 1.4 spread.1
  217.3 16.2 %all-to-all-done.4.arrived_ref = bf16[64,16,896]{2,1,0:T(8,128)(2,1)S(1)} async-done(((bf16[64,16,896]{2,1,0:T(8,128)(2,1)}), bf16[64,16,896]{2,1,0:T(8,128)(2,1)S(1)}, u32[]{:S(2)}, u32[]{:S(2)}) %all-to-all-start.4) | async-done | bytes 1835040 | tf_op jit(solution)/shard_map/all_to_all | solution.py:316
  233.5 2.9 %collect.1 = f32[32,16,896]{2,1,0:T(8,128)} custom-call(s32[64]{0:T(128)S(1)} %reshape.114.slot_ref, s32[64]{0:T(128)S(1)} %reshape.104.filled_ref, bf16[64,16,896]{2,1,0:T(8,128)(2,1)S(1)} %all-to-all-done.4.arrived_ref), custom_call_target="tpu_custom_call" | custom-call | tf_op jit(solution)/shard_map/collect/pallas_call | solution.py:273
  (76 shorter events, 4.4 us)
Async XLA Ops:
  7.2 3.2 %copy-start = (bf16[32,16,896]{2,1,0:T(8,128)(2,1)S(1)}, bf16[32,16,896]{2,1,0:T(8,128)(2,1)}, u32[]{:S(2)}) copy-start(bf16[32,16,896]{2,1,0:T(8,128)(2,1)} %param.9) | copy-start | bytes 2752516
  12.4 56.0 %all-to-all-start = ((bf16[64,16,896]{2,1,0:T(8,128)(2,1)}), bf16[64,16,896]{2,1,0:T(8,128)(2,1)S(1)}, u32[]{:S(2)}, u32[]{:S(2)}) async-start(bf16[64,16,896]{2,1,0:T(8,128)(2,1)} %gather_fusion), calls=%async_computation | async-start | bytes 3670016 | tf_op jit(solution)/shard_map/all_to_all | solution.py:316
  23.7 88.6 %all-gather.3.cloned.1.call-start = ((), (), s32[]{:S(2)}) async-start(), calls=%async_computation.7 | async-start | bytes 4128768 | tf_op jit(solution)/shard_map/all_gather | solution.py:357
  69.7 111.0 %reduce-scatter.2.cloned.1.call-start = ((), (), s32[]{:S(2)}) async-start(), calls=%async_computation.6 | async-start | bytes 4128768 | tf_op jit(solution)/shard_map/reduce_scatter | solution.py:362
  70.4 27.2 %copy-start.3 = (bf16[16,16,896]{2,1,0:T(8,128)(2,1)}, bf16[16,16,896]{2,1,0:T(8,128)(2,1)S(1)}, u32[]{:S(2)}) copy-start(bf16[16,16,896]{2,1,0:T(8,128)(2,1)S(1)} %gather_fusion.1) | copy-start | bytes 1376260
  70.4 10.6 %collective-permute-start.1 = (bf16[16,16,896]{2,1,0:T(8,128)(2,1)S(1)}, bf16[16,16,896]{2,1,0:T(8,128)(2,1)S(1)}, u32[]{:S(2)}, u32[]{:S(2)}) collective-permute-start(bf16[16,16,896]{2,1,0:T(8,128)(2,1)S(1)} %gather_fusion.1), channel_id=1, source_target_pairs={{0,2},{2,4},{4,6},{6,0},{1,3},{3,5},{5,7},{7,1},{8,10},{10,12},{12... | collective-permute-start | bytes 1376264 | tf_op jit(solution)/shard_map/ppermute | solution.py:39
  72.1 10.7 %collective-permute-start = (bf16[16,16,896]{2,1,0:T(8,128)(2,1)S(1)}, bf16[16,16,896]{2,1,0:T(8,128)(2,1)S(1)}, u32[]{:S(2)}, u32[]{:S(2)}) collective-permute-start(bf16[16,16,896]{2,1,0:T(8,128)(2,1)S(1)} %gather_fusion.1), channel_id=1, source_target_pairs={{2,0},{4,2},{6,4},{0,6},{3,1},{5,3},{7,5},{1,7},{10,8},{12,10},{14... | collective-permute-start | bytes 1376264 | tf_op jit(solution)/shard_map/ppermute | solution.py:40
  72.5 24.2 %collective-permute-start.4 = (bf16[16,16,896]{2,1,0:T(8,128)(2,1)S(1)}, bf16[16,16,896]{2,1,0:T(8,128)(2,1)S(1)}, u32[]{:S(2)}, u32[]{:S(2)}) collective-permute-start(bf16[16,16,896]{2,1,0:T(8,128)(2,1)S(1)} %gather_fusion.1), channel_id=1, source_target_pairs={{0,1},{1,0},{2,3},{3,2},{4,5},{5,4},{6,7},{7,6},{8,9},{9,8},{10,11... | collective-permute-start | bytes 1376264 | tf_op jit(solution)/shard_map/ppermute | solution.py:44
  81.1 16.5 %copy-start.6 = (bf16[16,16,896]{2,1,0:T(8,128)(2,1)}, bf16[16,16,896]{2,1,0:T(8,128)(2,1)S(1)}, u32[]{:S(2)}) copy-start(bf16[16,16,896]{2,1,0:T(8,128)(2,1)S(1)} %collective-permute-done.1.refs_2_) | copy-start | bytes 1376260
  81.1 12.0 %collective-permute-start.2 = (bf16[8,16,896]{2,1,0:T(8,128)(2,1)S(1)}, bf16[8,16,896]{2,1,0:T(8,128)(2,1)S(1)}, u32[]{:S(2)}, u32[]{:S(2)}) collective-permute-start(bf16[8,16,896]{2,1,0:T(8,128)(2,1)S(1)} %slice.136), channel_id=1, source_target_pairs={{0,2},{2,4},{4,6},{6,0},{1,3},{3,5},{5,7},{7,1},{8,10},{10,12},{12... | collective-permute-start | bytes 688136 | tf_op jit(solution)/shard_map/ppermute | solution.py:41
  82.8 14.0 %collective-permute-start.6 = (bf16[16,16,896]{2,1,0:T(8,128)(2,1)S(1)}, bf16[16,16,896]{2,1,0:T(8,128)(2,1)S(1)}, u32[]{:S(2)}, u32[]{:S(2)}) collective-permute-start(bf16[16,16,896]{2,1,0:T(8,128)(2,1)S(1)} %collective-permute-done.1.refs_2_), channel_id=1, source_target_pairs={{0,1},{1,0},{2,3},{3,2},{4,5},{5,4},{6,7},{7,6},{8,9},{9,8},{10,11... | collective-permute-start | bytes 1376264 | tf_op jit(solution)/shard_map/ppermute | solution.py:44
  82.8 14.8 %copy-start.7 = (bf16[16,16,896]{2,1,0:T(8,128)(2,1)}, bf16[16,16,896]{2,1,0:T(8,128)(2,1)S(1)}, u32[]{:S(2)}) copy-start(bf16[16,16,896]{2,1,0:T(8,128)(2,1)S(1)} %collective-permute-done.refs_1_) | copy-start | bytes 1376260
  82.8 13.3 %collective-permute-start.3 = (bf16[8,16,896]{2,1,0:T(8,128)(2,1)S(1)}, bf16[8,16,896]{2,1,0:T(8,128)(2,1)S(1)}, u32[]{:S(2)}, u32[]{:S(2)}) collective-permute-start(bf16[8,16,896]{2,1,0:T(8,128)(2,1)S(1)} %slice.137), channel_id=1, source_target_pairs={{2,0},{4,2},{6,4},{0,6},{3,1},{5,3},{7,5},{1,7},{10,8},{12,10},{14... | collective-permute-start | bytes 688136 | tf_op jit(solution)/shard_map/ppermute | solution.py:42
  84.1 13.4 %collective-permute-start.5 = (bf16[16,16,896]{2,1,0:T(8,128)(2,1)S(1)}, bf16[16,16,896]{2,1,0:T(8,128)(2,1)S(1)}, u32[]{:S(2)}, u32[]{:S(2)}) collective-permute-start(bf16[16,16,896]{2,1,0:T(8,128)(2,1)S(1)} %collective-permute-done.refs_1_), channel_id=1, source_target_pairs={{0,1},{1,0},{2,3},{3,2},{4,5},{5,4},{6,7},{7,6},{8,9},{9,8},{10,11... | collective-permute-start | bytes 1376264 | tf_op jit(solution)/shard_map/ppermute | solution.py:44
  93.1 4.5 %copy-start.11 = (bf16[8,16,896]{2,1,0:T(8,128)(2,1)}, bf16[8,16,896]{2,1,0:T(8,128)(2,1)S(1)}, u32[]{:S(2)}) copy-start(bf16[8,16,896]{2,1,0:T(8,128)(2,1)S(1)} %collective-permute-done.2.refs_3_) | copy-start | bytes 688132
  93.1 3.6 %collective-permute-start.7 = (bf16[8,16,896]{2,1,0:T(8,128)(2,1)S(1)}, bf16[8,16,896]{2,1,0:T(8,128)(2,1)S(1)}, u32[]{:S(2)}, u32[]{:S(2)}) collective-permute-start(bf16[8,16,896]{2,1,0:T(8,128)(2,1)S(1)} %collective-permute-done.2.refs_3_), channel_id=1, source_target_pairs={{0,1},{1,0},{2,3},{3,2},{4,5},{5,4},{6,7},{7,6},{8,9},{9,8},{10,11... | collective-permute-start | bytes 688136 | tf_op jit(solution)/shard_map/ppermute | solution.py:44
  96.1 1.5 copy-start.12
  96.1 1.5 collective-permute-start.8
  96.7 0.9 copy-start.8
  96.7 0.9 copy-start.13
  96.8 1.0 copy-start.9
  97.6 0.7 copy-start.14
  97.6 0.9 copy-start.10
  125.8 26.1 %copy-start.1 = (bf16[4,16,16,896]{3,2,1,0:T(8,128)(2,1)S(1)}, bf16[4,16,16,896]{3,2,1,0:T(8,128)(2,1)}, u32[]{:S(2)}) copy-start(bf16[4,16,16,896]{3,2,1,0:T(8,128)(2,1)} %get-tuple-element.39) | copy-start | bytes 5505028
  125.8 24.9 %collective-permute-start.9 = (bf16[4,16,16,896]{3,2,1,0:T(8,128)(2,1)}, bf16[4,16,16,896]{3,2,1,0:T(8,128)(2,1)S(1)}, u32[]{:S(2)}, u32[]{:S(2)}) collective-permute-start(bf16[4,16,16,896]{3,2,1,0:T(8,128)(2,1)} %get-tuple-element.40), channel_id=1, source_target_pairs={{0,1},{1,0},{2,3},{3,2},{4,5},{5,4},{6,7},{7,6},{8,9},{9,8},{10,11... | collective-permute-start | bytes 5505032 | tf_op jit(solution)/shard_map/ppermute | solution.py:56
  150.7 1.2 copy-start.2
  152.1 14.7 %all-to-all-start.2 = ((bf16[8,112,128]{2,1,0:T(8,128)(2,1)}), bf16[8,112,128]{2,1,0:T(8,128)(2,1)S(1)}, u32[]{:S(2)}, u32[]{:S(2)}) async-start(bf16[8,112,128]{2,1,0:T(8,128)(2,1)} %bitcast.41), calls=%async_computation.3 | async-start | bytes 458752 | tf_op jit(solution)/shard_map/all_to_all | solution.py:63
  155.6 6.8 %collective-permute-start.11 = (bf16[8,16,896]{2,1,0:T(8,128)(2,1)S(1)}, bf16[8,16,896]{2,1,0:T(8,128)(2,1)S(1)}, u32[]{:S(2)}, u32[]{:S(2)}) collective-permute-start(bf16[8,16,896]{2,1,0:T(8,128)(2,1)S(1)} %get-tuple-element.57), channel_id=1, source_target_pairs={{2,0},{4,2},{6,4},{0,6},{3,1},{5,3},{7,5},{1,7},{10,8},{12,10},{14... | collective-permute-start | bytes 688136 | tf_op jit(solution)/shard_map/ppermute | solution.py:62
  156.3 8.4 %collective-permute-start.10 = (bf16[8,16,896]{2,1,0:T(8,128)(2,1)S(1)}, bf16[8,16,896]{2,1,0:T(8,128)(2,1)S(1)}, u32[]{:S(2)}, u32[]{:S(2)}) collective-permute-start(bf16[8,16,896]{2,1,0:T(8,128)(2,1)S(1)} %get-tuple-element.58), channel_id=1, source_target_pairs={{0,2},{2,4},{4,6},{6,0},{1,3},{3,5},{5,7},{7,1},{8,10},{10,12},{12... | collective-permute-start | bytes 688136 | tf_op jit(solution)/shard_map/ppermute | solution.py:61
  166.9 12.3 %collective-permute-start.12 = (bf16[16,16,896]{2,1,0:T(8,128)(2,1)}, bf16[16,16,896]{2,1,0:T(8,128)(2,1)}, u32[]{:S(2)}, u32[]{:S(2)}) collective-permute-start(bf16[16,16,896]{2,1,0:T(8,128)(2,1)} %get-tuple-element.44), channel_id=1, source_target_pairs={{0,2},{2,4},{4,6},{6,0},{1,3},{3,5},{5,7},{7,1},{8,10},{10,12},{12... | collective-permute-start | bytes 1376264 | tf_op jit(solution)/shard_map/ppermute | solution.py:72
  167.8 11.4 %collective-permute-start.13 = (bf16[16,16,896]{2,1,0:T(8,128)(2,1)S(1)}, bf16[16,16,896]{2,1,0:T(8,128)(2,1)}, u32[]{:S(2)}, u32[]{:S(2)}) collective-permute-start(bf16[16,16,896]{2,1,0:T(8,128)(2,1)S(1)} %get-tuple-element.45), channel_id=1, source_target_pairs={{2,0},{4,2},{6,4},{0,6},{3,1},{5,3},{7,5},{1,7},{10,8},{12,10},{14... | collective-permute-start | bytes 1376264 | tf_op jit(solution)/shard_map/ppermute | solution.py:73
  171.0 17.0 %all-to-all-start.3 = ((bf16[8,112,128]{2,1,0:T(8,128)(2,1)}), bf16[8,112,128]{2,1,0:T(8,128)(2,1)S(1)}, u32[]{:S(2)}, u32[]{:S(2)}) async-start(bf16[8,112,128]{2,1,0:T(8,128)(2,1)} %broadcast_in_dim.64), calls=%async_computation.4 | async-start | bytes 458752 | tf_op jit(solution)/shard_map/all_to_all | solution.py:75
  187.9 8.8 %copy-start.4 = (bf16[512,256]{1,0:T(8,128)(2,1)S(1)}, bf16[512,256]{1,0:T(8,128)(2,1)}, u32[]{:S(2)}) copy-start(bf16[512,256]{1,0:T(8,128)(2,1)} %get-tuple-element.32) | copy-start | bytes 786436
  187.9 8.8 %copy-start.5 = (bf16[512,256]{1,0:T(8,128)(2,1)S(1)}, bf16[512,256]{1,0:T(8,128)(2,1)}, u32[]{:S(2)}) copy-start(bf16[512,256]{1,0:T(8,128)(2,1)} %get-tuple-element.35) | copy-start | bytes 786436
  187.9 45.5 %all-to-all-start.4 = ((bf16[64,16,896]{2,1,0:T(8,128)(2,1)}), bf16[64,16,896]{2,1,0:T(8,128)(2,1)S(1)}, u32[]{:S(2)}, u32[]{:S(2)}) async-start(bf16[64,16,896]{2,1,0:T(8,128)(2,1)} %gather_fusion.3), calls=%async_computation.5 | async-start | bytes 3670016 | tf_op jit(solution)/shard_map/all_to_all | solution.py:316
  192.1 18.1 %collective-permute-start.16 = (bf16[896,128]{1,0:T(8,128)(2,1)S(1)}, bf16[896,128]{1,0:T(8,128)(2,1)S(1)}, u32[]{:S(2)}, u32[]{:S(2)}) collective-permute-start(bf16[896,128]{1,0:T(8,128)(2,1)S(1)} %bitcast.37), channel_id=1, source_target_pairs={{0,24},{8,0},{16,8},{24,16},{1,25},{9,1},{17,9},{25,17},{2,26},{10... | collective-permute-start | bytes 688136 | tf_op jit(solution)/shard_map/ppermute | solution.py:297
  195.0 15.2 %collective-permute-start.15 = (bf16[896,128]{1,0:T(8,128)(2,1)S(1)}, bf16[896,128]{1,0:T(8,128)(2,1)S(1)}, u32[]{:S(2)}, u32[]{:S(2)}) collective-permute-start(bf16[896,128]{1,0:T(8,128)(2,1)S(1)} %bitcast.38), channel_id=1, source_target_pairs={{0,16},{8,24},{16,0},{24,8},{1,17},{9,25},{17,1},{25,9},{2,18},{10... | collective-permute-start | bytes 688136 | tf_op jit(solution)/shard_map/ppermute | solution.py:297
  195.9 20.0 %collective-permute-start.14 = (bf16[896,128]{1,0:T(8,128)(2,1)S(1)}, bf16[896,128]{1,0:T(8,128)(2,1)S(1)}, u32[]{:S(2)}, u32[]{:S(2)}) collective-permute-start(bf16[896,128]{1,0:T(8,128)(2,1)S(1)} %bitcast.39), channel_id=1, source_target_pairs={{0,8},{8,16},{16,24},{24,0},{1,9},{9,17},{17,25},{25,1},{2,10},{10... | collective-permute-start | bytes 688136 | tf_op jit(solution)/shard_map/ppermute | solution.py:297
Sparse Core Ops, SparseCore 0:
  69.8 33.7 all-gather.2
  112.4 38.1 reduce-scatter.1

commit v4 on v3

--- a/solution.py
+++ b/solution.py
@@ -51,30 +51,14 @@
     return total
 
 
-def scatter_and_reduce(mine, other, parts):
-    half = mine.shape[1] // 2
-    swapped = lax.ppermute(other, "core", SWAP)
+def reduce_weight_grads(parts):
     by_x = lax.all_to_all(parts, "x", split_axis=0, concat_axis=0, tiled=True)
     part = plus(*[by_x[k] for k in range(4)]).astype(BF16).reshape(8, -1, DH)
-    far = plus(mine[3], swapped[3]).astype(BF16)
-    far, part = lax.optimization_barrier((far, part))
-    got_low = lax.ppermute(far[:half], "y", UP)
-    got_high = lax.ppermute(far[half:], "y", DOWN)
     by_z = lax.all_to_all(part, "z", split_axis=0, concat_axis=0, tiled=True)
-    up_low = plus(mine[1, :half], swapped[1, :half], got_low).astype(BF16)
-    up_high = plus(mine[1, half:], swapped[1, half:]).astype(BF16)
-    down_low = plus(mine[2, :half], swapped[2, :half]).astype(BF16)
-    down_high = plus(mine[2, half:], swapped[2, half:], got_high).astype(BF16)
-    up = jnp.concatenate([up_low, up_high])
-    down = jnp.concatenate([down_low, down_high])
     total = plus(*[by_z[k] for k in range(8)]).astype(BF16)
-    up, down, total = lax.optimization_barrier((up, down, total))
-    from_below = lax.ppermute(up, "y", UP)
-    from_above = lax.ppermute(down, "y", DOWN)
     column = jnp.broadcast_to(total[None], part.shape)
     column = lax.all_to_all(column, "z", split_axis=0, concat_axis=0, tiled=True)
-    summed = plus(mine[0], swapped[0], from_below, from_above).astype(BF16)
-    return summed, column.reshape(-1, DH)
+    return column.reshape(-1, DH)
 
 
 def fill_from_pieces(step, refs, rows_ref):
@@ -102,13 +86,12 @@
             put(3, far_high)
 
 
-def fill_from_gathered(order_ref, gathered_ref, rows_ref):
+def fill_from_gathered(gathered_ref, rows_ref):
     for piece in range(PIECES):
-        source = order_ref[piece]
         for c in range(GROUP):
             at = c * SPAN + piece * KNB * ROWS
             rows_ref[at : at + KNB * ROWS, :] = gathered_ref[
-                source, c * KNB : (c + 1) * KNB
+                piece, c * KNB : (c + 1) * KNB
             ].reshape(KNB * ROWS, gathered_ref.shape[3])
 
 
@@ -117,16 +100,16 @@
     if first:
         pieces, refs = refs[:10], refs[10:]
     else:
-        gathered_ref, begun_ref, refs = refs[0], refs[1], refs[2:]
+        gathered_ref, begun_ref, _, refs = refs[0], refs[1], refs[2], refs[3:]
     key_weight_ref, value_weight_ref, query_ref, grad_ref, attended_ref, grad_query_ref = refs[:6]
     refs = refs[6:]
+    share_ref, out_ref, rows_ref, kv_ref, both_ref = refs[:5]
     if first:
-        share_ref, out_ref, rows_ref, kv_ref, both_ref = refs
         total_ref = out_ref
         fill_from_pieces(step, pieces, rows_ref)
     else:
-        mine_ref, other_ref, out_ref, rows_ref, kv_ref, both_ref, total_ref = refs
-        fill_from_gathered(order_ref, gathered_ref, rows_ref)
+        total_ref = refs[5]
+        fill_from_gathered(gathered_ref, rows_ref)
     local = key_weight_ref.shape[1]
     factor = 1.0 / math.sqrt(DH)
     key_cols, value_cols = slice(0, local), slice(local, 2 * local)
@@ -181,12 +164,7 @@
             at = piece * KNB * ROWS
             part = share[at : at + KNB * ROWS].reshape(KNB, ROWS, share.shape[1])
             panels = slice(c * KNB, (c + 1) * KNB)
-            if first:
-                share_ref[order_ref[piece], panels] = part
-            elif piece < 4:
-                mine_ref[piece, panels] = part
-            else:
-                other_ref[piece - 4, panels] = part
+            share_ref[order_ref[piece] if first else piece, panels] = part
     part = dot(rows_ref[...], both_ref[...], 0, 0)
 
     @pl.when(step == 0)
@@ -215,8 +193,8 @@
     plain = pl.BlockSpec(block, lambda i, *_: (i, 0, 0))
     low = pl.BlockSpec(block, lambda i, *_: (jnp.minimum(i, half_steps - 1), 0, 0))
     high = pl.BlockSpec(block, lambda i, *_: (jnp.maximum(i - half_steps, 0), 0, 0))
-    stacked = lambda n: pl.BlockSpec((n,) + block, lambda i, *_: (0, i, 0, 0))
-    stacked_shape = lambda n: jax.ShapeDtypeStruct((n, HALF * KNB, ROWS, width), BF16)
+    stacked = lambda begin: pl.BlockSpec((PIECES,) + block, lambda i, *_: (0, begin + i, 0, 0))
+    shares = jax.ShapeDtypeStruct((PIECES, CH_DEV * KNB, ROWS, width), BF16)
     token_in = pl.BlockSpec((GROUP * STRETCH, local), lambda i, *_: (i + half * steps, 0))
     token_out = pl.BlockSpec((GROUP * STRETCH, local), lambda i, *_: (i, 0))
     token_shape = jax.ShapeDtypeStruct((tokens, local), BF16)
@@ -229,24 +207,25 @@
     ]
     if first:
         in_specs = [plain, plain, plain, low, high] * 2
-        share_specs, share_shapes = [stacked(PIECES)], [stacked_shape(PIECES)]
         out = jax.ShapeDtypeStruct(total, F32)
+        aliases = {}
     else:
-        in_specs = [stacked(PIECES), whole(total)]
-        panels = [panels, begun]
-        share_specs, share_shapes = [stacked(4)] * 2, [stacked_shape(4)] * 2
+        in_specs = [stacked(0), whole(total), pl.BlockSpec(memory_space=pl.ANY)]
+        panels = (panels,) + begun
         out = jax.ShapeDtypeStruct((4, width, DH), BF16)
         scratch = scratch + [pltpu.VMEM(total, F32)]
+        aliases = {4: 2}
     return pl.pallas_call(
         functools.partial(attention_kernel, first),
         grid_spec=pltpu.PrefetchScalarGridSpec(
             num_scalar_prefetch=2,
             grid=(steps,),
             in_specs=in_specs + [whole(w_key.shape), whole(w_key.shape), token_in, token_in],
-            out_specs=[token_out, token_out] + share_specs + [whole(out.shape)],
+            out_specs=[token_out, token_out, stacked(half * steps), whole(out.shape)],
             scratch_shapes=scratch,
         ),
-        out_shape=[token_shape, token_shape] + share_shapes + [out],
+        out_shape=[token_shape, token_shape, shares, out],
+        input_output_aliases=aliases,
         compiler_params=pltpu.CompilerParams(vmem_limit_bytes=56 * 2**20),
         cost_estimate=pl.CostEstimate(
             flops=8 * 2**30, bytes_accessed=16 * 2**20, transcendentals=2**18
@@ -356,15 +335,15 @@
     pieces = gather_pieces(take(incoming, positions[:panels]))
     gathered = lax.all_gather(take(incoming, positions[panels:]), ("y", "core"), axis=0)
     weights = (w_key, w_value, queries, out_grad)
-    attended_0, grad_queries_0, share, begun = attention(
+    attended_0, grad_queries_0, shares, begun = attention(
         counts[:HALF], order, pieces, *weights, 0, None
     )
-    summed_0 = lax.psum_scatter(share, ("y", "core"), scatter_dimension=0)
-    attended_1, grad_queries_1, mine, other, parts = attention(
-        counts[HALF:], order, gathered, *weights, 1, begun
-    )
-    summed_1, column = scatter_and_reduce(mine, other, parts)
-    returning = take(jnp.concatenate([summed_0, summed_1]), back)
+    attended_1, grad_queries_1, shares, parts = attention(
+        counts[HALF:], order, gathered, *weights, 1, (begun, shares)
+    )
+    summed = lax.psum_scatter(shares, ("y", "core"), scatter_dimension=0)
+    column = reduce_weight_grads(parts)
+    returning = take(summed, back)
     returning, column = lax.optimization_barrier((returning, column))
     arrived = exchange(returning)
     grad_w_key, grad_w_value = spread_columns(column, place)

time: 246 us -> 247 us (level)
  blocking collectives: 23.9 us -> 35.6 us
  other arithmetic: 10.1 us -> 3.38 us
  starting transfers between devices: 41.2 us -> 36.4 us
    all_to_all x1 -> x2, blocking collectives: 23.9 us -> 35.6 us  [the longest x1 22.8 us: reduce_weight_grads(): by_x = lax.all_to_all(parts, 'x', split_axis=0, concat_axis=0, tiled=True)]
    reduce_scatter x1, waiting for transfers between devices: 0.02 us -> 9.65 us  [local(): summed = lax.psum_scatter(shares, ('y', 'core'), scatter_dimension=0)]
    ppermute x5 -> x0, waiting for transfers between devices: 7.28 us -> none  [the longest x1 3.54 us: scatter_and_reduce(): got_high = lax.ppermute(far[half:], 'y', DOWN)]
    all_to_all x2 -> x1, starting transfers between devices: 10.3 us -> 3.4 us  [reduce_weight_grads(): lax.all_to_all(column, 'z', split_axis=0, concat_axis=0, tiled=True)]
    all_to_all x2, starting transfers between devices: 15.4 us -> 21.5 us  [exchange(): lax.all_to_all(array, ('z', 'x'), split_axis=0, concat_axis=0, tiled=True)]
    ppermute x5 -> x0, starting transfers between devices: 5.66 us -> none  [the longest x1 2.42 us: scatter_and_reduce(): from_above = lax.ppermute(down, 'y', DOWN)]
    convert_element_type x5 -> x0, other arithmetic: 4.1 us -> none  [the longest x1 1.53 us: scatter_and_reduce(): summed = plus(mine[0], swapped[0], from_below, from_above).astype(BF16)]
    all_to_all x2 -> x1, waiting for transfers between devices: 4.09 us -> 0.01 us  [reduce_weight_grads(): lax.all_to_all(column, 'z', split_axis=0, concat_axis=0, tiled=True)]
  transfers between devices with their start and end apart: 23 -> 17, of which waited for: 12 -> 10; matrix products, arithmetic and copies ran while one was open for 6% -> 4% of each run, Pallas kernels for 12% -> 6%
where the time goes in v4:
time: 247 us; the launch traced here: 245 us
  waiting for transfers between devices  109 us (44%)
  starting transfers between devices  36.4 us (15%)
  blocking collectives  35.6 us (14%)
  Pallas kernels  31.7 us (13%)
  local copies, waits for them, and re-layouts  14.5 us (6%)
  between operations  14.4 us (6%)
  other arithmetic  3.38 us (1%)
    all_to_all x2, waiting for transfers between devices, exchange(): lax.all_to_all(array, ('z', 'x'), split_axis=0, concat_axis=0, tiled=True)  61.1 us
    pallas_call x2, Pallas kernels, attention(): pl.pallas_call(functools.partial(attention_kernel, first), grid_spec=pltp...  27.3 us
    all_to_all x1, blocking collectives, reduce_weight_grads(): by_x = lax.all_to_all(parts, 'x', split_axis=0, concat_axis=0, tiled=True)  22.8 us
    all_to_all x2, starting transfers between devices, exchange(): lax.all_to_all(array, ('z', 'x'), split_axis=0, concat_axis=0, tiled=True)  21.5 us
    ppermute x3, waiting for transfers between devices, spread_columns(): lax.ppermute(column, 'x', shift(4, k))  19.5 us
    all_to_all x1, blocking collectives, reduce_weight_grads(): by_z = lax.all_to_all(part, 'z', split_axis=0, concat_axis=0, tiled=True)  12.8 us
    reduce_scatter x1, waiting for transfers between devices, local(): summed = lax.psum_scatter(shares, ('y', 'core'), scatter_dimension=0)  9.65 us
    ppermute x1, waiting for transfers between devices, gather_pieces(): below = lax.ppermute(own, 'y', UP)  8.53 us
  transfers between devices with their start and end apart: 17, of which 10 were waited for; matrix products, arithmetic and copies ran while one was open for 4% of the time, Pallas kernels for 6%

profile of v4, /device:TPU:8, one launch (start us, length us, event | category | flops | bytes accessed | tf_op | source)
XLA Modules:
  0.0 245.4 jit_solution(9314299503331451930)
XLA Ops:
  7.2 0.9 copy.18
  8.1 0.1 reshape.63
  8.3 0.8 convert_reduce_fusion
  9.1 0.8 copy.20
  9.9 0.1 broadcast_in_dim.59
  10.1 0.1 select_reduce_fusion
  10.4 2.0 gather_fusion
  12.4 11.3 %all-to-all-start = ((bf16[64,16,896]{2,1,0:T(8,128)(2,1)}), bf16[64,16,896]{2,1,0:T(8,128)(2,1)S(1)}, u32[]{:S(2)}, u32[]{:S(2)}) async-start(bf16[64,16,896]{2,1,0:T(8,128)(2,1)} %gather_fusion), calls=%async_computation | async-start | bytes 3670016 | tf_op jit(solution)/shard_map/all_to_all | solution.py:295
  23.8 0.1 fusion.1
  24.1 0.8 dynamic_slice.12
  24.9 0.7 stack.35.order_ref
  25.8 42.6 %all-to-all-done = bf16[64,16,896]{2,1,0:T(8,128)(2,1)S(1)} async-done(((bf16[64,16,896]{2,1,0:T(8,128)(2,1)}), bf16[64,16,896]{2,1,0:T(8,128)(2,1)S(1)}, u32[]{:S(2)}, u32[]{:S(2)}) %all-to-all-start) | async-done | bytes 1835040 | tf_op jit(solution)/shard_map/all_to_all | solution.py:295
  68.3 1.4 gather_fusion.2
  69.8 0.6 gather_fusion.1
  70.4 1.7 collective-permute-start.1
  72.1 0.4 collective-permute-start
  72.5 8.5 %collective-permute-done.1.refs_2_ = bf16[16,16,896]{2,1,0:T(8,128)(2,1)S(1)} collective-permute-done((bf16[16,16,896]{2,1,0:T(8,128)(2,1)S(1)}, bf16[16,16,896]{2,1,0:T(8,128)(2,1)S(1)}, u32[]{:S(2)}, u32[]{:S(2)}) %collective-permute-start.1) | collective-permute-done | bytes 458784 | tf_op jit(solution)/shard_map/ppermute | solution.py:39
  81.1 1.7 collective-permute-start.2
  82.8 1.7 collective-permute-start.3
  84.5 0.5 collective-permute-start.6
  85.0 8.1 %collective-permute-done.2.refs_3_ = bf16[8,16,896]{2,1,0:T(8,128)(2,1)S(1)} collective-permute-done((bf16[8,16,896]{2,1,0:T(8,128)(2,1)S(1)}, bf16[8,16,896]{2,1,0:T(8,128)(2,1)S(1)}, u32[]{:S(2)}, u32[]{:S(2)}) %collective-permute-start.2) | collective-permute-done | bytes 229408 | tf_op jit(solution)/shard_map/ppermute | solution.py:41
  93.1 1.6 collective-permute-done.3.refs_4_
  94.7 0.6 fusion.4
  95.3 0.9 collective-permute-done.8.refs_9_
  96.3 0.6 copy-done.13
  96.9 0.2 copy-done.8
  97.1 0.2 copy-done.9
  97.2 13.8 %attention.2 = (bf16[512,256]{1,0:T(8,128)(2,1)}, bf16[512,256]{1,0:T(8,128)(2,1)}, bf16[8,32,16,896]{3,2,1,0:T(8,128)(2,1)}, f32[896,512]{1,0:T(8,128)}) custom-call(s32[8]{0:T(128)} %get-tuple-element.43.count_ref, s32[8]{0:T(128)} %stack.35.order_ref, bf16[16,16,896]{2,1,0:T(8,128)(2,1)} %copy-done.2, bf16[16,16,896]{2,1,0:T(8,128)(2,1)} %copy-done.6, ...), custom_call_target="tpu_custom_call" | custom-call | flops 8589934592 | bytes 16777216 | tf_op jit(solution)/shard_map/attention/pallas_call | solution.py:218
  111.1 13.5 %attention.3 = (bf16[512,256]{1,0:T(8,128)(2,1)}, bf16[512,256]{1,0:T(8,128)(2,1)}, bf16[8,32,16,896]{3,2,1,0:T(8,128)(2,1)}, bf16[4,896,128]{2,1,0:T(8,128)(2,1)}) custom-call(s32[8]{0:T(128)} %get-tuple-element.44.count_ref, s32[8]{0:T(128)} %stack.35.order_ref, bf16[8,16,16,896]{3,2,1,0:T(8,128)(2,1)} %bitcast.23, ...), custom_call_target="tpu_custom_call", output_to_operand_aliasing={{2}: (4, {})} | custom-call | flops 8589934592 | bytes 16777216 | tf_op jit(solution)/shard_map/attention/pallas_call | solution.py:218
  124.6 1.1 copy-done.1
  125.8 22.8 %all_to_all.25 = bf16[4,896,128]{2,1,0:T(8,128)(2,1)S(1)} all-to-all(bf16[4,896,128]{2,1,0:T(8,128)(2,1)S(1)} %copy-done.1), channel_id=1, replica_groups=mesh['z'=8,'x'=4,'y'=4,'core'=2] {'x'}, dimensions={0} | all-to-all | bytes 1835008 | tf_op jit(solution)/shard_map/all_to_all | solution.py:55
  148.6 0.1 add_convert_fusion
  148.7 12.8 %all_to_all.26 = bf16[8,112,128]{2,1,0:T(8,128)(2,1)S(1)} all-to-all(bf16[8,112,128]{2,1,0:T(8,128)(2,1)S(1)} %bitcast.22), channel_id=1, replica_groups=mesh['z'=8,'x'=4,'y'=4,'core'=2] {'z'}, dimensions={0} | all-to-all | bytes 458752 | tf_op jit(solution)/shard_map/all_to_all | solution.py:57
  161.5 0.7 broadcast_in_dim.67
  162.3 3.4 %all-to-all-start.3 = ((bf16[8,112,128]{2,1,0:T(8,128)(2,1)}), bf16[8,112,128]{2,1,0:T(8,128)(2,1)S(1)}, u32[]{:S(2)}, u32[]{:S(2)}) async-start(bf16[8,112,128]{2,1,0:T(8,128)(2,1)} %broadcast_in_dim.67), calls=%async_computation.4 | async-start | bytes 458752 | tf_op jit(solution)/shard_map/all_to_all | solution.py:60
  165.7 9.7 %reduce-scatter.2.cloned.1.call-done = bf16[1,32,16,896]{3,2,1,0:T(8,128)(2,1)} async-done(((bf16[8,32,16,896]{3,2,1,0:T(8,128)(2,1)}), bf16[1,32,16,896]{3,2,1,0:T(8,128)(2,1)}) %reduce-scatter.2.cloned.1.call-update) | async-done | bytes 917520 | tf_op jit(solution)/shard_map/reduce_scatter | solution.py:344
  175.3 3.2 %gather_fusion.3 = bf16[64,16,896]{2,1,0:T(8,128)(2,1)} fusion(bf16[32,16,896]{2,1,0:T(8,128)(2,1)} %bitcast.21, s32[1024]{0:T(1024)S(1)} %pad_clamp_fusion), kind=kCustom, calls=%fused_computation.3 | custom fusion | bytes 3670272 | tf_op jit(solution)/shard_map/jit(_take)/gather | solution.py:323
  178.5 10.2 %all-to-all-start.4 = ((bf16[64,16,896]{2,1,0:T(8,128)(2,1)}), bf16[64,16,896]{2,1,0:T(8,128)(2,1)S(1)}, u32[]{:S(2)}, u32[]{:S(2)}) async-start(bf16[64,16,896]{2,1,0:T(8,128)(2,1)} %gather_fusion.3), calls=%async_computation.5 | async-start | bytes 3670016 | tf_op jit(solution)/shard_map/all_to_all | solution.py:295
  188.7 3.4 %collective-permute-start.10 = (bf16[896,128]{1,0:T(8,128)(2,1)S(1)}, bf16[896,128]{1,0:T(8,128)(2,1)S(1)}, u32[]{:S(2)}, u32[]{:S(2)}) collective-permute-start(bf16[896,128]{1,0:T(8,128)(2,1)S(1)} %bitcast.17), channel_id=1, source_target_pairs={{0,16},{8,24},{16,0},{24,8},{1,17},{9,25},{17,1},{25,9},{2,18},{10... | collective-permute-start | bytes 688136 | tf_op jit(solution)/shard_map/ppermute | solution.py:276
  192.0 1.2 collective-permute-start.11
  193.2 0.9 collective-permute-start.9
  194.1 2.1 pad_maximum_fusion
  196.1 12.7 %collective-permute-done.10.refs_2_ = bf16[896,128]{1,0:T(8,128)(2,1)S(1)} collective-permute-done((bf16[896,128]{1,0:T(8,128)(2,1)S(1)}, bf16[896,128]{1,0:T(8,128)(2,1)S(1)}, u32[]{:S(2)}, u32[]{:S(2)}) %collective-permute-start.10) | collective-permute-done | bytes 229408 | tf_op jit(solution)/shard_map/ppermute | solution.py:276
  208.8 5.6 %collective-permute-done.11.refs_3_ = bf16[896,128]{1,0:T(8,128)(2,1)S(1)} collective-permute-done((bf16[896,128]{1,0:T(8,128)(2,1)S(1)}, bf16[896,128]{1,0:T(8,128)(2,1)S(1)}, u32[]{:S(2)}, u32[]{:S(2)}) %collective-permute-start.11) | collective-permute-done | bytes 229408 | tf_op jit(solution)/shard_map/ppermute | solution.py:276
  214.4 1.2 collective-permute-done.9.refs_1_
  215.6 1.4 spread.1
  217.1 18.6 %all-to-all-done.4.arrived_ref = bf16[64,16,896]{2,1,0:T(8,128)(2,1)S(1)} async-done(((bf16[64,16,896]{2,1,0:T(8,128)(2,1)}), bf16[64,16,896]{2,1,0:T(8,128)(2,1)S(1)}, u32[]{:S(2)}, u32[]{:S(2)}) %all-to-all-start.4) | async-done | bytes 1835040 | tf_op jit(solution)/shard_map/all_to_all | solution.py:295
  235.6 2.9 %collect.1 = f32[32,16,896]{2,1,0:T(8,128)} custom-call(s32[64]{0:T(128)S(1)} %reshape.70.slot_ref, s32[64]{0:T(128)S(1)} %reshape.67.filled_ref, bf16[64,16,896]{2,1,0:T(8,128)(2,1)S(1)} %all-to-all-done.4.arrived_ref), custom_call_target="tpu_custom_call" | custom-call | tf_op jit(solution)/shard_map/collect/pallas_call | solution.py:252
  (56 shorter events, 0.9 us)
Async XLA Ops:
  7.2 3.2 %copy-start = (bf16[32,16,896]{2,1,0:T(8,128)(2,1)S(1)}, bf16[32,16,896]{2,1,0:T(8,128)(2,1)}, u32[]{:S(2)}) copy-start(bf16[32,16,896]{2,1,0:T(8,128)(2,1)} %param.9) | copy-start | bytes 2752516
  12.4 56.0 %all-to-all-start = ((bf16[64,16,896]{2,1,0:T(8,128)(2,1)}), bf16[64,16,896]{2,1,0:T(8,128)(2,1)S(1)}, u32[]{:S(2)}, u32[]{:S(2)}) async-start(bf16[64,16,896]{2,1,0:T(8,128)(2,1)} %gather_fusion), calls=%async_computation | async-start | bytes 3670016 | tf_op jit(solution)/shard_map/all_to_all | solution.py:295
  23.7 87.3 %all-gather.3.cloned.1.call-start = ((), (), s32[]{:S(2)}) async-start(), calls=%async_computation.7 | async-start | bytes 4128768 | tf_op jit(solution)/shard_map/all_gather | solution.py:336
  69.7 105.6 %reduce-scatter.2.cloned.1.call-start = ((), (), s32[]{:S(2)}) async-start(), calls=%async_computation.6 | async-start | bytes 8257536 | tf_op jit(solution)/shard_map/reduce_scatter | solution.py:344
  70.4 25.8 %copy-start.2 = (bf16[16,16,896]{2,1,0:T(8,128)(2,1)}, bf16[16,16,896]{2,1,0:T(8,128)(2,1)S(1)}, u32[]{:S(2)}) copy-start(bf16[16,16,896]{2,1,0:T(8,128)(2,1)S(1)} %gather_fusion.1) | copy-start | bytes 1376260
  70.4 10.6 %collective-permute-start.1 = (bf16[16,16,896]{2,1,0:T(8,128)(2,1)S(1)}, bf16[16,16,896]{2,1,0:T(8,128)(2,1)S(1)}, u32[]{:S(2)}, u32[]{:S(2)}) collective-permute-start(bf16[16,16,896]{2,1,0:T(8,128)(2,1)S(1)} %gather_fusion.1), channel_id=1, source_target_pairs={{0,2},{2,4},{4,6},{6,0},{1,3},{3,5},{5,7},{7,1},{8,10},{10,12},{12... | collective-permute-start | bytes 1376264 | tf_op jit(solution)/shard_map/ppermute | solution.py:39
  72.1 10.7 %collective-permute-start = (bf16[16,16,896]{2,1,0:T(8,128)(2,1)S(1)}, bf16[16,16,896]{2,1,0:T(8,128)(2,1)S(1)}, u32[]{:S(2)}, u32[]{:S(2)}) collective-permute-start(bf16[16,16,896]{2,1,0:T(8,128)(2,1)S(1)} %gather_fusion.1), channel_id=1, source_target_pairs={{2,0},{4,2},{6,4},{0,6},{3,1},{5,3},{7,5},{1,7},{10,8},{12,10},{14... | collective-permute-start | bytes 1376264 | tf_op jit(solution)/shard_map/ppermute | solution.py:40
  72.5 22.8 %collective-permute-start.4 = (bf16[16,16,896]{2,1,0:T(8,128)(2,1)S(1)}, bf16[16,16,896]{2,1,0:T(8,128)(2,1)S(1)}, u32[]{:S(2)}, u32[]{:S(2)}) collective-permute-start(bf16[16,16,896]{2,1,0:T(8,128)(2,1)S(1)} %gather_fusion.1), channel_id=1, source_target_pairs={{0,1},{1,0},{2,3},{3,2},{4,5},{5,4},{6,7},{7,6},{8,9},{9,8},{10,11... | collective-permute-start | bytes 1376264 | tf_op jit(solution)/shard_map/ppermute | solution.py:44
  81.1 15.2 %copy-start.5 = (bf16[16,16,896]{2,1,0:T(8,128)(2,1)}, bf16[16,16,896]{2,1,0:T(8,128)(2,1)S(1)}, u32[]{:S(2)}) copy-start(bf16[16,16,896]{2,1,0:T(8,128)(2,1)S(1)} %collective-permute-done.1.refs_2_) | copy-start | bytes 1376260
  81.1 12.0 %collective-permute-start.2 = (bf16[8,16,896]{2,1,0:T(8,128)(2,1)S(1)}, bf16[8,16,896]{2,1,0:T(8,128)(2,1)S(1)}, u32[]{:S(2)}, u32[]{:S(2)}) collective-permute-start(bf16[8,16,896]{2,1,0:T(8,128)(2,1)S(1)} %slice.80), channel_id=1, source_target_pairs={{0,2},{2,4},{4,6},{6,0},{1,3},{3,5},{5,7},{7,1},{8,10},{10,12},{12... | collective-permute-start | bytes 688136 | tf_op jit(solution)/shard_map/ppermute | solution.py:41
  82.8 13.5 %copy-start.6 = (bf16[16,16,896]{2,1,0:T(8,128)(2,1)}, bf16[16,16,896]{2,1,0:T(8,128)(2,1)S(1)}, u32[]{:S(2)}) copy-start(bf16[16,16,896]{2,1,0:T(8,128)(2,1)S(1)} %collective-permute-done.refs_1_) | copy-start | bytes 1376260
  82.8 11.9 %collective-permute-start.3 = (bf16[8,16,896]{2,1,0:T(8,128)(2,1)S(1)}, bf16[8,16,896]{2,1,0:T(8,128)(2,1)S(1)}, u32[]{:S(2)}, u32[]{:S(2)}) collective-permute-start(bf16[8,16,896]{2,1,0:T(8,128)(2,1)S(1)} %slice.81), channel_id=1, source_target_pairs={{2,0},{4,2},{6,4},{0,6},{3,1},{5,3},{7,5},{1,7},{10,8},{12,10},{14... | collective-permute-start | bytes 688136 | tf_op jit(solution)/shard_map/ppermute | solution.py:42
  84.5 11.7 %collective-permute-start.5 = (bf16[16,16,896]{2,1,0:T(8,128)(2,1)S(1)}, bf16[16,16,896]{2,1,0:T(8,128)(2,1)S(1)}, u32[]{:S(2)}, u32[]{:S(2)}) collective-permute-start(bf16[16,16,896]{2,1,0:T(8,128)(2,1)S(1)} %collective-permute-done.refs_1_), channel_id=1, source_target_pairs={{0,1},{1,0},{2,3},{3,2},{4,5},{5,4},{6,7},{7,6},{8,9},{9,8},{10,11... | collective-permute-start | bytes 1376264 | tf_op jit(solution)/shard_map/ppermute | solution.py:44
  84.5 11.7 %collective-permute-start.6 = (bf16[16,16,896]{2,1,0:T(8,128)(2,1)S(1)}, bf16[16,16,896]{2,1,0:T(8,128)(2,1)S(1)}, u32[]{:S(2)}, u32[]{:S(2)}) collective-permute-start(bf16[16,16,896]{2,1,0:T(8,128)(2,1)S(1)} %collective-permute-done.1.refs_2_), channel_id=1, source_target_pairs={{0,1},{1,0},{2,3},{3,2},{4,5},{5,4},{6,7},{7,6},{8,9},{9,8},{10,11... | collective-permute-start | bytes 1376264 | tf_op jit(solution)/shard_map/ppermute | solution.py:44
  93.1 3.2 %copy-start.10 = (bf16[8,16,896]{2,1,0:T(8,128)(2,1)}, bf16[8,16,896]{2,1,0:T(8,128)(2,1)S(1)}, u32[]{:S(2)}) copy-start(bf16[8,16,896]{2,1,0:T(8,128)(2,1)S(1)} %collective-permute-done.2.refs_3_) | copy-start | bytes 688132
  93.1 2.2 collective-permute-start.7
  94.7 1.6 copy-start.11
  94.7 1.5 collective-permute-start.8
  95.3 1.0 copy-start.7
  95.3 1.0 copy-start.12
  96.2 0.7 copy-start.13
  96.2 0.8 copy-start.8
  96.2 1.0 copy-start.9
  124.6 1.2 copy-start.1
  162.3 16.2 %all-to-all-start.3 = ((bf16[8,112,128]{2,1,0:T(8,128)(2,1)}), bf16[8,112,128]{2,1,0:T(8,128)(2,1)S(1)}, u32[]{:S(2)}, u32[]{:S(2)}) async-start(bf16[8,112,128]{2,1,0:T(8,128)(2,1)} %broadcast_in_dim.67), calls=%async_computation.4 | async-start | bytes 458752 | tf_op jit(solution)/shard_map/all_to_all | solution.py:60
  178.5 15.6 %copy-start.3 = (bf16[512,256]{1,0:T(8,128)(2,1)S(1)}, bf16[512,256]{1,0:T(8,128)(2,1)}, u32[]{:S(2)}) copy-start(bf16[512,256]{1,0:T(8,128)(2,1)} %get-tuple-element.26) | copy-start | bytes 786436
  178.5 15.6 %copy-start.4 = (bf16[512,256]{1,0:T(8,128)(2,1)S(1)}, bf16[512,256]{1,0:T(8,128)(2,1)}, u32[]{:S(2)}) copy-start(bf16[512,256]{1,0:T(8,128)(2,1)} %get-tuple-element.30) | copy-start | bytes 786436
  178.5 57.1 %all-to-all-start.4 = ((bf16[64,16,896]{2,1,0:T(8,128)(2,1)}), bf16[64,16,896]{2,1,0:T(8,128)(2,1)S(1)}, u32[]{:S(2)}, u32[]{:S(2)}) async-start(bf16[64,16,896]{2,1,0:T(8,128)(2,1)} %gather_fusion.3), calls=%async_computation.5 | async-start | bytes 3670016 | tf_op jit(solution)/shard_map/all_to_all | solution.py:295
  188.7 20.2 %collective-permute-start.10 = (bf16[896,128]{1,0:T(8,128)(2,1)S(1)}, bf16[896,128]{1,0:T(8,128)(2,1)S(1)}, u32[]{:S(2)}, u32[]{:S(2)}) collective-permute-start(bf16[896,128]{1,0:T(8,128)(2,1)S(1)} %bitcast.17), channel_id=1, source_target_pairs={{0,16},{8,24},{16,0},{24,8},{1,17},{9,25},{17,1},{25,9},{2,18},{10... | collective-permute-start | bytes 688136 | tf_op jit(solution)/shard_map/ppermute | solution.py:276
  192.0 22.4 %collective-permute-start.11 = (bf16[896,128]{1,0:T(8,128)(2,1)S(1)}, bf16[896,128]{1,0:T(8,128)(2,1)S(1)}, u32[]{:S(2)}, u32[]{:S(2)}) collective-permute-start(bf16[896,128]{1,0:T(8,128)(2,1)S(1)} %bitcast.18), channel_id=1, source_target_pairs={{0,24},{8,0},{16,8},{24,16},{1,25},{9,1},{17,9},{25,17},{2,26},{10... | collective-permute-start | bytes 688136 | tf_op jit(solution)/shard_map/ppermute | solution.py:276
  193.2 22.4 %collective-permute-start.9 = (bf16[896,128]{1,0:T(8,128)(2,1)S(1)}, bf16[896,128]{1,0:T(8,128)(2,1)S(1)}, u32[]{:S(2)}, u32[]{:S(2)}) collective-permute-start(bf16[896,128]{1,0:T(8,128)(2,1)S(1)} %bitcast.19), channel_id=1, source_target_pairs={{0,8},{8,16},{16,24},{24,0},{1,9},{9,17},{17,25},{25,1},{2,10},{10... | collective-permute-start | bytes 688136 | tf_op jit(solution)/shard_map/ppermute | solution.py:276
Sparse Core Ops, SparseCore 0:
  69.8 33.5 all-gather.2
  124.7 50.5 reduce-scatter.1

commit v5 on v3

--- a/solution.py
+++ b/solution.py
@@ -54,27 +54,25 @@
 def scatter_and_reduce(mine, other, parts):
     half = mine.shape[1] // 2
     swapped = lax.ppermute(other, "core", SWAP)
+    far = plus(mine[3], swapped[3]).astype(BF16)
+    far, parts = lax.optimization_barrier((far, parts))
+    got_low = lax.ppermute(far[:half], "y", UP)
+    got_high = lax.ppermute(far[half:], "y", DOWN)
     by_x = lax.all_to_all(parts, "x", split_axis=0, concat_axis=0, tiled=True)
     part = plus(*[by_x[k] for k in range(4)]).astype(BF16).reshape(8, -1, DH)
-    far = plus(mine[3], swapped[3]).astype(BF16)
-    far, part = lax.optimization_barrier((far, part))
-    got_low = lax.ppermute(far[:half], "y", UP)
-    got_high = lax.ppermute(far[half:], "y", DOWN)
-    by_z = lax.all_to_all(part, "z", split_axis=0, concat_axis=0, tiled=True)
     up_low = plus(mine[1, :half], swapped[1, :half], got_low).astype(BF16)
     up_high = plus(mine[1, half:], swapped[1, half:]).astype(BF16)
     down_low = plus(mine[2, :half], swapped[2, :half]).astype(BF16)
     down_high = plus(mine[2, half:], swapped[2, half:], got_high).astype(BF16)
     up = jnp.concatenate([up_low, up_high])
     down = jnp.concatenate([down_low, down_high])
-    total = plus(*[by_z[k] for k in range(8)]).astype(BF16)
-    up, down, total = lax.optimization_barrier((up, down, total))
+    up, down, part = lax.optimization_barrier((up, down, part))
     from_below = lax.ppermute(up, "y", UP)
     from_above = lax.ppermute(down, "y", DOWN)
-    column = jnp.broadcast_to(total[None], part.shape)
-    column = lax.all_to_all(column, "z", split_axis=0, concat_axis=0, tiled=True)
+    by_z = lax.all_to_all(part, "z", split_axis=0, concat_axis=0, tiled=True)
+    total = plus(*[by_z[k] for k in range(8)]).astype(BF16)
     summed = plus(mine[0], swapped[0], from_below, from_above).astype(BF16)
-    return summed, column.reshape(-1, DH)
+    return summed, total
 
 
 def fill_from_pieces(step, refs, rows_ref):
@@ -286,13 +284,23 @@
 
 def spread_kernel(place_ref, *refs):
     pieces, (key_ref, value_ref, held_ref) = refs[:4], refs[4:]
+    x, z = place_ref[0], place_ref[1]
+    rows = key_ref.shape[0] // 8
     for k in range(4):
-        held_ref[lax.rem(place_ref[0] - k + 4, 4)] = pieces[k][...].astype(F32)
+        group = lax.rem(x - k + 4, 4)
+        for j in range(8):
+            at = pl.multiple_of(jnp.bitwise_xor(z, j) * rows, 16)
+            part = pieces[k][j * rows : (j + 1) * rows, :]
+            held_ref[group, pl.ds(at, rows), :] = part.astype(F32)
     key_ref[:, :DH], key_ref[:, DH:] = held_ref[0], held_ref[1]
     value_ref[:, :DH], value_ref[:, DH:] = held_ref[2], held_ref[3]
 
 
-def spread_columns(column, place):
+def spread_columns(block, place):
+    column = block
+    for bit in (1, 2, 4):
+        swap = [(i, i ^ bit) for i in range(8)]
+        column = jnp.concatenate([column, lax.ppermute(column, "z", swap)])
     width = column.shape[0]
     pieces = [column] + [lax.ppermute(column, "x", shift(4, k)) for k in (1, 3, 2)]
     pieces = [pieces[0], pieces[1], pieces[3], pieces[2]]
@@ -348,7 +356,7 @@
     order = jnp.stack(
         [(y + dy) % 4 * 2 + (core + other) % 2 for other in (0, 1) for dy in (0, 1, 3, 2)]
     ).astype(jnp.int32)
-    place = lax.axis_index("x").astype(jnp.int32).reshape(1)
+    place = jnp.stack([lax.axis_index("x"), lax.axis_index("z")]).astype(jnp.int32)
     positions, back, counts, order, filled, place = lax.optimization_barrier(
         (positions, back, counts, order, filled, place)
     )
@@ -363,11 +371,11 @@
     attended_1, grad_queries_1, mine, other, parts = attention(
         counts[HALF:], order, gathered, *weights, 1, begun
     )
-    summed_1, column = scatter_and_reduce(mine, other, parts)
+    summed_1, total = scatter_and_reduce(mine, other, parts)
     returning = take(jnp.concatenate([summed_0, summed_1]), back)
-    returning, column = lax.optimization_barrier((returning, column))
+    returning, total = lax.optimization_barrier((returning, total))
     arrived = exchange(returning)
-    grad_w_key, grad_w_value = spread_columns(column, place)
+    grad_w_key, grad_w_value = spread_columns(total, place)
     grad_pool = collect(picked_slot, filled, arrived, pool.shape[0])
     return (
         jnp.concatenate([attended_0, attended_1]),

time: 246 us -> 269 us (1.093)
  waiting for transfers between devices: 109 us -> 138 us
  blocking collectives: 23.9 us -> 0 us
  starting transfers between devices: 41.2 us -> 57.5 us
    ppermute x0 -> x3, waiting for transfers between devices: none -> 45.9 us  [spread_columns(): column = jnp.concatenate([column, lax.ppermute(column, 'z', swap)])]
    all_to_all x1 -> x0, blocking collectives: 23.9 us -> none  [scatter_and_reduce(): by_x = lax.all_to_all(parts, 'x', split_axis=0, concat_axis=0, tiled=True)]
    all_to_all x2, waiting for transfers between devices: 58.8 us -> 42.5 us  [exchange(): lax.all_to_all(array, ('z', 'x'), split_axis=0, concat_axis=0, tiled=True)]
    ppermute x3, waiting for transfers between devices: 17 us -> 5.79 us  [spread_columns(): lax.ppermute(column, 'x', shift(4, k))]
    ppermute x0 -> x3, starting transfers between devices: none -> 8.2 us  [spread_columns(): column = jnp.concatenate([column, lax.ppermute(column, 'z', swap)])]
    all_to_all x1, waiting for transfers between devices: 0.01 us -> 8.04 us  [scatter_and_reduce(): by_z = lax.all_to_all(part, 'z', split_axis=0, concat_axis=0, tiled=True)]
    all_to_all x2, starting transfers between devices: 15.4 us -> 21 us  [exchange(): lax.all_to_all(array, ('z', 'x'), split_axis=0, concat_axis=0, tiled=True)]
    all_to_all x1, waiting for transfers between devices: 4.09 us -> 0.01 us  [scatter_and_reduce(): by_x = lax.all_to_all(parts, 'x', split_axis=0, concat_axis=0, tiled=True)]
  transfers between devices with their start and end apart: 23 -> 26, of which waited for: 12 -> 17; matrix products, arithmetic and copies ran while one was open for 6% -> 5% of each run, Pallas kernels for 12% -> 11%
where the time goes in v5:
time: 269 us; the launch traced here: 266 us
  waiting for transfers between devices  138 us (51%)
  starting transfers between devices  57.5 us (21%)
  Pallas kernels  32.2 us (12%)
  between operations  14.4 us (5%)
  local copies, waits for them, and re-layouts  12.7 us (5%)
  other arithmetic  11.6 us (4%)
    ppermute x3, waiting for transfers between devices, spread_columns(): column = jnp.concatenate([column, lax.ppermute(column, 'z', swap)])  45.9 us
    all_to_all x2, waiting for transfers between devices, exchange(): lax.all_to_all(array, ('z', 'x'), split_axis=0, concat_axis=0, tiled=True)  42.5 us
    pallas_call x2, Pallas kernels, attention(): pl.pallas_call(functools.partial(attention_kernel, first), grid_spec=pltp...  27.3 us
    all_to_all x2, starting transfers between devices, exchange(): lax.all_to_all(array, ('z', 'x'), split_axis=0, concat_axis=0, tiled=True)  21 us
    all_to_all x1, starting transfers between devices, scatter_and_reduce(): by_x = lax.all_to_all(parts, 'x', split_axis=0, concat_axis=0, tiled=True)  9.52 us
    ppermute x1, waiting for transfers between devices, gather_pieces(): far_low = lax.ppermute(below[:half], 'y', UP)  8.96 us
    ppermute x1, waiting for transfers between devices, gather_pieces(): below = lax.ppermute(own, 'y', UP)  8.53 us
    ppermute x3, starting transfers between devices, spread_columns(): column = jnp.concatenate([column, lax.ppermute(column, 'z', swap)])  8.2 us
  transfers between devices with their start and end apart: 26, of which 17 were waited for; matrix products, arithmetic and copies ran while one was open for 5% of the time, Pallas kernels for 11%

profile of v5, /device:TPU:8, one launch (start us, length us, event | category | flops | bytes accessed | tf_op | source)
XLA Modules:
  0.0 266.4 jit_solution(12431937170098699255)
XLA Ops:
  7.2 0.9 copy.17
  10.4 2.0 gather_fusion
  12.4 11.3 %all-to-all-start = ((bf16[64,16,896]{2,1,0:T(8,128)(2,1)}), bf16[64,16,896]{2,1,0:T(8,128)(2,1)S(1)}, u32[]{:S(2)}, u32[]{:S(2)}) async-start(bf16[64,16,896]{2,1,0:T(8,128)(2,1)} %gather_fusion), calls=%async_computation | async-start | bytes 3670016 | tf_op jit(solution)/shard_map/all_to_all | solution.py:324
  25.8 42.5 %all-to-all-done = bf16[64,16,896]{2,1,0:T(8,128)(2,1)S(1)} async-done(((bf16[64,16,896]{2,1,0:T(8,128)(2,1)}), bf16[64,16,896]{2,1,0:T(8,128)(2,1)S(1)}, u32[]{:S(2)}, u32[]{:S(2)}) %all-to-all-start) | async-done | bytes 1835040 | tf_op jit(solution)/shard_map/all_to_all | solution.py:324
  68.3 1.4 gather_fusion.2
  70.4 1.7 collective-permute-start.1
  72.5 8.5 %collective-permute-done.1.refs_2_ = bf16[16,16,896]{2,1,0:T(8,128)(2,1)S(1)} collective-permute-done((bf16[16,16,896]{2,1,0:T(8,128)(2,1)S(1)}, bf16[16,16,896]{2,1,0:T(8,128)(2,1)S(1)}, u32[]{:S(2)}, u32[]{:S(2)}) %collective-permute-start.1) | collective-permute-done | bytes 458784 | tf_op jit(solution)/shard_map/ppermute | solution.py:39
  81.1 1.7 collective-permute-start.2
  82.8 1.3 collective-permute-start.3
  84.1 9.0 %collective-permute-done.2.refs_3_ = bf16[8,16,896]{2,1,0:T(8,128)(2,1)S(1)} collective-permute-done((bf16[8,16,896]{2,1,0:T(8,128)(2,1)S(1)}, bf16[8,16,896]{2,1,0:T(8,128)(2,1)S(1)}, u32[]{:S(2)}, u32[]{:S(2)}) %collective-permute-start.2) | collective-permute-done | bytes 229408 | tf_op jit(solution)/shard_map/ppermute | solution.py:41
  93.1 3.0 %collective-permute-done.3.refs_4_ = bf16[8,16,896]{2,1,0:T(8,128)(2,1)S(1)} collective-permute-done((bf16[8,16,896]{2,1,0:T(8,128)(2,1)S(1)}, bf16[8,16,896]{2,1,0:T(8,128)(2,1)S(1)}, u32[]{:S(2)}, u32[]{:S(2)}) %collective-permute-start.3) | collective-permute-done | bytes 229408 | tf_op jit(solution)/shard_map/ppermute | solution.py:42
  96.7 0.8 collective-permute-done.8.refs_9_
  98.5 13.8 %attention.2 = (bf16[512,256]{1,0:T(8,128)(2,1)}, bf16[512,256]{1,0:T(8,128)(2,1)}, bf16[8,16,16,896]{3,2,1,0:T(8,128)(2,1)}, f32[896,512]{1,0:T(8,128)}) custom-call(s32[8]{0:T(128)} %get-tuple-element.61.count_ref, s32[8]{0:T(128)} %stack.44.order_ref, bf16[16,16,896]{2,1,0:T(8,128)(2,1)} %copy-done.2, bf16[16,16,896]{2,1,0:T(8,128)(2,1)} %copy-done.6, ...), custom_call_target="tpu_custom_call" | custom-call | flops 8589934592 | bytes 16777216 | tf_op jit(solution)/shard_map/attention/pallas_call | solution.py:238
  112.3 13.5 %attention.3 = (bf16[512,256]{1,0:T(8,128)(2,1)}, bf16[512,256]{1,0:T(8,128)(2,1)}, bf16[4,16,16,896]{3,2,1,0:T(8,128)(2,1)}, bf16[4,16,16,896]{3,2,1,0:T(8,128)(2,1)}, bf16[4,896,128]{2,1,0:T(8,128)(2,1)}) custom-call(s32[8]{0:T(128)} %get-tuple-element.62.count_ref, s32[8]{0:T(128)} %stack.44.order_ref, bf16[8,16,16,896]{3,2,1,0:T(8,128)(2,1)} %bitcast.38, ...), custom_call_target="tpu_custom_call" | custom-call | flops 8589934592 | bytes 16777216 | tf_op jit(solution)/shard_map/attention/pallas_call | solution.py:238
  126.0 3.9 %collective-permute-done.9 = bf16[4,16,16,896]{3,2,1,0:T(8,128)(2,1)S(1)} collective-permute-done((bf16[4,16,16,896]{3,2,1,0:T(8,128)(2,1)}, bf16[4,16,16,896]{3,2,1,0:T(8,128)(2,1)S(1)}, u32[]{:S(2)}, u32[]{:S(2)}) %collective-permute-start.9) | collective-permute-done | bytes 1835040 | tf_op jit(solution)/shard_map/ppermute | solution.py:56
  129.9 1.2 copy-done.1
  131.1 1.2 fusion.2
  132.3 9.5 %all-to-all-start.1 = ((bf16[4,896,128]{2,1,0:T(8,128)(2,1)}), bf16[4,896,128]{2,1,0:T(8,128)(2,1)S(1)}, u32[]{:S(2)}, u32[]{:S(2)}) async-start(bf16[4,896,128]{2,1,0:T(8,128)(2,1)} %get-tuple-element.43), calls=%async_computation.2 | async-start | bytes 1835008 | tf_op jit(solution)/shard_map/all_to_all | solution.py:61
  141.8 0.9 collective-permute-start.11
  142.7 1.2 collective-permute-start.10
  143.9 1.4 fusion.6
  145.4 7.0 %collective-permute-done.11 = bf16[8,16,896]{2,1,0:T(8,128)(2,1)S(1)} collective-permute-done((bf16[8,16,896]{2,1,0:T(8,128)(2,1)S(1)}, bf16[8,16,896]{2,1,0:T(8,128)(2,1)S(1)}, u32[]{:S(2)}, u32[]{:S(2)}) %collective-permute-start.11) | collective-permute-done | bytes 229408 | tf_op jit(solution)/shard_map/ppermute | solution.py:60
  152.3 1.9 collective-permute-done.10
  154.2 1.5 fusion.3
  155.6 0.9 pad_maximum_fusion.3
  157.3 3.4 %all-to-all-start.2 = ((bf16[8,112,128]{2,1,0:T(8,128)(2,1)}), bf16[8,112,128]{2,1,0:T(8,128)(2,1)S(1)}, u32[]{:S(2)}, u32[]{:S(2)}) async-start(bf16[8,112,128]{2,1,0:T(8,128)(2,1)} %bitcast.19), calls=%async_computation.3 | async-start | bytes 458752 | tf_op jit(solution)/shard_map/all_to_all | solution.py:72
  161.5 2.4 collective-permute-start.13
  163.9 8.0 %all-to-all-done.2 = bf16[8,112,128]{2,1,0:T(8,128)(2,1)S(1)} async-done(((bf16[8,112,128]{2,1,0:T(8,128)(2,1)}), bf16[8,112,128]{2,1,0:T(8,128)(2,1)S(1)}, u32[]{:S(2)}, u32[]{:S(2)}) %all-to-all-start.2) | async-done | bytes 229408 | tf_op jit(solution)/shard_map/all_to_all | solution.py:72
  172.0 1.2 collective-permute-done.12
  173.7 1.4 fusion.1
  175.2 1.1 pad_maximum_fusion
  176.3 2.0 gather_fusion.3
  178.3 9.7 %all-to-all-start.3 = ((bf16[64,16,896]{2,1,0:T(8,128)(2,1)}), bf16[64,16,896]{2,1,0:T(8,128)(2,1)S(1)}, u32[]{:S(2)}, u32[]{:S(2)}) async-start(bf16[64,16,896]{2,1,0:T(8,128)(2,1)} %gather_fusion.3), calls=%async_computation.4 | async-start | bytes 3670016 | tf_op jit(solution)/shard_map/all_to_all | solution.py:324
  188.0 1.9 collective-permute-start.14
  189.9 37.5 %collective-permute-done.14 = bf16[112,128]{1,0:T(8,128)(2,1)S(1)} collective-permute-done((bf16[112,128]{1,0:T(8,128)(2,1)S(1)}, bf16[112,128]{1,0:T(8,128)(2,1)S(1)}, u32[]{:S(2)}, u32[]{:S(2)}) %collective-permute-start.14) | collective-permute-done | bytes 28704 | tf_op jit(solution)/shard_map/ppermute | solution.py:303
  227.4 1.4 collective-permute-start.15
  228.8 4.3 %collective-permute-done.15 = bf16[224,128]{1,0:T(8,128)(2,1)S(1)} collective-permute-done((bf16[224,128]{1,0:T(8,128)(2,1)S(1)}, bf16[224,128]{1,0:T(8,128)(2,1)S(1)}, u32[]{:S(2)}, u32[]{:S(2)}) %collective-permute-start.15) | collective-permute-done | bytes 57376 | tf_op jit(solution)/shard_map/ppermute | solution.py:303
  233.1 4.9 %collective-permute-start.16 = (bf16[448,128]{1,0:T(8,128)(2,1)S(1)}, bf16[448,128]{1,0:T(8,128)(2,1)S(1)}, u32[]{:S(2)}, u32[]{:S(2)}) collective-permute-start(bf16[448,128]{1,0:T(8,128)(2,1)S(1)} %pad_maximum_fusion.5), channel_id=1, source_target_pairs={{0,128},{32,160},{64,192},{96,224},{128,0},{160,32},{192,64},{224,... | collective-permute-start | bytes 344072 | tf_op jit(solution)/shard_map/ppermute | solution.py:303
  238.0 4.1 %collective-permute-done.16 = bf16[448,128]{1,0:T(8,128)(2,1)S(1)} collective-permute-done((bf16[448,128]{1,0:T(8,128)(2,1)S(1)}, bf16[448,128]{1,0:T(8,128)(2,1)S(1)}, u32[]{:S(2)}, u32[]{:S(2)}) %collective-permute-start.16) | collective-permute-done | bytes 114720 | tf_op jit(solution)/shard_map/ppermute | solution.py:303
  242.1 2.5 collective-permute-start.19
  244.6 1.0 collective-permute-start.18
  245.6 1.2 collective-permute-start.17
  246.8 2.1 pad_maximum_fusion.1
  248.9 2.1 collective-permute-done.19.refs_3_
  251.0 1.4 collective-permute-done.18.refs_2_
  252.3 2.4 collective-permute-done.17.refs_1_
  254.7 2.0 spread.1
  256.6 2.9 %collect.1 = f32[32,16,896]{2,1,0:T(8,128)} custom-call(s32[64]{0:T(128)S(1)} %reshape.105.slot_ref, s32[64]{0:T(128)S(1)} %reshape.95.filled_ref, bf16[64,16,896]{2,1,0:T(8,128)(2,1)S(1)} %all-to-all-done.3.arrived_ref), custom_call_target="tpu_custom_call" | custom-call | tf_op jit(solution)/shard_map/collect/pallas_call | solution.py:271
  (85 shorter events, 9.5 us)
Async XLA Ops:
  7.2 3.2 %copy-start = (bf16[32,16,896]{2,1,0:T(8,128)(2,1)S(1)}, bf16[32,16,896]{2,1,0:T(8,128)(2,1)}, u32[]{:S(2)}) copy-start(bf16[32,16,896]{2,1,0:T(8,128)(2,1)} %param.9) | copy-start | bytes 2752516
  12.4 56.0 %all-to-all-start = ((bf16[64,16,896]{2,1,0:T(8,128)(2,1)}), bf16[64,16,896]{2,1,0:T(8,128)(2,1)S(1)}, u32[]{:S(2)}, u32[]{:S(2)}) async-start(bf16[64,16,896]{2,1,0:T(8,128)(2,1)} %gather_fusion), calls=%async_computation | async-start | bytes 3670016 | tf_op jit(solution)/shard_map/all_to_all | solution.py:324
  23.7 88.6 %all-gather.3.cloned.1.call-start = ((), (), s32[]{:S(2)}) async-start(), calls=%async_computation.6 | async-start | bytes 4128768 | tf_op jit(solution)/shard_map/all_gather | solution.py:365
  69.7 105.4 %reduce-scatter.2.cloned.1.call-start = ((), (), s32[]{:S(2)}) async-start(), calls=%async_computation.5 | async-start | bytes 4128768 | tf_op jit(solution)/shard_map/reduce_scatter | solution.py:370
  70.4 27.2 %copy-start.2 = (bf16[16,16,896]{2,1,0:T(8,128)(2,1)}, bf16[16,16,896]{2,1,0:T(8,128)(2,1)S(1)}, u32[]{:S(2)}) copy-start(bf16[16,16,896]{2,1,0:T(8,128)(2,1)S(1)} %gather_fusion.1) | copy-start | bytes 1376260
  70.4 10.6 %collective-permute-start.1 = (bf16[16,16,896]{2,1,0:T(8,128)(2,1)S(1)}, bf16[16,16,896]{2,1,0:T(8,128)(2,1)S(1)}, u32[]{:S(2)}, u32[]{:S(2)}) collective-permute-start(bf16[16,16,896]{2,1,0:T(8,128)(2,1)S(1)} %gather_fusion.1), channel_id=1, source_target_pairs={{0,2},{2,4},{4,6},{6,0},{1,3},{3,5},{5,7},{7,1},{8,10},{10,12},{12... | collective-permute-start | bytes 1376264 | tf_op jit(solution)/shard_map/ppermute | solution.py:39
  72.1 10.7 %collective-permute-start = (bf16[16,16,896]{2,1,0:T(8,128)(2,1)S(1)}, bf16[16,16,896]{2,1,0:T(8,128)(2,1)S(1)}, u32[]{:S(2)}, u32[]{:S(2)}) collective-permute-start(bf16[16,16,896]{2,1,0:T(8,128)(2,1)S(1)} %gather_fusion.1), channel_id=1, source_target_pairs={{2,0},{4,2},{6,4},{0,6},{3,1},{5,3},{7,5},{1,7},{10,8},{12,10},{14... | collective-permute-start | bytes 1376264 | tf_op jit(solution)/shard_map/ppermute | solution.py:40
  72.5 24.2 %collective-permute-start.4 = (bf16[16,16,896]{2,1,0:T(8,128)(2,1)S(1)}, bf16[16,16,896]{2,1,0:T(8,128)(2,1)S(1)}, u32[]{:S(2)}, u32[]{:S(2)}) collective-permute-start(bf16[16,16,896]{2,1,0:T(8,128)(2,1)S(1)} %gather_fusion.1), channel_id=1, source_target_pairs={{0,1},{1,0},{2,3},{3,2},{4,5},{5,4},{6,7},{7,6},{8,9},{9,8},{10,11... | collective-permute-start | bytes 1376264 | tf_op jit(solution)/shard_map/ppermute | solution.py:44
  81.1 16.5 %copy-start.5 = (bf16[16,16,896]{2,1,0:T(8,128)(2,1)}, bf16[16,16,896]{2,1,0:T(8,128)(2,1)S(1)}, u32[]{:S(2)}) copy-start(bf16[16,16,896]{2,1,0:T(8,128)(2,1)S(1)} %collective-permute-done.1.refs_2_) | copy-start | bytes 1376260
  81.1 12.0 %collective-permute-start.2 = (bf16[8,16,896]{2,1,0:T(8,128)(2,1)S(1)}, bf16[8,16,896]{2,1,0:T(8,128)(2,1)S(1)}, u32[]{:S(2)}, u32[]{:S(2)}) collective-permute-start(bf16[8,16,896]{2,1,0:T(8,128)(2,1)S(1)} %slice.136), channel_id=1, source_target_pairs={{0,2},{2,4},{4,6},{6,0},{1,3},{3,5},{5,7},{7,1},{8,10},{10,12},{12... | collective-permute-start | bytes 688136 | tf_op jit(solution)/shard_map/ppermute | solution.py:41
  82.8 14.0 %collective-permute-start.6 = (bf16[16,16,896]{2,1,0:T(8,128)(2,1)S(1)}, bf16[16,16,896]{2,1,0:T(8,128)(2,1)S(1)}, u32[]{:S(2)}, u32[]{:S(2)}) collective-permute-start(bf16[16,16,896]{2,1,0:T(8,128)(2,1)S(1)} %collective-permute-done.1.refs_2_), channel_id=1, source_target_pairs={{0,1},{1,0},{2,3},{3,2},{4,5},{5,4},{6,7},{7,6},{8,9},{9,8},{10,11... | collective-permute-start | bytes 1376264 | tf_op jit(solution)/shard_map/ppermute | solution.py:44
  82.8 14.8 %copy-start.6 = (bf16[16,16,896]{2,1,0:T(8,128)(2,1)}, bf16[16,16,896]{2,1,0:T(8,128)(2,1)S(1)}, u32[]{:S(2)}) copy-start(bf16[16,16,896]{2,1,0:T(8,128)(2,1)S(1)} %collective-permute-done.refs_1_) | copy-start | bytes 1376260
  82.8 13.3 %collective-permute-start.3 = (bf16[8,16,896]{2,1,0:T(8,128)(2,1)S(1)}, bf16[8,16,896]{2,1,0:T(8,128)(2,1)S(1)}, u32[]{:S(2)}, u32[]{:S(2)}) collective-permute-start(bf16[8,16,896]{2,1,0:T(8,128)(2,1)S(1)} %slice.137), channel_id=1, source_target_pairs={{2,0},{4,2},{6,4},{0,6},{3,1},{5,3},{7,5},{1,7},{10,8},{12,10},{14... | collective-permute-start | bytes 688136 | tf_op jit(solution)/shard_map/ppermute | solution.py:42
  84.1 13.4 %collective-permute-start.5 = (bf16[16,16,896]{2,1,0:T(8,128)(2,1)S(1)}, bf16[16,16,896]{2,1,0:T(8,128)(2,1)S(1)}, u32[]{:S(2)}, u32[]{:S(2)}) collective-permute-start(bf16[16,16,896]{2,1,0:T(8,128)(2,1)S(1)} %collective-permute-done.refs_1_), channel_id=1, source_target_pairs={{0,1},{1,0},{2,3},{3,2},{4,5},{5,4},{6,7},{7,6},{8,9},{9,8},{10,11... | collective-permute-start | bytes 1376264 | tf_op jit(solution)/shard_map/ppermute | solution.py:44
  93.1 4.5 %copy-start.10 = (bf16[8,16,896]{2,1,0:T(8,128)(2,1)}, bf16[8,16,896]{2,1,0:T(8,128)(2,1)S(1)}, u32[]{:S(2)}) copy-start(bf16[8,16,896]{2,1,0:T(8,128)(2,1)S(1)} %collective-permute-done.2.refs_3_) | copy-start | bytes 688132
  93.1 3.6 %collective-permute-start.7 = (bf16[8,16,896]{2,1,0:T(8,128)(2,1)S(1)}, bf16[8,16,896]{2,1,0:T(8,128)(2,1)S(1)}, u32[]{:S(2)}, u32[]{:S(2)}) collective-permute-start(bf16[8,16,896]{2,1,0:T(8,128)(2,1)S(1)} %collective-permute-done.2.refs_3_), channel_id=1, source_target_pairs={{0,1},{1,0},{2,3},{3,2},{4,5},{5,4},{6,7},{7,6},{8,9},{9,8},{10,11... | collective-permute-start | bytes 688136 | tf_op jit(solution)/shard_map/ppermute | solution.py:44
  96.1 1.5 copy-start.11
  96.1 1.5 collective-permute-start.8
  96.7 0.9 copy-start.7
  96.7 0.9 copy-start.12
  96.7 1.1 copy-start.8
  97.6 0.7 copy-start.13
  97.6 0.9 copy-start.9
  125.8 4.1 %collective-permute-start.9 = (bf16[4,16,16,896]{3,2,1,0:T(8,128)(2,1)}, bf16[4,16,16,896]{3,2,1,0:T(8,128)(2,1)S(1)}, u32[]{:S(2)}, u32[]{:S(2)}) collective-permute-start(bf16[4,16,16,896]{3,2,1,0:T(8,128)(2,1)} %get-tuple-element.40), channel_id=1, source_target_pairs={{0,1},{1,0},{2,3},{3,2},{4,5},{5,4},{6,7},{7,6},{8,9},{9,8},{10,11... | collective-permute-start | bytes 5505032 | tf_op jit(solution)/shard_map/ppermute | solution.py:56
  129.9 1.2 copy-start.1
  132.3 24.2 %all-to-all-start.1 = ((bf16[4,896,128]{2,1,0:T(8,128)(2,1)}), bf16[4,896,128]{2,1,0:T(8,128)(2,1)S(1)}, u32[]{:S(2)}, u32[]{:S(2)}) async-start(bf16[4,896,128]{2,1,0:T(8,128)(2,1)} %get-tuple-element.43), calls=%async_computation.2 | async-start | bytes 1835008 | tf_op jit(solution)/shard_map/all_to_all | solution.py:61
  141.8 10.5 %collective-permute-start.11 = (bf16[8,16,896]{2,1,0:T(8,128)(2,1)S(1)}, bf16[8,16,896]{2,1,0:T(8,128)(2,1)S(1)}, u32[]{:S(2)}, u32[]{:S(2)}) collective-permute-start(bf16[8,16,896]{2,1,0:T(8,128)(2,1)S(1)} %get-tuple-element.57), channel_id=1, source_target_pairs={{2,0},{4,2},{6,4},{0,6},{3,1},{5,3},{7,5},{1,7},{10,8},{12,10},{14... | collective-permute-start | bytes 688136 | tf_op jit(solution)/shard_map/ppermute | solution.py:60
  142.7 11.5 %collective-permute-start.10 = (bf16[8,16,896]{2,1,0:T(8,128)(2,1)S(1)}, bf16[8,16,896]{2,1,0:T(8,128)(2,1)S(1)}, u32[]{:S(2)}, u32[]{:S(2)}) collective-permute-start(bf16[8,16,896]{2,1,0:T(8,128)(2,1)S(1)} %get-tuple-element.58), channel_id=1, source_target_pairs={{0,2},{2,4},{4,6},{6,0},{1,3},{3,5},{5,7},{7,1},{8,10},{10,12},{12... | collective-permute-start | bytes 688136 | tf_op jit(solution)/shard_map/ppermute | solution.py:59
  157.3 14.6 %all-to-all-start.2 = ((bf16[8,112,128]{2,1,0:T(8,128)(2,1)}), bf16[8,112,128]{2,1,0:T(8,128)(2,1)S(1)}, u32[]{:S(2)}, u32[]{:S(2)}) async-start(bf16[8,112,128]{2,1,0:T(8,128)(2,1)} %bitcast.19), calls=%async_computation.3 | async-start | bytes 458752 | tf_op jit(solution)/shard_map/all_to_all | solution.py:72
  160.7 12.4 %collective-permute-start.12 = (bf16[16,16,896]{2,1,0:T(8,128)(2,1)}, bf16[16,16,896]{2,1,0:T(8,128)(2,1)S(1)}, u32[]{:S(2)}, u32[]{:S(2)}) collective-permute-start(bf16[16,16,896]{2,1,0:T(8,128)(2,1)} %get-tuple-element.44), channel_id=1, source_target_pairs={{0,2},{2,4},{4,6},{6,0},{1,3},{3,5},{5,7},{7,1},{8,10},{10,12},{12... | collective-permute-start | bytes 1376264 | tf_op jit(solution)/shard_map/ppermute | solution.py:70
  161.5 12.2 %collective-permute-start.13 = (bf16[16,16,896]{2,1,0:T(8,128)(2,1)S(1)}, bf16[16,16,896]{2,1,0:T(8,128)(2,1)S(1)}, u32[]{:S(2)}, u32[]{:S(2)}) collective-permute-start(bf16[16,16,896]{2,1,0:T(8,128)(2,1)S(1)} %get-tuple-element.45), channel_id=1, source_target_pairs={{2,0},{4,2},{6,4},{0,6},{3,1},{5,3},{7,5},{1,7},{10,8},{12,10},{14... | collective-permute-start | bytes 1376264 | tf_op jit(solution)/shard_map/ppermute | solution.py:71
  178.2 68.6 %copy-start.3 = (bf16[512,256]{1,0:T(8,128)(2,1)S(1)}, bf16[512,256]{1,0:T(8,128)(2,1)}, u32[]{:S(2)}) copy-start(bf16[512,256]{1,0:T(8,128)(2,1)} %get-tuple-element.32) | copy-start | bytes 786436
  178.3 68.6 %copy-start.4 = (bf16[512,256]{1,0:T(8,128)(2,1)S(1)}, bf16[512,256]{1,0:T(8,128)(2,1)}, u32[]{:S(2)}) copy-start(bf16[512,256]{1,0:T(8,128)(2,1)} %get-tuple-element.35) | copy-start | bytes 786436
  178.3 78.4 %all-to-all-start.3 = ((bf16[64,16,896]{2,1,0:T(8,128)(2,1)}), bf16[64,16,896]{2,1,0:T(8,128)(2,1)S(1)}, u32[]{:S(2)}, u32[]{:S(2)}) async-start(bf16[64,16,896]{2,1,0:T(8,128)(2,1)} %gather_fusion.3), calls=%async_computation.4 | async-start | bytes 3670016 | tf_op jit(solution)/shard_map/all_to_all | solution.py:324
  188.0 39.4 %collective-permute-start.14 = (bf16[112,128]{1,0:T(8,128)(2,1)S(1)}, bf16[112,128]{1,0:T(8,128)(2,1)S(1)}, u32[]{:S(2)}, u32[]{:S(2)}) collective-permute-start(bf16[112,128]{1,0:T(8,128)(2,1)S(1)} %fusion.9), channel_id=1, source_target_pairs={{0,32},{32,0},{64,96},{96,64},{128,160},{160,128},{192,224},{224,1... | collective-permute-start | bytes 86024 | tf_op jit(solution)/shard_map/ppermute | solution.py:303
  227.4 5.7 %collective-permute-start.15 = (bf16[224,128]{1,0:T(8,128)(2,1)S(1)}, bf16[224,128]{1,0:T(8,128)(2,1)S(1)}, u32[]{:S(2)}, u32[]{:S(2)}) collective-permute-start(bf16[224,128]{1,0:T(8,128)(2,1)S(1)} %pad_maximum_fusion.6), channel_id=1, source_target_pairs={{0,64},{32,96},{64,0},{96,32},{128,192},{160,224},{192,128},{224,1... | collective-permute-start | bytes 172040 | tf_op jit(solution)/shard_map/ppermute | solution.py:303
  233.1 9.0 %collective-permute-start.16 = (bf16[448,128]{1,0:T(8,128)(2,1)S(1)}, bf16[448,128]{1,0:T(8,128)(2,1)S(1)}, u32[]{:S(2)}, u32[]{:S(2)}) collective-permute-start(bf16[448,128]{1,0:T(8,128)(2,1)S(1)} %pad_maximum_fusion.5), channel_id=1, source_target_pairs={{0,128},{32,160},{64,192},{96,224},{128,0},{160,32},{192,64},{224,... | collective-permute-start | bytes 344072 | tf_op jit(solution)/shard_map/ppermute | solution.py:303
  242.1 8.9 %collective-permute-start.19 = (bf16[896,128]{1,0:T(8,128)(2,1)S(1)}, bf16[896,128]{1,0:T(8,128)(2,1)S(1)}, u32[]{:S(2)}, u32[]{:S(2)}) collective-permute-start(bf16[896,128]{1,0:T(8,128)(2,1)S(1)} %constant_dynamic-update-slice_fusion.refs_0_), channel_id=1, source_target_pairs={{0,24},{8,0},{16,8},{24,16},{1,25},{9,1},{17,9},{25,17},{2,26},{10... | collective-permute-start | bytes 688136 | tf_op jit(solution)/shard_map/ppermute | solution.py:305
  244.6 7.7 %collective-permute-start.18 = (bf16[896,128]{1,0:T(8,128)(2,1)S(1)}, bf16[896,128]{1,0:T(8,128)(2,1)S(1)}, u32[]{:S(2)}, u32[]{:S(2)}) collective-permute-start(bf16[896,128]{1,0:T(8,128)(2,1)S(1)} %constant_dynamic-update-slice_fusion.refs_0_), channel_id=1, source_target_pairs={{0,16},{8,24},{16,0},{24,8},{1,17},{9,25},{17,1},{25,9},{2,18},{10... | collective-permute-start | bytes 688136 | tf_op jit(solution)/shard_map/ppermute | solution.py:305
  245.6 9.1 %collective-permute-start.17 = (bf16[896,128]{1,0:T(8,128)(2,1)S(1)}, bf16[896,128]{1,0:T(8,128)(2,1)S(1)}, u32[]{:S(2)}, u32[]{:S(2)}) collective-permute-start(bf16[896,128]{1,0:T(8,128)(2,1)S(1)} %constant_dynamic-update-slice_fusion.refs_0_), channel_id=1, source_target_pairs={{0,8},{8,16},{16,24},{24,0},{1,9},{9,17},{17,25},{25,1},{2,10},{10... | collective-permute-start | bytes 688136 | tf_op jit(solution)/shard_map/ppermute | solution.py:305
Sparse Core Ops, SparseCore 0:
  69.8 33.7 all-gather.2
  112.4 42.1 reduce-scatter.1

commit v6 on v4

--- a/solution.py
+++ b/solution.py
@@ -16,8 +16,7 @@
 ROWS = 16
 PIECES = 8
 SPAN = KNB * ROWS * PIECES
-HALF = 8
-GROUP = 4
+PARTS = ((0, 6, 3), (6, 10, 2))
 F32 = jnp.float32
 BF16 = jnp.bfloat16
 
@@ -61,13 +60,12 @@
     return column.reshape(-1, DH)
 
 
-def fill_from_pieces(step, refs, rows_ref):
-    half_steps = HALF // GROUP // 2
+def fill_from_pieces(step, group, half_steps, refs, rows_ref):
     for core in range(2):
         own, above, below, far_low, far_high = refs[core * 5 : core * 5 + 5]
 
         def put(place, ref):
-            for c in range(GROUP):
+            for c in range(group):
                 at = c * SPAN + (core * 4 + place) * KNB * ROWS
                 rows_ref[at : at + KNB * ROWS, :] = ref[c * KNB : (c + 1) * KNB].reshape(
                     KNB * ROWS, ref.shape[2]
@@ -86,16 +84,16 @@
             put(3, far_high)
 
 
-def fill_from_gathered(gathered_ref, rows_ref):
+def fill_from_gathered(group, gathered_ref, rows_ref):
     for piece in range(PIECES):
-        for c in range(GROUP):
+        for c in range(group):
             at = c * SPAN + piece * KNB * ROWS
             rows_ref[at : at + KNB * ROWS, :] = gathered_ref[
                 piece, c * KNB : (c + 1) * KNB
             ].reshape(KNB * ROWS, gathered_ref.shape[3])
 
 
-def attention_kernel(first, count_ref, order_ref, *refs):
+def attention_kernel(first, begin, stretch_count, group, count_ref, order_ref, *refs):
     step = pl.program_id(0)
     if first:
         pieces, refs = refs[:10], refs[10:]
@@ -103,13 +101,11 @@
         gathered_ref, begun_ref, _, refs = refs[0], refs[1], refs[2], refs[3:]
     key_weight_ref, value_weight_ref, query_ref, grad_ref, attended_ref, grad_query_ref = refs[:6]
     refs = refs[6:]
-    share_ref, out_ref, rows_ref, kv_ref, both_ref = refs[:5]
+    share_ref, out_ref, rows_ref, kv_ref, both_ref, total_ref = refs
     if first:
-        total_ref = out_ref
-        fill_from_pieces(step, pieces, rows_ref)
+        fill_from_pieces(step, group, stretch_count // group // 2, pieces, rows_ref)
     else:
-        total_ref = refs[5]
-        fill_from_gathered(gathered_ref, rows_ref)
+        fill_from_gathered(group, gathered_ref, rows_ref)
     local = key_weight_ref.shape[1]
     factor = 1.0 / math.sqrt(DH)
     key_cols, value_cols = slice(0, local), slice(local, 2 * local)
@@ -125,7 +121,7 @@
 
     stretches = [
         (slice(c * SPAN, (c + 1) * SPAN), slice(c * STRETCH, (c + 1) * STRETCH))
-        for c in range(GROUP)
+        for c in range(group)
     ]
     for rows, _ in stretches:
         panel = rows_ref[rows, :]
@@ -138,9 +134,9 @@
         dprobs = dot(kv_ref[rows, value_cols], grad, 1, 1)
         products.append((query, grad, scores, dprobs))
     softened = []
-    for c in range(GROUP):
+    for c in range(group):
         _, _, scores, dprobs = products[c]
-        scores = jnp.where(neighbour < count_ref[step * GROUP + c], scores, -jnp.inf)
+        scores = jnp.where(neighbour < count_ref[begin + step * group + c], scores, -jnp.inf)
         powers = jnp.exp(scores - jnp.max(scores, axis=0, keepdims=True))
         probs = powers * (1.0 / jnp.sum(powers, axis=0, keepdims=True))
         row_dot = jnp.sum(probs * dprobs, axis=0, keepdims=True)
@@ -169,59 +165,61 @@
 
     @pl.when(step == 0)
     def _():
-        total_ref[...] = part if first else begun_ref[...] + part
+        total_ref[...] = part if first else begun_ref[...].astype(F32) + part
 
     @pl.when(step > 0)
     def _():
         total_ref[...] += part
 
-    if not first:
-
-        @pl.when(step == pl.num_programs(0) - 1)
-        def _():
+    @pl.when(step == pl.num_programs(0) - 1)
+    def _():
+        if first:
+            out_ref[...] = total_ref[...].astype(BF16)
+        else:
             for g in range(4):
                 out_ref[g] = total_ref[:, g * DH : (g + 1) * DH].astype(BF16)
 
 
-def attention(counts, order, panels, w_key, w_value, queries, out_grad, half, begun):
+def attention(counts, order, panels, w_key, w_value, queries, out_grad, part, begun):
     width, local = w_key.shape
-    tokens = HALF * STRETCH
-    steps = HALF // GROUP
+    begin, stretch_count, group = part
+    tokens = stretch_count * STRETCH
+    steps, skip = stretch_count // group, begin // group
     half_steps = steps // 2
     first = begun is None
-    block = (GROUP * KNB, ROWS, width)
+    block = (group * KNB, ROWS, width)
     plain = pl.BlockSpec(block, lambda i, *_: (i, 0, 0))
     low = pl.BlockSpec(block, lambda i, *_: (jnp.minimum(i, half_steps - 1), 0, 0))
     high = pl.BlockSpec(block, lambda i, *_: (jnp.maximum(i - half_steps, 0), 0, 0))
-    stacked = lambda begin: pl.BlockSpec((PIECES,) + block, lambda i, *_: (0, begin + i, 0, 0))
+    stacked = lambda skip: pl.BlockSpec((PIECES,) + block, lambda i, *_: (0, skip + i, 0, 0))
     shares = jax.ShapeDtypeStruct((PIECES, CH_DEV * KNB, ROWS, width), BF16)
-    token_in = pl.BlockSpec((GROUP * STRETCH, local), lambda i, *_: (i + half * steps, 0))
-    token_out = pl.BlockSpec((GROUP * STRETCH, local), lambda i, *_: (i, 0))
+    token_in = pl.BlockSpec((group * STRETCH, local), lambda i, *_: (i + skip, 0))
+    token_out = pl.BlockSpec((group * STRETCH, local), lambda i, *_: (i, 0))
     token_shape = jax.ShapeDtypeStruct((tokens, local), BF16)
     whole = lambda shape: pl.BlockSpec(shape, lambda i, *_: (0,) * len(shape))
     total = (width, 2 * local)
     scratch = [
-        pltpu.VMEM((GROUP * SPAN, width), BF16),
-        pltpu.VMEM((GROUP * SPAN, 2 * local), BF16),
-        pltpu.VMEM((GROUP * SPAN, 2 * local), BF16),
+        pltpu.VMEM((group * SPAN, width), BF16),
+        pltpu.VMEM((group * SPAN, 2 * local), BF16),
+        pltpu.VMEM((group * SPAN, 2 * local), BF16),
+        pltpu.VMEM(total, F32),
     ]
     if first:
         in_specs = [plain, plain, plain, low, high] * 2
-        out = jax.ShapeDtypeStruct(total, F32)
+        out = jax.ShapeDtypeStruct(total, BF16)
         aliases = {}
     else:
         in_specs = [stacked(0), whole(total), pl.BlockSpec(memory_space=pl.ANY)]
         panels = (panels,) + begun
         out = jax.ShapeDtypeStruct((4, width, DH), BF16)
-        scratch = scratch + [pltpu.VMEM(total, F32)]
         aliases = {4: 2}
     return pl.pallas_call(
-        functools.partial(attention_kernel, first),
+        functools.partial(attention_kernel, first, begin, stretch_count, group),
         grid_spec=pltpu.PrefetchScalarGridSpec(
             num_scalar_prefetch=2,
             grid=(steps,),
             in_specs=in_specs + [whole(w_key.shape), whole(w_key.shape), token_in, token_in],
-            out_specs=[token_out, token_out, stacked(half * steps), whole(out.shape)],
+            out_specs=[token_out, token_out, stacked(skip), whole(out.shape)],
             scratch_shapes=scratch,
         ),
         out_shape=[token_shape, token_shape, shares, out],
@@ -301,8 +299,9 @@
     requests = CH_DEV * KNB
     capacity = max(2, 2 * requests // seq_count)
     slot_span = seq_count * capacity
-    source_table = nb_source.reshape(seq_count, requests)
-    slot_table = nb_slot.reshape(seq_count, requests)
+    pool_count = pool.shape[0]
+    packed = (nb_source * pool_count + nb_slot).reshape(seq_count, requests)
+    source_table, slot_table = packed // pool_count, packed % pool_count
     order_ids = jnp.arange(requests)
     matches = source_table[:, :, None] == source_table[:, None, :]
     before = order_ids[None, :] < order_ids[:, None]
@@ -331,15 +330,15 @@
     positions, back, counts, order, filled, place = lax.optimization_barrier(
         (positions, back, counts, order, filled, place)
     )
-    panels = HALF * KNB
+    panels = PARTS[0][1] * KNB
     pieces = gather_pieces(take(incoming, positions[:panels]))
     gathered = lax.all_gather(take(incoming, positions[panels:]), ("y", "core"), axis=0)
     weights = (w_key, w_value, queries, out_grad)
     attended_0, grad_queries_0, shares, begun = attention(
-        counts[:HALF], order, pieces, *weights, 0, None
+        counts, order, pieces, *weights, PARTS[0], None
     )
     attended_1, grad_queries_1, shares, parts = attention(
-        counts[HALF:], order, gathered, *weights, 1, (begun, shares)
+        counts, order, gathered, *weights, PARTS[1], (begun, shares)
     )
     summed = lax.psum_scatter(shares, ("y", "core"), scatter_dimension=0)
     column = reduce_weight_grads(parts)

time: 247 us -> 239 us (0.968)
  waiting for transfers between devices: 109 us -> 104 us
    all_to_all x1, blocking collectives: 22.8 us -> 19.9 us  [reduce_weight_grads(): by_x = lax.all_to_all(parts, 'x', split_axis=0, concat_axis=0, tiled=True)]
  transfers between devices with their start and end apart: 17 -> 17, of which waited for: 10 -> 11; matrix products, arithmetic and copies ran while one was open for 4% -> 4% of each run, Pallas kernels for 6% -> 5%
where the time goes in v6:
time: 239 us; the launch traced here: 237 us
  waiting for transfers between devices  104 us (44%)
  starting transfers between devices  35.2 us (15%)
  blocking collectives  33.5 us (14%)
  Pallas kernels  32.2 us (13%)
  between operations  14.4 us (6%)
  local copies, waits for them, and re-layouts  13.3 us (6%)
  other arithmetic  4.81 us (2%)
    all_to_all x2, waiting for transfers between devices, exchange(): lax.all_to_all(array, ('z', 'x'), split_axis=0, concat_axis=0, tiled=True)  60.6 us
    pallas_call x2, Pallas kernels, attention(): pl.pallas_call(functools.partial(attention_kernel, first, begin, stretch_...  27.8 us
    all_to_all x2, starting transfers between devices, exchange(): lax.all_to_all(array, ('z', 'x'), split_axis=0, concat_axis=0, tiled=True)  21.5 us
    all_to_all x1, blocking collectives, reduce_weight_grads(): by_x = lax.all_to_all(parts, 'x', split_axis=0, concat_axis=0, tiled=True)  19.9 us
    ppermute x3, waiting for transfers between devices, spread_columns(): lax.ppermute(column, 'x', shift(4, k))  18.9 us
    all_to_all x1, blocking collectives, reduce_weight_grads(): by_z = lax.all_to_all(part, 'z', split_axis=0, concat_axis=0, tiled=True)  13.6 us
    reduce_scatter x1, waiting for transfers between devices, local(): summed = lax.psum_scatter(shares, ('y', 'core'), scatter_dimension=0)  7.96 us
    gather x4, local copies, waits for them, and re-layouts, local(): take = lambda array, index: jnp.take(array, index, axis=0, mode='clip')  7.19 us
  transfers between devices with their start and end apart: 17, of which 11 were waited for; matrix products, arithmetic and copies ran while one was open for 4% of the time, Pallas kernels for 5%

profile of v6, /device:TPU:8, one launch (start us, length us, event | category | flops | bytes accessed | tf_op | source)
XLA Modules:
  0.0 237.3 jit_solution(17464739765895594154)
XLA Ops:
  7.2 0.8 multiply_add_fusion
  8.0 0.1 copy.16
  8.1 0.2 reshape.142
  8.3 0.8 convert_reduce_fusion
  9.1 0.1 select_reduce_fusion
  9.5 2.0 gather_fusion
  11.4 11.3 %all-to-all-start = ((bf16[64,16,896]{2,1,0:T(8,128)(2,1)}), bf16[64,16,896]{2,1,0:T(8,128)(2,1)S(1)}, u32[]{:S(2)}, u32[]{:S(2)}) async-start(bf16[64,16,896]{2,1,0:T(8,128)(2,1)} %gather_fusion), calls=%async_computation | async-start | bytes 3670016 | tf_op jit(solution)/shard_map/all_to_all | solution.py:293
  22.9 0.1 fusion.1
  23.2 1.3 dynamic_slice.12.count_ref
  24.5 0.7 stack.35.order_ref
  25.4 42.0 %all-to-all-done = bf16[64,16,896]{2,1,0:T(8,128)(2,1)S(1)} async-done(((bf16[64,16,896]{2,1,0:T(8,128)(2,1)}), bf16[64,16,896]{2,1,0:T(8,128)(2,1)S(1)}, u32[]{:S(2)}, u32[]{:S(2)}) %all-to-all-start) | async-done | bytes 1835040 | tf_op jit(solution)/shard_map/all_to_all | solution.py:293
  67.4 1.5 gather_fusion.2
  68.9 0.6 gather_fusion.1
  69.6 1.7 collective-permute-start.1
  71.2 0.4 collective-permute-start
  71.7 6.1 %collective-permute-done.1.refs_2_ = bf16[12,16,896]{2,1,0:T(8,128)(2,1)S(1)} collective-permute-done((bf16[12,16,896]{2,1,0:T(8,128)(2,1)S(1)}, bf16[12,16,896]{2,1,0:T(8,128)(2,1)S(1)}, u32[]{:S(2)}, u32[]{:S(2)}) %collective-permute-start.1) | collective-permute-done | bytes 344096 | tf_op jit(solution)/shard_map/ppermute | solution.py:38
  77.8 1.7 collective-permute-start.2
  79.5 0.5 collective-permute-start.3
  80.0 0.5 collective-permute-start.6
  80.5 6.1 %collective-permute-done.2.refs_3_ = bf16[6,16,896]{2,1,0:T(8,128)(2,1)S(1)} collective-permute-done((bf16[6,16,896]{2,1,0:T(8,128)(2,1)S(1)}, bf16[6,16,896]{2,1,0:T(8,128)(2,1)S(1)}, u32[]{:S(2)}, u32[]{:S(2)}) %collective-permute-start.2) | collective-permute-done | bytes 172064 | tf_op jit(solution)/shard_map/ppermute | solution.py:40
  86.6 1.9 collective-permute-done.3.refs_4_
  88.5 1.4 collective-permute-done.8.refs_9_
  89.9 0.6 copy-done.13
  90.5 0.1 copy-done.8
  90.6 0.8 copy-done.9
  91.4 11.2 %attention.2 = (bf16[384,256]{1,0:T(8,128)(2,1)}, bf16[384,256]{1,0:T(8,128)(2,1)}, bf16[8,32,16,896]{3,2,1,0:T(8,128)(2,1)}, bf16[896,512]{1,0:T(8,128)(2,1)}) custom-call(s32[16]{0:T(128)} %dynamic_slice.12.count_ref, s32[8]{0:T(128)} %stack.35.order_ref, bf16[12,16,896]{2,1,0:T(8,128)(2,1)} %copy-done.2, bf16[12,16,896]{2,1,0:T(8,128)(2,1)} %copy-done.6, ...), custom_call_target="tpu_custom_call" | custom-call | flops 8589934592 | bytes 16777216 | tf_op jit(solution)/shard_map/attention/pallas_call | solution.py:216
  102.6 1.0 all-gather.3.cloned.1.call-done
  103.6 16.6 %attention.3 = (bf16[640,256]{1,0:T(8,128)(2,1)}, bf16[640,256]{1,0:T(8,128)(2,1)}, bf16[8,32,16,896]{3,2,1,0:T(8,128)(2,1)}, bf16[4,896,128]{2,1,0:T(8,128)(2,1)}) custom-call(s32[16]{0:T(128)} %dynamic_slice.12.count_ref, s32[8]{0:T(128)} %stack.35.order_ref, bf16[8,20,16,896]{3,2,1,0:T(8,128)(2,1)} %bitcast.25, ...), custom_call_target="tpu_custom_call", output_to_operand_aliasing={{2}: (4, {})} | custom-call | flops 8589934592 | bytes 16777216 | tf_op jit(solution)/shard_map/attention/pallas_call | solution.py:216
  120.3 1.1 copy-done.1
  121.4 19.9 %all_to_all.25 = bf16[4,896,128]{2,1,0:T(8,128)(2,1)S(1)} all-to-all(bf16[4,896,128]{2,1,0:T(8,128)(2,1)S(1)} %copy-done.1), channel_id=1, replica_groups=mesh['z'=8,'x'=4,'y'=4,'core'=2] {'x'}, dimensions={0} | all-to-all | bytes 1835008 | tf_op jit(solution)/shard_map/all_to_all | solution.py:54
  141.3 0.1 add_convert_fusion
  141.5 13.6 %all_to_all.26 = bf16[8,112,128]{2,1,0:T(8,128)(2,1)S(1)} all-to-all(bf16[8,112,128]{2,1,0:T(8,128)(2,1)S(1)} %bitcast.23), channel_id=1, replica_groups=mesh['z'=8,'x'=4,'y'=4,'core'=2] {'z'}, dimensions={0} | all-to-all | bytes 458752 | tf_op jit(solution)/shard_map/all_to_all | solution.py:56
  155.1 0.7 broadcast_in_dim.68
  155.8 3.4 %all-to-all-start.3 = ((bf16[8,112,128]{2,1,0:T(8,128)(2,1)}), bf16[8,112,128]{2,1,0:T(8,128)(2,1)S(1)}, u32[]{:S(2)}, u32[]{:S(2)}) async-start(bf16[8,112,128]{2,1,0:T(8,128)(2,1)} %broadcast_in_dim.68), calls=%async_computation.4 | async-start | bytes 458752 | tf_op jit(solution)/shard_map/all_to_all | solution.py:59
  159.3 8.0 %reduce-scatter.2.cloned.1.call-done = bf16[1,32,16,896]{3,2,1,0:T(8,128)(2,1)} async-done(((bf16[8,32,16,896]{3,2,1,0:T(8,128)(2,1)}), bf16[1,32,16,896]{3,2,1,0:T(8,128)(2,1)}) %reduce-scatter.2.cloned.1.call-update) | async-done | bytes 917520 | tf_op jit(solution)/shard_map/reduce_scatter | solution.py:343
  167.2 3.2 %gather_fusion.3 = bf16[64,16,896]{2,1,0:T(8,128)(2,1)} fusion(bf16[32,16,896]{2,1,0:T(8,128)(2,1)} %bitcast.22, s32[1024]{0:T(1024)S(1)} %pad_clamp_fusion), kind=kCustom, calls=%fused_computation.3 | custom fusion | bytes 3670272 | tf_op jit(solution)/shard_map/jit(_take)/gather | solution.py:322
  170.4 10.2 %all-to-all-start.4 = ((bf16[64,16,896]{2,1,0:T(8,128)(2,1)}), bf16[64,16,896]{2,1,0:T(8,128)(2,1)S(1)}, u32[]{:S(2)}, u32[]{:S(2)}) async-start(bf16[64,16,896]{2,1,0:T(8,128)(2,1)} %gather_fusion.3), calls=%async_computation.5 | async-start | bytes 3670016 | tf_op jit(solution)/shard_map/all_to_all | solution.py:293
  180.6 3.4 %collective-permute-start.10 = (bf16[896,128]{1,0:T(8,128)(2,1)S(1)}, bf16[896,128]{1,0:T(8,128)(2,1)S(1)}, u32[]{:S(2)}, u32[]{:S(2)}) collective-permute-start(bf16[896,128]{1,0:T(8,128)(2,1)S(1)} %bitcast.18), channel_id=1, source_target_pairs={{0,16},{8,24},{16,0},{24,8},{1,17},{9,25},{17,1},{25,9},{2,18},{10... | collective-permute-start | bytes 688136 | tf_op jit(solution)/shard_map/ppermute | solution.py:274
  183.9 1.2 collective-permute-start.11
  185.1 0.9 collective-permute-start.9
  186.0 1.9 pad_maximum_fusion.1
  187.8 0.8 pad_maximum_fusion
  188.6 12.1 %collective-permute-done.10.refs_2_ = bf16[896,128]{1,0:T(8,128)(2,1)S(1)} collective-permute-done((bf16[896,128]{1,0:T(8,128)(2,1)S(1)}, bf16[896,128]{1,0:T(8,128)(2,1)S(1)}, u32[]{:S(2)}, u32[]{:S(2)}) %collective-permute-start.10) | collective-permute-done | bytes 229408 | tf_op jit(solution)/shard_map/ppermute | solution.py:274
  200.7 5.6 %collective-permute-done.11.refs_3_ = bf16[896,128]{1,0:T(8,128)(2,1)S(1)} collective-permute-done((bf16[896,128]{1,0:T(8,128)(2,1)S(1)}, bf16[896,128]{1,0:T(8,128)(2,1)S(1)}, u32[]{:S(2)}, u32[]{:S(2)}) %collective-permute-start.11) | collective-permute-done | bytes 229408 | tf_op jit(solution)/shard_map/ppermute | solution.py:274
  206.3 1.2 collective-permute-done.9.refs_1_
  207.5 1.4 spread.1
  208.9 18.6 %all-to-all-done.4.arrived_ref = bf16[64,16,896]{2,1,0:T(8,128)(2,1)S(1)} async-done(((bf16[64,16,896]{2,1,0:T(8,128)(2,1)}), bf16[64,16,896]{2,1,0:T(8,128)(2,1)S(1)}, u32[]{:S(2)}, u32[]{:S(2)}) %all-to-all-start.4) | async-done | bytes 1835040 | tf_op jit(solution)/shard_map/all_to_all | solution.py:293
  227.5 2.9 %collect.1 = f32[32,16,896]{2,1,0:T(8,128)} custom-call(s32[64]{0:T(128)S(1)} %reshape.149.slot_ref, s32[64]{0:T(128)S(1)} %reshape.146.filled_ref, bf16[64,16,896]{2,1,0:T(8,128)(2,1)S(1)} %all-to-all-done.4.arrived_ref), custom_call_target="tpu_custom_call" | custom-call | tf_op jit(solution)/shard_map/collect/pallas_call | solution.py:250
  (55 shorter events, 0.9 us)
Async XLA Ops:
  7.2 2.3 copy-start
  11.4 56.0 %all-to-all-start = ((bf16[64,16,896]{2,1,0:T(8,128)(2,1)}), bf16[64,16,896]{2,1,0:T(8,128)(2,1)S(1)}, u32[]{:S(2)}, u32[]{:S(2)}) async-start(bf16[64,16,896]{2,1,0:T(8,128)(2,1)} %gather_fusion), calls=%async_computation | async-start | bytes 3670016 | tf_op jit(solution)/shard_map/all_to_all | solution.py:293
  22.8 80.9 %all-gather.3.cloned.1.call-start = ((), (), s32[]{:S(2)}) async-start(), calls=%async_computation.7 | async-start | bytes 5160960 | tf_op jit(solution)/shard_map/all_gather | solution.py:335
  68.9 98.3 %reduce-scatter.2.cloned.1.call-start = ((), (), s32[]{:S(2)}) async-start(), calls=%async_computation.6 | async-start | bytes 8257536 | tf_op jit(solution)/shard_map/reduce_scatter | solution.py:343
  69.6 20.3 %copy-start.2 = (bf16[12,16,896]{2,1,0:T(8,128)(2,1)}, bf16[12,16,896]{2,1,0:T(8,128)(2,1)S(1)}, u32[]{:S(2)}) copy-start(bf16[12,16,896]{2,1,0:T(8,128)(2,1)S(1)} %gather_fusion.1) | copy-start | bytes 1032196
  69.6 8.2 %collective-permute-start.1 = (bf16[12,16,896]{2,1,0:T(8,128)(2,1)S(1)}, bf16[12,16,896]{2,1,0:T(8,128)(2,1)S(1)}, u32[]{:S(2)}, u32[]{:S(2)}) collective-permute-start(bf16[12,16,896]{2,1,0:T(8,128)(2,1)S(1)} %gather_fusion.1), channel_id=1, source_target_pairs={{0,2},{2,4},{4,6},{6,0},{1,3},{3,5},{5,7},{7,1},{8,10},{10,12},{12... | collective-permute-start | bytes 1032200 | tf_op jit(solution)/shard_map/ppermute | solution.py:38
  71.2 8.2 %collective-permute-start = (bf16[12,16,896]{2,1,0:T(8,128)(2,1)S(1)}, bf16[12,16,896]{2,1,0:T(8,128)(2,1)S(1)}, u32[]{:S(2)}, u32[]{:S(2)}) collective-permute-start(bf16[12,16,896]{2,1,0:T(8,128)(2,1)S(1)} %gather_fusion.1), channel_id=1, source_target_pairs={{2,0},{4,2},{6,4},{0,6},{3,1},{5,3},{7,5},{1,7},{10,8},{12,10},{14... | collective-permute-start | bytes 1032200 | tf_op jit(solution)/shard_map/ppermute | solution.py:39
  71.7 16.8 %collective-permute-start.4 = (bf16[12,16,896]{2,1,0:T(8,128)(2,1)S(1)}, bf16[12,16,896]{2,1,0:T(8,128)(2,1)S(1)}, u32[]{:S(2)}, u32[]{:S(2)}) collective-permute-start(bf16[12,16,896]{2,1,0:T(8,128)(2,1)S(1)} %gather_fusion.1), channel_id=1, source_target_pairs={{0,1},{1,0},{2,3},{3,2},{4,5},{5,4},{6,7},{7,6},{8,9},{9,8},{10,11... | collective-permute-start | bytes 1032200 | tf_op jit(solution)/shard_map/ppermute | solution.py:43
  77.8 12.1 %copy-start.5 = (bf16[12,16,896]{2,1,0:T(8,128)(2,1)}, bf16[12,16,896]{2,1,0:T(8,128)(2,1)S(1)}, u32[]{:S(2)}) copy-start(bf16[12,16,896]{2,1,0:T(8,128)(2,1)S(1)} %collective-permute-done.1.refs_2_) | copy-start | bytes 1032196
  77.8 8.8 %collective-permute-start.2 = (bf16[6,16,896]{2,1,0:T(8,128)(2,1)S(1)}, bf16[6,16,896]{2,1,0:T(8,128)(2,1)S(1)}, u32[]{:S(2)}, u32[]{:S(2)}) collective-permute-start(bf16[6,16,896]{2,1,0:T(8,128)(2,1)S(1)} %slice.72), channel_id=1, source_target_pairs={{0,2},{2,4},{4,6},{6,0},{1,3},{3,5},{5,7},{7,1},{8,10},{10,12},{12... | collective-permute-start | bytes 516104 | tf_op jit(solution)/shard_map/ppermute | solution.py:40
  79.5 10.4 %copy-start.6 = (bf16[12,16,896]{2,1,0:T(8,128)(2,1)}, bf16[12,16,896]{2,1,0:T(8,128)(2,1)S(1)}, u32[]{:S(2)}) copy-start(bf16[12,16,896]{2,1,0:T(8,128)(2,1)S(1)} %collective-permute-done.refs_1_) | copy-start | bytes 1032196
  79.5 9.0 %collective-permute-start.3 = (bf16[6,16,896]{2,1,0:T(8,128)(2,1)S(1)}, bf16[6,16,896]{2,1,0:T(8,128)(2,1)S(1)}, u32[]{:S(2)}, u32[]{:S(2)}) collective-permute-start(bf16[6,16,896]{2,1,0:T(8,128)(2,1)S(1)} %slice.73), channel_id=1, source_target_pairs={{2,0},{4,2},{6,4},{0,6},{3,1},{5,3},{7,5},{1,7},{10,8},{12,10},{14... | collective-permute-start | bytes 516104 | tf_op jit(solution)/shard_map/ppermute | solution.py:41
  80.0 9.9 %collective-permute-start.5 = (bf16[12,16,896]{2,1,0:T(8,128)(2,1)S(1)}, bf16[12,16,896]{2,1,0:T(8,128)(2,1)S(1)}, u32[]{:S(2)}, u32[]{:S(2)}) collective-permute-start(bf16[12,16,896]{2,1,0:T(8,128)(2,1)S(1)} %collective-permute-done.refs_1_), channel_id=1, source_target_pairs={{0,1},{1,0},{2,3},{3,2},{4,5},{5,4},{6,7},{7,6},{8,9},{9,8},{10,11... | collective-permute-start | bytes 1032200 | tf_op jit(solution)/shard_map/ppermute | solution.py:43
  80.0 9.9 %collective-permute-start.6 = (bf16[12,16,896]{2,1,0:T(8,128)(2,1)S(1)}, bf16[12,16,896]{2,1,0:T(8,128)(2,1)S(1)}, u32[]{:S(2)}, u32[]{:S(2)}) collective-permute-start(bf16[12,16,896]{2,1,0:T(8,128)(2,1)S(1)} %collective-permute-done.1.refs_2_), channel_id=1, source_target_pairs={{0,1},{1,0},{2,3},{3,2},{4,5},{5,4},{6,7},{7,6},{8,9},{9,8},{10,11... | collective-permute-start | bytes 1032200 | tf_op jit(solution)/shard_map/ppermute | solution.py:43
  86.6 3.3 %copy-start.10 = (bf16[6,16,896]{2,1,0:T(8,128)(2,1)}, bf16[6,16,896]{2,1,0:T(8,128)(2,1)S(1)}, u32[]{:S(2)}) copy-start(bf16[6,16,896]{2,1,0:T(8,128)(2,1)S(1)} %collective-permute-done.2.refs_3_) | copy-start | bytes 516100
  86.6 1.9 collective-permute-start.7
  88.4 1.5 copy-start.11
  88.4 1.4 collective-permute-start.8
  88.4 1.5 copy-start.7
  88.5 1.5 copy-start.12
  89.8 0.7 copy-start.13
  89.8 0.8 copy-start.8
  90.6 0.8 copy-start.9
  120.2 1.2 copy-start.1
  155.8 14.5 %all-to-all-start.3 = ((bf16[8,112,128]{2,1,0:T(8,128)(2,1)}), bf16[8,112,128]{2,1,0:T(8,128)(2,1)S(1)}, u32[]{:S(2)}, u32[]{:S(2)}) async-start(bf16[8,112,128]{2,1,0:T(8,128)(2,1)} %broadcast_in_dim.68), calls=%async_computation.4 | async-start | bytes 458752 | tf_op jit(solution)/shard_map/all_to_all | solution.py:59
  170.4 17.4 %copy-start.3 = (bf16[640,256]{1,0:T(8,128)(2,1)S(1)}, bf16[640,256]{1,0:T(8,128)(2,1)}, u32[]{:S(2)}) copy-start(bf16[640,256]{1,0:T(8,128)(2,1)} %get-tuple-element.29) | copy-start | bytes 983044
  170.4 17.4 %copy-start.4 = (bf16[384,256]{1,0:T(8,128)(2,1)S(1)}, bf16[384,256]{1,0:T(8,128)(2,1)}, u32[]{:S(2)}) copy-start(bf16[384,256]{1,0:T(8,128)(2,1)} %get-tuple-element.26) | copy-start | bytes 589828
  170.4 57.1 %all-to-all-start.4 = ((bf16[64,16,896]{2,1,0:T(8,128)(2,1)}), bf16[64,16,896]{2,1,0:T(8,128)(2,1)S(1)}, u32[]{:S(2)}, u32[]{:S(2)}) async-start(bf16[64,16,896]{2,1,0:T(8,128)(2,1)} %gather_fusion.3), calls=%async_computation.5 | async-start | bytes 3670016 | tf_op jit(solution)/shard_map/all_to_all | solution.py:293
  180.6 20.2 %collective-permute-start.10 = (bf16[896,128]{1,0:T(8,128)(2,1)S(1)}, bf16[896,128]{1,0:T(8,128)(2,1)S(1)}, u32[]{:S(2)}, u32[]{:S(2)}) collective-permute-start(bf16[896,128]{1,0:T(8,128)(2,1)S(1)} %bitcast.18), channel_id=1, source_target_pairs={{0,16},{8,24},{16,0},{24,8},{1,17},{9,25},{17,1},{25,9},{2,18},{10... | collective-permute-start | bytes 688136 | tf_op jit(solution)/shard_map/ppermute | solution.py:274
  183.9 22.4 %collective-permute-start.11 = (bf16[896,128]{1,0:T(8,128)(2,1)S(1)}, bf16[896,128]{1,0:T(8,128)(2,1)S(1)}, u32[]{:S(2)}, u32[]{:S(2)}) collective-permute-start(bf16[896,128]{1,0:T(8,128)(2,1)S(1)} %bitcast.19), channel_id=1, source_target_pairs={{0,24},{8,0},{16,8},{24,16},{1,25},{9,1},{17,9},{25,17},{2,26},{10... | collective-permute-start | bytes 688136 | tf_op jit(solution)/shard_map/ppermute | solution.py:274
  185.1 22.4 %collective-permute-start.9 = (bf16[896,128]{1,0:T(8,128)(2,1)S(1)}, bf16[896,128]{1,0:T(8,128)(2,1)S(1)}, u32[]{:S(2)}, u32[]{:S(2)}) collective-permute-start(bf16[896,128]{1,0:T(8,128)(2,1)S(1)} %bitcast.20), channel_id=1, source_target_pairs={{0,8},{8,16},{16,24},{24,0},{1,9},{9,17},{17,25},{25,1},{2,10},{10... | collective-permute-start | bytes 688136 | tf_op jit(solution)/shard_map/ppermute | solution.py:274
Sparse Core Ops, SparseCore 0:
  69.0 34.5 all-gather.2
  120.4 46.7 reduce-scatter.1

commit v7 on v6

--- a/solution.py
+++ b/solution.py
@@ -224,7 +224,7 @@
         ),
         out_shape=[token_shape, token_shape, shares, out],
         input_output_aliases=aliases,
-        compiler_params=pltpu.CompilerParams(vmem_limit_bytes=56 * 2**20),
+        compiler_params=pltpu.CompilerParams(vmem_limit_bytes=51 * 2**20),
         cost_estimate=pl.CostEstimate(
             flops=8 * 2**30, bytes_accessed=16 * 2**20, transcendentals=2**18
         ),

time: 239 us -> 238 us (level)
  no operation moved by 1% of the time
where the time goes in v7:
time: 238 us; the launch traced here: 236 us
  waiting for transfers between devices  105 us (44%)
  starting transfers between devices  35 us (15%)
  blocking collectives  33.5 us (14%)
  Pallas kernels  30.7 us (13%)
  between operations  14.3 us (6%)
  local copies, waits for them, and re-layouts  12.9 us (5%)
  other arithmetic  4.81 us (2%)
    all_to_all x2, waiting for transfers between devices, exchange(): lax.all_to_all(array, ('z', 'x'), split_axis=0, concat_axis=0, tiled=True)  60.5 us
    pallas_call x2, Pallas kernels, attention(): pl.pallas_call(functools.partial(attention_kernel, first, begin, stretch_...  26.3 us
    all_to_all x2, starting transfers between devices, exchange(): lax.all_to_all(array, ('z', 'x'), split_axis=0, concat_axis=0, tiled=True)  21.3 us
    all_to_all x1, blocking collectives, reduce_weight_grads(): by_x = lax.all_to_all(parts, 'x', split_axis=0, concat_axis=0, tiled=True)  19.9 us
    ppermute x3, waiting for transfers between devices, spread_columns(): lax.ppermute(column, 'x', shift(4, k))  18.9 us
    all_to_all x1, blocking collectives, reduce_weight_grads(): by_z = lax.all_to_all(part, 'z', split_axis=0, concat_axis=0, tiled=True)  13.6 us
    reduce_scatter x1, waiting for transfers between devices, local(): summed = lax.psum_scatter(shares, ('y', 'core'), scatter_dimension=0)  7.94 us
    gather x4, local copies, waits for them, and re-layouts, local(): take = lambda array, index: jnp.take(array, index, axis=0, mode='clip')  7.19 us
  transfers between devices with their start and end apart: 17, of which 11 were waited for; matrix products, arithmetic and copies ran while one was open for 4% of the time, Pallas kernels for 5%

profile of v7, /device:TPU:8, one launch (start us, length us, event | category | flops | bytes accessed | tf_op | source)
XLA Modules:
  0.0 236.1 jit_solution(6719624684501961313)
XLA Ops:
  7.2 0.8 multiply_add_fusion
  8.0 0.1 copy.16
  8.1 0.2 reshape.142
  8.3 0.8 convert_reduce_fusion
  9.1 0.1 select_reduce_fusion
  9.5 2.0 gather_fusion
  11.4 11.3 %all-to-all-start = ((bf16[64,16,896]{2,1,0:T(8,128)(2,1)}), bf16[64,16,896]{2,1,0:T(8,128)(2,1)S(1)}, u32[]{:S(2)}, u32[]{:S(2)}) async-start(bf16[64,16,896]{2,1,0:T(8,128)(2,1)} %gather_fusion), calls=%async_computation | async-start | bytes 3670016 | tf_op jit(solution)/shard_map/all_to_all | solution.py:293
  22.9 0.1 fusion.1
  23.1 0.1 reshape.146.filled_ref
  23.2 0.8 dynamic_slice.12.count_ref
  24.2 43.2 %all-to-all-done = bf16[64,16,896]{2,1,0:T(8,128)(2,1)S(1)} async-done(((bf16[64,16,896]{2,1,0:T(8,128)(2,1)}), bf16[64,16,896]{2,1,0:T(8,128)(2,1)S(1)}, u32[]{:S(2)}, u32[]{:S(2)}) %all-to-all-start) | async-done | bytes 1835040 | tf_op jit(solution)/shard_map/all_to_all | solution.py:293
  67.4 1.5 gather_fusion.2
  68.9 0.6 gather_fusion.1
  69.6 1.7 collective-permute-start.1
  71.2 0.4 collective-permute-start
  71.7 6.1 %collective-permute-done.1.refs_2_ = bf16[12,16,896]{2,1,0:T(8,128)(2,1)S(1)} collective-permute-done((bf16[12,16,896]{2,1,0:T(8,128)(2,1)S(1)}, bf16[12,16,896]{2,1,0:T(8,128)(2,1)S(1)}, u32[]{:S(2)}, u32[]{:S(2)}) %collective-permute-start.1) | collective-permute-done | bytes 344096 | tf_op jit(solution)/shard_map/ppermute | solution.py:38
  77.8 1.7 collective-permute-start.2
  79.5 0.5 collective-permute-start.3
  80.0 0.5 collective-permute-start.6
  80.5 6.0 %collective-permute-done.2.refs_3_ = bf16[6,16,896]{2,1,0:T(8,128)(2,1)S(1)} collective-permute-done((bf16[6,16,896]{2,1,0:T(8,128)(2,1)S(1)}, bf16[6,16,896]{2,1,0:T(8,128)(2,1)S(1)}, u32[]{:S(2)}, u32[]{:S(2)}) %collective-permute-start.2) | collective-permute-done | bytes 172064 | tf_op jit(solution)/shard_map/ppermute | solution.py:40
  86.6 1.9 collective-permute-done.3.refs_4_
  88.5 1.4 collective-permute-done.8.refs_9_
  89.9 0.7 copy-done.8
  90.6 10.3 %attention.2 = (bf16[384,256]{1,0:T(8,128)(2,1)S(1)}, bf16[384,256]{1,0:T(8,128)(2,1)S(1)}, bf16[8,32,16,896]{3,2,1,0:T(8,128)(2,1)}, bf16[896,512]{1,0:T(8,128)(2,1)}) custom-call(s32[16]{0:T(128)S(1)} %dynamic_slice.12.count_ref, s32[8]{0:T(128)S(1)} %stack.35.order_ref, bf16[12,16,896]{2,1,0:T(8,128)(2,1)S(1)} %gather_fusion.1, ...), custom_call_target="tpu_custom_call" | custom-call | flops 8589934592 | bytes 16777216 | tf_op jit(solution)/shard_map/attention/pallas_call | solution.py:216
  101.0 0.7 copy-done.2
  101.6 2.0 all-gather.3.cloned.1.call-done
  103.6 16.0 %attention.3 = (bf16[640,256]{1,0:T(8,128)(2,1)S(1)}, bf16[640,256]{1,0:T(8,128)(2,1)S(1)}, bf16[8,32,16,896]{3,2,1,0:T(8,128)(2,1)}, bf16[4,896,128]{2,1,0:T(8,128)(2,1)}) custom-call(s32[16]{0:T(128)S(1)} %dynamic_slice.12.count_ref, s32[8]{0:T(128)S(1)} %stack.35.order_ref, bf16[8,20,16,896]{3,2,1,0:T(8,128)(2,1)} %bitcast.25, ...), custom_call_target="tpu_custom_call", output_to_operand_aliasing={{2}: (4, {})} | custom-call | flops 8589934592 | bytes 16777216 | tf_op jit(solution)/shard_map/attention/pallas_call | solution.py:216
  119.7 0.7 copy-done.1
  120.4 1.2 copy-done.7
  121.6 19.9 %all_to_all.25 = bf16[4,896,128]{2,1,0:T(8,128)(2,1)S(1)} all-to-all(bf16[4,896,128]{2,1,0:T(8,128)(2,1)S(1)} %copy-done.7), channel_id=1, replica_groups=mesh['z'=8,'x'=4,'y'=4,'core'=2] {'x'}, dimensions={0} | all-to-all | bytes 1835008 | tf_op jit(solution)/shard_map/all_to_all | solution.py:54
  141.5 0.1 add_convert_fusion
  141.6 13.6 %all_to_all.26 = bf16[8,112,128]{2,1,0:T(8,128)(2,1)S(1)} all-to-all(bf16[8,112,128]{2,1,0:T(8,128)(2,1)S(1)} %bitcast.23), channel_id=1, replica_groups=mesh['z'=8,'x'=4,'y'=4,'core'=2] {'z'}, dimensions={0} | all-to-all | bytes 458752 | tf_op jit(solution)/shard_map/all_to_all | solution.py:56
  155.3 0.7 broadcast_in_dim.68
  156.0 3.4 %all-to-all-start.3 = ((bf16[8,112,128]{2,1,0:T(8,128)(2,1)}), bf16[8,112,128]{2,1,0:T(8,128)(2,1)S(1)}, u32[]{:S(2)}, u32[]{:S(2)}) async-start(bf16[8,112,128]{2,1,0:T(8,128)(2,1)} %broadcast_in_dim.68), calls=%async_computation.4 | async-start | bytes 458752 | tf_op jit(solution)/shard_map/all_to_all | solution.py:59
  159.4 7.9 %reduce-scatter.2.cloned.1.call-done = bf16[1,32,16,896]{3,2,1,0:T(8,128)(2,1)} async-done(((bf16[8,32,16,896]{3,2,1,0:T(8,128)(2,1)}), bf16[1,32,16,896]{3,2,1,0:T(8,128)(2,1)}) %reduce-scatter.2.cloned.1.call-update) | async-done | bytes 917520 | tf_op jit(solution)/shard_map/reduce_scatter | solution.py:343
  167.3 3.2 %gather_fusion.3 = bf16[64,16,896]{2,1,0:T(8,128)(2,1)} fusion(bf16[32,16,896]{2,1,0:T(8,128)(2,1)} %bitcast.22, s32[1024]{0:T(1024)S(1)} %pad_clamp_fusion), kind=kCustom, calls=%fused_computation.3 | custom fusion | bytes 3670272 | tf_op jit(solution)/shard_map/jit(_take)/gather | solution.py:322
  170.5 10.0 %all-to-all-start.4 = ((bf16[64,16,896]{2,1,0:T(8,128)(2,1)}), bf16[64,16,896]{2,1,0:T(8,128)(2,1)S(1)}, u32[]{:S(2)}, u32[]{:S(2)}) async-start(bf16[64,16,896]{2,1,0:T(8,128)(2,1)} %gather_fusion.3), calls=%async_computation.5 | async-start | bytes 3670016 | tf_op jit(solution)/shard_map/all_to_all | solution.py:293
  180.5 3.4 %collective-permute-start.10 = (bf16[896,128]{1,0:T(8,128)(2,1)S(1)}, bf16[896,128]{1,0:T(8,128)(2,1)S(1)}, u32[]{:S(2)}, u32[]{:S(2)}) collective-permute-start(bf16[896,128]{1,0:T(8,128)(2,1)S(1)} %bitcast.18), channel_id=1, source_target_pairs={{0,16},{8,24},{16,0},{24,8},{1,17},{9,25},{17,1},{25,9},{2,18},{10... | collective-permute-start | bytes 688136 | tf_op jit(solution)/shard_map/ppermute | solution.py:274
  183.9 1.2 collective-permute-start.11
  185.1 0.9 collective-permute-start.9
  185.9 1.9 pad_maximum_fusion.1
  187.8 0.8 pad_maximum_fusion
  188.6 12.0 %collective-permute-done.10.refs_2_ = bf16[896,128]{1,0:T(8,128)(2,1)S(1)} collective-permute-done((bf16[896,128]{1,0:T(8,128)(2,1)S(1)}, bf16[896,128]{1,0:T(8,128)(2,1)S(1)}, u32[]{:S(2)}, u32[]{:S(2)}) %collective-permute-start.10) | collective-permute-done | bytes 229408 | tf_op jit(solution)/shard_map/ppermute | solution.py:274
  200.7 5.6 %collective-permute-done.11.refs_3_ = bf16[896,128]{1,0:T(8,128)(2,1)S(1)} collective-permute-done((bf16[896,128]{1,0:T(8,128)(2,1)S(1)}, bf16[896,128]{1,0:T(8,128)(2,1)S(1)}, u32[]{:S(2)}, u32[]{:S(2)}) %collective-permute-start.11) | collective-permute-done | bytes 229408 | tf_op jit(solution)/shard_map/ppermute | solution.py:274
  206.3 1.2 collective-permute-done.9.refs_1_
  207.5 1.4 spread.1
  208.9 17.4 %all-to-all-done.4.arrived_ref = bf16[64,16,896]{2,1,0:T(8,128)(2,1)S(1)} async-done(((bf16[64,16,896]{2,1,0:T(8,128)(2,1)}), bf16[64,16,896]{2,1,0:T(8,128)(2,1)S(1)}, u32[]{:S(2)}, u32[]{:S(2)}) %all-to-all-start.4) | async-done | bytes 1835040 | tf_op jit(solution)/shard_map/all_to_all | solution.py:293
  226.3 2.9 %collect.1 = f32[32,16,896]{2,1,0:T(8,128)} custom-call(s32[64]{0:T(128)S(1)} %reshape.149.slot_ref, s32[64]{0:T(128)S(1)} %reshape.146.filled_ref, bf16[64,16,896]{2,1,0:T(8,128)(2,1)S(1)} %all-to-all-done.4.arrived_ref), custom_call_target="tpu_custom_call" | custom-call | tf_op jit(solution)/shard_map/collect/pallas_call | solution.py:250
  (45 shorter events, 0.9 us)
Async XLA Ops:
  7.2 2.3 copy-start
  11.4 56.0 %all-to-all-start = ((bf16[64,16,896]{2,1,0:T(8,128)(2,1)}), bf16[64,16,896]{2,1,0:T(8,128)(2,1)S(1)}, u32[]{:S(2)}, u32[]{:S(2)}) async-start(bf16[64,16,896]{2,1,0:T(8,128)(2,1)} %gather_fusion), calls=%async_computation | async-start | bytes 3670016 | tf_op jit(solution)/shard_map/all_to_all | solution.py:293
  22.8 80.9 %all-gather.3.cloned.1.call-start = ((), (), s32[]{:S(2)}) async-start(), calls=%async_computation.7 | async-start | bytes 5160960 | tf_op jit(solution)/shard_map/all_gather | solution.py:335
  68.9 98.5 %reduce-scatter.2.cloned.1.call-start = ((), (), s32[]{:S(2)}) async-start(), calls=%async_computation.6 | async-start | bytes 8257536 | tf_op jit(solution)/shard_map/reduce_scatter | solution.py:343
  69.6 8.2 %collective-permute-start.1 = (bf16[12,16,896]{2,1,0:T(8,128)(2,1)S(1)}, bf16[12,16,896]{2,1,0:T(8,128)(2,1)S(1)}, u32[]{:S(2)}, u32[]{:S(2)}) collective-permute-start(bf16[12,16,896]{2,1,0:T(8,128)(2,1)S(1)} %gather_fusion.1), channel_id=1, source_target_pairs={{0,2},{2,4},{4,6},{6,0},{1,3},{3,5},{5,7},{7,1},{8,10},{10,12},{12... | collective-permute-start | bytes 1032200 | tf_op jit(solution)/shard_map/ppermute | solution.py:38
  71.2 8.2 %collective-permute-start = (bf16[12,16,896]{2,1,0:T(8,128)(2,1)S(1)}, bf16[12,16,896]{2,1,0:T(8,128)(2,1)S(1)}, u32[]{:S(2)}, u32[]{:S(2)}) collective-permute-start(bf16[12,16,896]{2,1,0:T(8,128)(2,1)S(1)} %gather_fusion.1), channel_id=1, source_target_pairs={{2,0},{4,2},{6,4},{0,6},{3,1},{5,3},{7,5},{1,7},{10,8},{12,10},{14... | collective-permute-start | bytes 1032200 | tf_op jit(solution)/shard_map/ppermute | solution.py:39
  71.7 16.8 %collective-permute-start.4 = (bf16[12,16,896]{2,1,0:T(8,128)(2,1)S(1)}, bf16[12,16,896]{2,1,0:T(8,128)(2,1)S(1)}, u32[]{:S(2)}, u32[]{:S(2)}) collective-permute-start(bf16[12,16,896]{2,1,0:T(8,128)(2,1)S(1)} %gather_fusion.1), channel_id=1, source_target_pairs={{0,1},{1,0},{2,3},{3,2},{4,5},{5,4},{6,7},{7,6},{8,9},{9,8},{10,11... | collective-permute-start | bytes 1032200 | tf_op jit(solution)/shard_map/ppermute | solution.py:43
  77.8 8.8 %collective-permute-start.2 = (bf16[6,16,896]{2,1,0:T(8,128)(2,1)S(1)}, bf16[6,16,896]{2,1,0:T(8,128)(2,1)S(1)}, u32[]{:S(2)}, u32[]{:S(2)}) collective-permute-start(bf16[6,16,896]{2,1,0:T(8,128)(2,1)S(1)} %slice.72), channel_id=1, source_target_pairs={{0,2},{2,4},{4,6},{6,0},{1,3},{3,5},{5,7},{7,1},{8,10},{10,12},{12... | collective-permute-start | bytes 516104 | tf_op jit(solution)/shard_map/ppermute | solution.py:40
  79.5 24.2 %copy-start.3 = (bf16[1024,256]{1,0:T(8,128)(2,1)S(1)}, bf16[1024,256]{1,0:T(8,128)(2,1)}, u32[]{:S(2)}) copy-start(bf16[1024,256]{1,0:T(8,128)(2,1)} %refs_5_.1) | copy-start | bytes 1572868
  79.5 24.2 %copy-start.4 = (bf16[1024,256]{1,0:T(8,128)(2,1)S(1)}, bf16[1024,256]{1,0:T(8,128)(2,1)}, u32[]{:S(2)}) copy-start(bf16[1024,256]{1,0:T(8,128)(2,1)} %refs_6_.1) | copy-start | bytes 1572868
  79.5 24.1 %copy-start.5 = (bf16[896,256]{1,0:T(8,128)(2,1)S(1)}, bf16[896,256]{1,0:T(8,128)(2,1)}, u32[]{:S(2)}) copy-start(bf16[896,256]{1,0:T(8,128)(2,1)} %refs_3_.1) | copy-start | bytes 1376260
  79.5 24.1 %copy-start.6 = (bf16[896,256]{1,0:T(8,128)(2,1)S(1)}, bf16[896,256]{1,0:T(8,128)(2,1)}, u32[]{:S(2)}) copy-start(bf16[896,256]{1,0:T(8,128)(2,1)} %refs_4_.1) | copy-start | bytes 1376260
  79.5 9.0 %collective-permute-start.3 = (bf16[6,16,896]{2,1,0:T(8,128)(2,1)S(1)}, bf16[6,16,896]{2,1,0:T(8,128)(2,1)S(1)}, u32[]{:S(2)}, u32[]{:S(2)}) collective-permute-start(bf16[6,16,896]{2,1,0:T(8,128)(2,1)S(1)} %slice.73), channel_id=1, source_target_pairs={{2,0},{4,2},{6,4},{0,6},{3,1},{5,3},{7,5},{1,7},{10,8},{12,10},{14... | collective-permute-start | bytes 516104 | tf_op jit(solution)/shard_map/ppermute | solution.py:41
  80.0 9.9 %collective-permute-start.5 = (bf16[12,16,896]{2,1,0:T(8,128)(2,1)S(1)}, bf16[12,16,896]{2,1,0:T(8,128)(2,1)S(1)}, u32[]{:S(2)}, u32[]{:S(2)}) collective-permute-start(bf16[12,16,896]{2,1,0:T(8,128)(2,1)S(1)} %collective-permute-done.refs_1_), channel_id=1, source_target_pairs={{0,1},{1,0},{2,3},{3,2},{4,5},{5,4},{6,7},{7,6},{8,9},{9,8},{10,11... | collective-permute-start | bytes 1032200 | tf_op jit(solution)/shard_map/ppermute | solution.py:43
  80.0 9.9 %collective-permute-start.6 = (bf16[12,16,896]{2,1,0:T(8,128)(2,1)S(1)}, bf16[12,16,896]{2,1,0:T(8,128)(2,1)S(1)}, u32[]{:S(2)}, u32[]{:S(2)}) collective-permute-start(bf16[12,16,896]{2,1,0:T(8,128)(2,1)S(1)} %collective-permute-done.1.refs_2_), channel_id=1, source_target_pairs={{0,1},{1,0},{2,3},{3,2},{4,5},{5,4},{6,7},{7,6},{8,9},{9,8},{10,11... | collective-permute-start | bytes 1032200 | tf_op jit(solution)/shard_map/ppermute | solution.py:43
  86.6 1.9 collective-permute-start.7
  88.5 1.4 collective-permute-start.8
  89.9 0.7 copy-start.8
  101.0 0.7 copy-start.2
  119.7 0.7 copy-start.1
  120.4 1.2 copy-start.7
  156.0 14.5 %all-to-all-start.3 = ((bf16[8,112,128]{2,1,0:T(8,128)(2,1)}), bf16[8,112,128]{2,1,0:T(8,128)(2,1)S(1)}, u32[]{:S(2)}, u32[]{:S(2)}) async-start(bf16[8,112,128]{2,1,0:T(8,128)(2,1)} %broadcast_in_dim.68), calls=%async_computation.4 | async-start | bytes 458752 | tf_op jit(solution)/shard_map/all_to_all | solution.py:59
  170.5 55.8 %all-to-all-start.4 = ((bf16[64,16,896]{2,1,0:T(8,128)(2,1)}), bf16[64,16,896]{2,1,0:T(8,128)(2,1)S(1)}, u32[]{:S(2)}, u32[]{:S(2)}) async-start(bf16[64,16,896]{2,1,0:T(8,128)(2,1)} %gather_fusion.3), calls=%async_computation.5 | async-start | bytes 3670016 | tf_op jit(solution)/shard_map/all_to_all | solution.py:293
  180.5 20.1 %collective-permute-start.10 = (bf16[896,128]{1,0:T(8,128)(2,1)S(1)}, bf16[896,128]{1,0:T(8,128)(2,1)S(1)}, u32[]{:S(2)}, u32[]{:S(2)}) collective-permute-start(bf16[896,128]{1,0:T(8,128)(2,1)S(1)} %bitcast.18), channel_id=1, source_target_pairs={{0,16},{8,24},{16,0},{24,8},{1,17},{9,25},{17,1},{25,9},{2,18},{10... | collective-permute-start | bytes 688136 | tf_op jit(solution)/shard_map/ppermute | solution.py:274
  183.9 22.4 %collective-permute-start.11 = (bf16[896,128]{1,0:T(8,128)(2,1)S(1)}, bf16[896,128]{1,0:T(8,128)(2,1)S(1)}, u32[]{:S(2)}, u32[]{:S(2)}) collective-permute-start(bf16[896,128]{1,0:T(8,128)(2,1)S(1)} %bitcast.19), channel_id=1, source_target_pairs={{0,24},{8,0},{16,8},{24,16},{1,25},{9,1},{17,9},{25,17},{2,26},{10... | collective-permute-start | bytes 688136 | tf_op jit(solution)/shard_map/ppermute | solution.py:274
  185.1 22.4 %collective-permute-start.9 = (bf16[896,128]{1,0:T(8,128)(2,1)S(1)}, bf16[896,128]{1,0:T(8,128)(2,1)S(1)}, u32[]{:S(2)}, u32[]{:S(2)}) collective-permute-start(bf16[896,128]{1,0:T(8,128)(2,1)S(1)} %bitcast.20), channel_id=1, source_target_pairs={{0,8},{8,16},{16,24},{24,0},{1,9},{9,17},{17,25},{25,1},{2,10},{10... | collective-permute-start | bytes 688136 | tf_op jit(solution)/shard_map/ppermute | solution.py:274
Sparse Core Ops, SparseCore 0:
  69.0 34.5 all-gather.2
  120.5 46.7 reduce-scatter.1

commit v8 on v6

--- a/solution.py
+++ b/solution.py
@@ -271,8 +271,8 @@
 
 def spread_columns(column, place):
     width = column.shape[0]
-    pieces = [column] + [lax.ppermute(column, "x", shift(4, k)) for k in (1, 3, 2)]
-    pieces = [pieces[0], pieces[1], pieces[3], pieces[2]]
+    pieces = [column] + [lax.ppermute(column, "x", shift(4, k)) for k in (2, 3, 1)]
+    pieces = [pieces[0], pieces[3], pieces[1], pieces[2]]
     shape = jax.ShapeDtypeStruct((width, 2 * DH), F32)
     return pl.pallas_call(
         spread_kernel,
@@ -331,8 +331,11 @@
         (positions, back, counts, order, filled, place)
     )
     panels = PARTS[0][1] * KNB
-    pieces = gather_pieces(take(incoming, positions[:panels]))
-    gathered = lax.all_gather(take(incoming, positions[panels:]), ("y", "core"), axis=0)
+    wanted, later = lax.optimization_barrier(
+        (take(incoming, positions[:panels]), take(incoming, positions[panels:]))
+    )
+    pieces = gather_pieces(wanted)
+    gathered = lax.all_gather(later, ("y", "core"), axis=0)
     weights = (w_key, w_value, queries, out_grad)
     attended_0, grad_queries_0, shares, begun = attention(
         counts, order, pieces, *weights, PARTS[0], None

time: 239 us -> 239 us (level)
  no operation moved by 1% of the time
where the time goes in v8:
time: 239 us; the launch traced here: 238 us
  waiting for transfers between devices  104 us (44%)
  starting transfers between devices  35.2 us (15%)
  blocking collectives  33.6 us (14%)
  Pallas kernels  32.2 us (13%)
  between operations  14.4 us (6%)
  local copies, waits for them, and re-layouts  13.3 us (6%)
  other arithmetic  4.81 us (2%)
    all_to_all x2, waiting for transfers between devices, exchange(): lax.all_to_all(array, ('z', 'x'), split_axis=0, concat_axis=0, tiled=True)  60.6 us
    pallas_call x2, Pallas kernels, attention(): pl.pallas_call(functools.partial(attention_kernel, first, begin, stretch_...  27.8 us
    all_to_all x2, starting transfers between devices, exchange(): lax.all_to_all(array, ('z', 'x'), split_axis=0, concat_axis=0, tiled=True)  21.5 us
    all_to_all x1, blocking collectives, reduce_weight_grads(): by_x = lax.all_to_all(parts, 'x', split_axis=0, concat_axis=0, tiled=True)  19.6 us
    ppermute x3, waiting for transfers between devices, spread_columns(): lax.ppermute(column, 'x', shift(4, k))  18.9 us
    all_to_all x1, blocking collectives, reduce_weight_grads(): by_z = lax.all_to_all(part, 'z', split_axis=0, concat_axis=0, tiled=True)  13.9 us
    reduce_scatter x1, waiting for transfers between devices, local(): summed = lax.psum_scatter(shares, ('y', 'core'), scatter_dimension=0)  7.87 us
    gather x4, local copies, waits for them, and re-layouts, local(): take = lambda array, index: jnp.take(array, index, axis=0, mode='clip')  7.18 us
  transfers between devices with their start and end apart: 17, of which 11 were waited for; matrix products, arithmetic and copies ran while one was open for 4% of the time, Pallas kernels for 5%

profile of v8, /device:TPU:8, one launch (start us, length us, event | category | flops | bytes accessed | tf_op | source)
XLA Modules:
  0.0 237.9 jit_solution(4988931991025328239)
XLA Ops:
  7.2 0.8 multiply_add_fusion
  8.0 0.1 copy.16
  8.1 0.2 reshape.142
  8.3 0.8 convert_reduce_fusion
  9.1 0.1 select_reduce_fusion
  9.5 2.0 gather_fusion
  11.4 11.3 %all-to-all-start = ((bf16[64,16,896]{2,1,0:T(8,128)(2,1)}), bf16[64,16,896]{2,1,0:T(8,128)(2,1)S(1)}, u32[]{:S(2)}, u32[]{:S(2)}) async-start(bf16[64,16,896]{2,1,0:T(8,128)(2,1)} %gather_fusion), calls=%async_computation | async-start | bytes 3670016 | tf_op jit(solution)/shard_map/all_to_all | solution.py:293
  22.9 0.1 fusion.1
  23.2 1.3 dynamic_slice.12.count_ref
  24.5 0.7 stack.35.order_ref
  25.4 42.0 %all-to-all-done = bf16[64,16,896]{2,1,0:T(8,128)(2,1)S(1)} async-done(((bf16[64,16,896]{2,1,0:T(8,128)(2,1)}), bf16[64,16,896]{2,1,0:T(8,128)(2,1)S(1)}, u32[]{:S(2)}, u32[]{:S(2)}) %all-to-all-start) | async-done | bytes 1835040 | tf_op jit(solution)/shard_map/all_to_all | solution.py:293
  67.4 1.5 gather_fusion.2
  68.9 0.6 gather_fusion.1
  69.6 1.7 collective-permute-start.1
  71.2 0.4 collective-permute-start
  71.7 6.1 %collective-permute-done.1.refs_2_ = bf16[12,16,896]{2,1,0:T(8,128)(2,1)S(1)} collective-permute-done((bf16[12,16,896]{2,1,0:T(8,128)(2,1)S(1)}, bf16[12,16,896]{2,1,0:T(8,128)(2,1)S(1)}, u32[]{:S(2)}, u32[]{:S(2)}) %collective-permute-start.1) | collective-permute-done | bytes 344096 | tf_op jit(solution)/shard_map/ppermute | solution.py:38
  77.7 1.7 collective-permute-start.2
  79.5 0.5 collective-permute-start.3
  79.9 0.5 collective-permute-start.6
  80.4 6.1 %collective-permute-done.2.refs_3_ = bf16[6,16,896]{2,1,0:T(8,128)(2,1)S(1)} collective-permute-done((bf16[6,16,896]{2,1,0:T(8,128)(2,1)S(1)}, bf16[6,16,896]{2,1,0:T(8,128)(2,1)S(1)}, u32[]{:S(2)}, u32[]{:S(2)}) %collective-permute-start.2) | collective-permute-done | bytes 172064 | tf_op jit(solution)/shard_map/ppermute | solution.py:40
  86.6 1.7 collective-permute-done.3.refs_4_
  88.3 1.4 collective-permute-done.8.refs_9_
  89.7 0.6 copy-done.13
  90.3 0.1 copy-done.8
  90.5 0.8 copy-done.9
  91.2 11.2 %attention.2 = (bf16[384,256]{1,0:T(8,128)(2,1)}, bf16[384,256]{1,0:T(8,128)(2,1)}, bf16[8,32,16,896]{3,2,1,0:T(8,128)(2,1)}, bf16[896,512]{1,0:T(8,128)(2,1)}) custom-call(s32[16]{0:T(128)} %dynamic_slice.12.count_ref, s32[8]{0:T(128)} %stack.35.order_ref, bf16[12,16,896]{2,1,0:T(8,128)(2,1)} %copy-done.2, bf16[12,16,896]{2,1,0:T(8,128)(2,1)} %copy-done.6, ...), custom_call_target="tpu_custom_call" | custom-call | flops 8589934592 | bytes 16777216 | tf_op jit(solution)/shard_map/attention/pallas_call | solution.py:216
  102.4 1.8 all-gather.3.cloned.1.call-done
  104.2 16.6 %attention.3 = (bf16[640,256]{1,0:T(8,128)(2,1)}, bf16[640,256]{1,0:T(8,128)(2,1)}, bf16[8,32,16,896]{3,2,1,0:T(8,128)(2,1)}, bf16[4,896,128]{2,1,0:T(8,128)(2,1)}) custom-call(s32[16]{0:T(128)} %dynamic_slice.12.count_ref, s32[8]{0:T(128)} %stack.35.order_ref, bf16[8,20,16,896]{3,2,1,0:T(8,128)(2,1)} %bitcast.25, ...), custom_call_target="tpu_custom_call", output_to_operand_aliasing={{2}: (4, {})} | custom-call | flops 8589934592 | bytes 16777216 | tf_op jit(solution)/shard_map/attention/pallas_call | solution.py:216
  120.9 1.1 copy-done.1
  122.0 19.6 %all_to_all.25 = bf16[4,896,128]{2,1,0:T(8,128)(2,1)S(1)} all-to-all(bf16[4,896,128]{2,1,0:T(8,128)(2,1)S(1)} %copy-done.1), channel_id=1, replica_groups=mesh['z'=8,'x'=4,'y'=4,'core'=2] {'x'}, dimensions={0} | all-to-all | bytes 1835008 | tf_op jit(solution)/shard_map/all_to_all | solution.py:54
  141.7 0.1 add_convert_fusion
  141.8 13.9 %all_to_all.26 = bf16[8,112,128]{2,1,0:T(8,128)(2,1)S(1)} all-to-all(bf16[8,112,128]{2,1,0:T(8,128)(2,1)S(1)} %bitcast.23), channel_id=1, replica_groups=mesh['z'=8,'x'=4,'y'=4,'core'=2] {'z'}, dimensions={0} | all-to-all | bytes 458752 | tf_op jit(solution)/shard_map/all_to_all | solution.py:56
  155.8 0.7 broadcast_in_dim.68
  156.5 3.4 %all-to-all-start.3 = ((bf16[8,112,128]{2,1,0:T(8,128)(2,1)}), bf16[8,112,128]{2,1,0:T(8,128)(2,1)S(1)}, u32[]{:S(2)}, u32[]{:S(2)}) async-start(bf16[8,112,128]{2,1,0:T(8,128)(2,1)} %broadcast_in_dim.68), calls=%async_computation.4 | async-start | bytes 458752 | tf_op jit(solution)/shard_map/all_to_all | solution.py:59
  159.9 7.9 %reduce-scatter.2.cloned.1.call-done = bf16[1,32,16,896]{3,2,1,0:T(8,128)(2,1)} async-done(((bf16[8,32,16,896]{3,2,1,0:T(8,128)(2,1)}), bf16[1,32,16,896]{3,2,1,0:T(8,128)(2,1)}) %reduce-scatter.2.cloned.1.call-update) | async-done | bytes 917520 | tf_op jit(solution)/shard_map/reduce_scatter | solution.py:346
  167.8 3.2 %gather_fusion.3 = bf16[64,16,896]{2,1,0:T(8,128)(2,1)} fusion(bf16[32,16,896]{2,1,0:T(8,128)(2,1)} %bitcast.22, s32[1024]{0:T(1024)S(1)} %pad_clamp_fusion), kind=kCustom, calls=%fused_computation.3 | custom fusion | bytes 3670272 | tf_op jit(solution)/shard_map/jit(_take)/gather | solution.py:322
  171.0 10.2 %all-to-all-start.4 = ((bf16[64,16,896]{2,1,0:T(8,128)(2,1)}), bf16[64,16,896]{2,1,0:T(8,128)(2,1)S(1)}, u32[]{:S(2)}, u32[]{:S(2)}) async-start(bf16[64,16,896]{2,1,0:T(8,128)(2,1)} %gather_fusion.3), calls=%async_computation.5 | async-start | bytes 3670016 | tf_op jit(solution)/shard_map/all_to_all | solution.py:293
  181.1 3.4 %collective-permute-start.10 = (bf16[896,128]{1,0:T(8,128)(2,1)S(1)}, bf16[896,128]{1,0:T(8,128)(2,1)S(1)}, u32[]{:S(2)}, u32[]{:S(2)}) collective-permute-start(bf16[896,128]{1,0:T(8,128)(2,1)S(1)} %bitcast.18), channel_id=1, source_target_pairs={{0,16},{8,24},{16,0},{24,8},{1,17},{9,25},{17,1},{25,9},{2,18},{10... | collective-permute-start | bytes 688136 | tf_op jit(solution)/shard_map/ppermute | solution.py:274
  184.5 1.2 collective-permute-start.11
  185.7 0.9 collective-permute-start.9
  186.6 1.9 pad_maximum_fusion.1
  188.4 0.8 pad_maximum_fusion
  189.2 12.1 %collective-permute-done.10.refs_2_ = bf16[896,128]{1,0:T(8,128)(2,1)S(1)} collective-permute-done((bf16[896,128]{1,0:T(8,128)(2,1)S(1)}, bf16[896,128]{1,0:T(8,128)(2,1)S(1)}, u32[]{:S(2)}, u32[]{:S(2)}) %collective-permute-start.10) | collective-permute-done | bytes 229408 | tf_op jit(solution)/shard_map/ppermute | solution.py:274
  201.3 5.5 %collective-permute-done.11.refs_3_ = bf16[896,128]{1,0:T(8,128)(2,1)S(1)} collective-permute-done((bf16[896,128]{1,0:T(8,128)(2,1)S(1)}, bf16[896,128]{1,0:T(8,128)(2,1)S(1)}, u32[]{:S(2)}, u32[]{:S(2)}) %collective-permute-start.11) | collective-permute-done | bytes 229408 | tf_op jit(solution)/shard_map/ppermute | solution.py:274
  206.8 1.3 collective-permute-done.9.refs_1_
  208.1 1.4 spread.1
  209.5 18.6 %all-to-all-done.4.arrived_ref = bf16[64,16,896]{2,1,0:T(8,128)(2,1)S(1)} async-done(((bf16[64,16,896]{2,1,0:T(8,128)(2,1)}), bf16[64,16,896]{2,1,0:T(8,128)(2,1)S(1)}, u32[]{:S(2)}, u32[]{:S(2)}) %all-to-all-start.4) | async-done | bytes 1835040 | tf_op jit(solution)/shard_map/all_to_all | solution.py:293
  228.1 2.9 %collect.1 = f32[32,16,896]{2,1,0:T(8,128)} custom-call(s32[64]{0:T(128)S(1)} %reshape.149.slot_ref, s32[64]{0:T(128)S(1)} %reshape.146.filled_ref, bf16[64,16,896]{2,1,0:T(8,128)(2,1)S(1)} %all-to-all-done.4.arrived_ref), custom_call_target="tpu_custom_call" | custom-call | tf_op jit(solution)/shard_map/collect/pallas_call | solution.py:250
  (55 shorter events, 0.9 us)
Async XLA Ops:
  7.2 2.3 copy-start
  11.4 56.0 %all-to-all-start = ((bf16[64,16,896]{2,1,0:T(8,128)(2,1)}), bf16[64,16,896]{2,1,0:T(8,128)(2,1)S(1)}, u32[]{:S(2)}, u32[]{:S(2)}) async-start(bf16[64,16,896]{2,1,0:T(8,128)(2,1)} %gather_fusion), calls=%async_computation | async-start | bytes 3670016 | tf_op jit(solution)/shard_map/all_to_all | solution.py:293
  22.8 81.5 %all-gather.3.cloned.1.call-start = ((), (), s32[]{:S(2)}) async-start(), calls=%async_computation.7 | async-start | bytes 5160960 | tf_op jit(solution)/shard_map/all_gather | solution.py:338
  69.5 20.2 %copy-start.2 = (bf16[12,16,896]{2,1,0:T(8,128)(2,1)}, bf16[12,16,896]{2,1,0:T(8,128)(2,1)S(1)}, u32[]{:S(2)}) copy-start(bf16[12,16,896]{2,1,0:T(8,128)(2,1)S(1)} %gather_fusion.1) | copy-start | bytes 1032196
  69.5 98.3 %reduce-scatter.2.cloned.1.call-start = ((), (), s32[]{:S(2)}) async-start(), calls=%async_computation.6 | async-start | bytes 8257536 | tf_op jit(solution)/shard_map/reduce_scatter | solution.py:346
  69.6 8.2 %collective-permute-start.1 = (bf16[12,16,896]{2,1,0:T(8,128)(2,1)S(1)}, bf16[12,16,896]{2,1,0:T(8,128)(2,1)S(1)}, u32[]{:S(2)}, u32[]{:S(2)}) collective-permute-start(bf16[12,16,896]{2,1,0:T(8,128)(2,1)S(1)} %gather_fusion.1), channel_id=1, source_target_pairs={{0,2},{2,4},{4,6},{6,0},{1,3},{3,5},{5,7},{7,1},{8,10},{10,12},{12... | collective-permute-start | bytes 1032200 | tf_op jit(solution)/shard_map/ppermute | solution.py:38
  71.2 8.2 %collective-permute-start = (bf16[12,16,896]{2,1,0:T(8,128)(2,1)S(1)}, bf16[12,16,896]{2,1,0:T(8,128)(2,1)S(1)}, u32[]{:S(2)}, u32[]{:S(2)}) collective-permute-start(bf16[12,16,896]{2,1,0:T(8,128)(2,1)S(1)} %gather_fusion.1), channel_id=1, source_target_pairs={{2,0},{4,2},{6,4},{0,6},{3,1},{5,3},{7,5},{1,7},{10,8},{12,10},{14... | collective-permute-start | bytes 1032200 | tf_op jit(solution)/shard_map/ppermute | solution.py:39
  71.7 16.6 %collective-permute-start.4 = (bf16[12,16,896]{2,1,0:T(8,128)(2,1)S(1)}, bf16[12,16,896]{2,1,0:T(8,128)(2,1)S(1)}, u32[]{:S(2)}, u32[]{:S(2)}) collective-permute-start(bf16[12,16,896]{2,1,0:T(8,128)(2,1)S(1)} %gather_fusion.1), channel_id=1, source_target_pairs={{0,1},{1,0},{2,3},{3,2},{4,5},{5,4},{6,7},{7,6},{8,9},{9,8},{10,11... | collective-permute-start | bytes 1032200 | tf_op jit(solution)/shard_map/ppermute | solution.py:43
  77.7 12.0 %copy-start.5 = (bf16[12,16,896]{2,1,0:T(8,128)(2,1)}, bf16[12,16,896]{2,1,0:T(8,128)(2,1)S(1)}, u32[]{:S(2)}) copy-start(bf16[12,16,896]{2,1,0:T(8,128)(2,1)S(1)} %collective-permute-done.1.refs_2_) | copy-start | bytes 1032196
  77.7 8.8 %collective-permute-start.2 = (bf16[6,16,896]{2,1,0:T(8,128)(2,1)S(1)}, bf16[6,16,896]{2,1,0:T(8,128)(2,1)S(1)}, u32[]{:S(2)}, u32[]{:S(2)}) collective-permute-start(bf16[6,16,896]{2,1,0:T(8,128)(2,1)S(1)} %slice.72), channel_id=1, source_target_pairs={{0,2},{2,4},{4,6},{6,0},{1,3},{3,5},{5,7},{7,1},{8,10},{10,12},{12... | collective-permute-start | bytes 516104 | tf_op jit(solution)/shard_map/ppermute | solution.py:40
  79.4 10.2 %copy-start.6 = (bf16[12,16,896]{2,1,0:T(8,128)(2,1)}, bf16[12,16,896]{2,1,0:T(8,128)(2,1)S(1)}, u32[]{:S(2)}) copy-start(bf16[12,16,896]{2,1,0:T(8,128)(2,1)S(1)} %collective-permute-done.refs_1_) | copy-start | bytes 1032196
  79.5 8.8 %collective-permute-start.3 = (bf16[6,16,896]{2,1,0:T(8,128)(2,1)S(1)}, bf16[6,16,896]{2,1,0:T(8,128)(2,1)S(1)}, u32[]{:S(2)}, u32[]{:S(2)}) collective-permute-start(bf16[6,16,896]{2,1,0:T(8,128)(2,1)S(1)} %slice.73), channel_id=1, source_target_pairs={{2,0},{4,2},{6,4},{0,6},{3,1},{5,3},{7,5},{1,7},{10,8},{12,10},{14... | collective-permute-start | bytes 516104 | tf_op jit(solution)/shard_map/ppermute | solution.py:41
  79.9 9.7 %collective-permute-start.5 = (bf16[12,16,896]{2,1,0:T(8,128)(2,1)S(1)}, bf16[12,16,896]{2,1,0:T(8,128)(2,1)S(1)}, u32[]{:S(2)}, u32[]{:S(2)}) collective-permute-start(bf16[12,16,896]{2,1,0:T(8,128)(2,1)S(1)} %collective-permute-done.refs_1_), channel_id=1, source_target_pairs={{0,1},{1,0},{2,3},{3,2},{4,5},{5,4},{6,7},{7,6},{8,9},{9,8},{10,11... | collective-permute-start | bytes 1032200 | tf_op jit(solution)/shard_map/ppermute | solution.py:43
  79.9 9.7 %collective-permute-start.6 = (bf16[12,16,896]{2,1,0:T(8,128)(2,1)S(1)}, bf16[12,16,896]{2,1,0:T(8,128)(2,1)S(1)}, u32[]{:S(2)}, u32[]{:S(2)}) collective-permute-start(bf16[12,16,896]{2,1,0:T(8,128)(2,1)S(1)} %collective-permute-done.1.refs_2_), channel_id=1, source_target_pairs={{0,1},{1,0},{2,3},{3,2},{4,5},{5,4},{6,7},{7,6},{8,9},{9,8},{10,11... | collective-permute-start | bytes 1032200 | tf_op jit(solution)/shard_map/ppermute | solution.py:43
  86.6 3.1 %copy-start.10 = (bf16[6,16,896]{2,1,0:T(8,128)(2,1)}, bf16[6,16,896]{2,1,0:T(8,128)(2,1)S(1)}, u32[]{:S(2)}) copy-start(bf16[6,16,896]{2,1,0:T(8,128)(2,1)S(1)} %collective-permute-done.2.refs_3_) | copy-start | bytes 516100
  86.6 1.7 collective-permute-start.7
  88.2 1.5 copy-start.11
  88.2 1.4 collective-permute-start.8
  88.2 1.5 copy-start.7
  88.3 1.5 copy-start.12
  89.6 0.7 copy-start.13
  89.7 0.8 copy-start.8
  90.5 0.8 copy-start.9
  120.8 1.2 copy-start.1
  156.5 14.5 %all-to-all-start.3 = ((bf16[8,112,128]{2,1,0:T(8,128)(2,1)}), bf16[8,112,128]{2,1,0:T(8,128)(2,1)S(1)}, u32[]{:S(2)}, u32[]{:S(2)}) async-start(bf16[8,112,128]{2,1,0:T(8,128)(2,1)} %broadcast_in_dim.68), calls=%async_computation.4 | async-start | bytes 458752 | tf_op jit(solution)/shard_map/all_to_all | solution.py:59
  170.9 17.5 %copy-start.3 = (bf16[640,256]{1,0:T(8,128)(2,1)S(1)}, bf16[640,256]{1,0:T(8,128)(2,1)}, u32[]{:S(2)}) copy-start(bf16[640,256]{1,0:T(8,128)(2,1)} %get-tuple-element.33) | copy-start | bytes 983044
  171.0 17.5 %copy-start.4 = (bf16[384,256]{1,0:T(8,128)(2,1)S(1)}, bf16[384,256]{1,0:T(8,128)(2,1)}, u32[]{:S(2)}) copy-start(bf16[384,256]{1,0:T(8,128)(2,1)} %get-tuple-element.29) | copy-start | bytes 589828
  171.0 57.2 %all-to-all-start.4 = ((bf16[64,16,896]{2,1,0:T(8,128)(2,1)}), bf16[64,16,896]{2,1,0:T(8,128)(2,1)S(1)}, u32[]{:S(2)}, u32[]{:S(2)}) async-start(bf16[64,16,896]{2,1,0:T(8,128)(2,1)} %gather_fusion.3), calls=%async_computation.5 | async-start | bytes 3670016 | tf_op jit(solution)/shard_map/all_to_all | solution.py:293
  181.1 20.2 %collective-permute-start.10 = (bf16[896,128]{1,0:T(8,128)(2,1)S(1)}, bf16[896,128]{1,0:T(8,128)(2,1)S(1)}, u32[]{:S(2)}, u32[]{:S(2)}) collective-permute-start(bf16[896,128]{1,0:T(8,128)(2,1)S(1)} %bitcast.18), channel_id=1, source_target_pairs={{0,16},{8,24},{16,0},{24,8},{1,17},{9,25},{17,1},{25,9},{2,18},{10... | collective-permute-start | bytes 688136 | tf_op jit(solution)/shard_map/ppermute | solution.py:274
  184.5 22.3 %collective-permute-start.11 = (bf16[896,128]{1,0:T(8,128)(2,1)S(1)}, bf16[896,128]{1,0:T(8,128)(2,1)S(1)}, u32[]{:S(2)}, u32[]{:S(2)}) collective-permute-start(bf16[896,128]{1,0:T(8,128)(2,1)S(1)} %bitcast.19), channel_id=1, source_target_pairs={{0,24},{8,0},{16,8},{24,16},{1,25},{9,1},{17,9},{25,17},{2,26},{10... | collective-permute-start | bytes 688136 | tf_op jit(solution)/shard_map/ppermute | solution.py:274
  185.7 22.4 %collective-permute-start.9 = (bf16[896,128]{1,0:T(8,128)(2,1)S(1)}, bf16[896,128]{1,0:T(8,128)(2,1)S(1)}, u32[]{:S(2)}, u32[]{:S(2)}) collective-permute-start(bf16[896,128]{1,0:T(8,128)(2,1)S(1)} %bitcast.20), channel_id=1, source_target_pairs={{0,8},{8,16},{16,24},{24,0},{1,9},{9,17},{17,25},{25,1},{2,10},{10... | collective-permute-start | bytes 688136 | tf_op jit(solution)/shard_map/ppermute | solution.py:274
Sparse Core Ops, SparseCore 0:
  69.6 34.5 all-gather.2
  121.0 46.7 reduce-scatter.1
